TPU v7x, 32 devices: a whole 2x2x4 slice. The times are simulated.
32 devices in a mesh: band: 2 (over x), row: 16 (over z, y, core).
Axes of the slice: x: 2, y: 2, z: 4, core: 2. Of those that a mesh axis runs over, the one named last changes fastest.
Arguments:
- prior_cov: float32 [16384, 8192], P(('band', 'row')), parts along dimension 0, as said below
- snapshots: bfloat16 [2, 16384, 256], P(None, ('band', 'row')), parts along dimension 1, may hold values from -6 to 6
- prior_basis: float32 [16384, 128], P(('band', 'row')), parts along dimension 0, may hold values from -0.0625 to 0.0625
Outputs:
- new_cov: float32 [16384, 8192], P(('band', 'row')), parts along dimension 0
- new_basis: float32 [16384, 128], P(('band', 'row')), parts along dimension 0
There are 2 independent parts, one for each index of `band`. A program takes and returns all parts, laid end to end along the dimension named above; each array names one. Nothing has to cross between parts.
Inputs may be any that keep to these rules, and one draw needn't show every extreme that they name: prior_cov is symmetric and positive definite.
All inputs are finite; a program needn't handle non-finite values.
Results may differ from a plain program's by a relative error of at most 0.0003.
Values may be sent and summed in bfloat16 or wider, within the bound.
No kernel may reach another device: no remote copies, remote signals or barrier semaphores. Data moves between devices by JAX's collectives and lax.ppermute only.
A program may use at most 128 MiB of HBM per device.

v0:
```python
import jax
import jax.numpy as jnp
from jax import lax
from jax.sharding import PartitionSpec as P

forget_factor = 0.9
exact = lax.Precision.HIGHEST


def lead_contract(left_side, right_side, precision_mode):
    return lax.dot_general(
        left_side,
        right_side,
        (((0,), (0,)), ((), ())),
        precision=precision_mode,
        preferred_element_type=jnp.float32,
    )


def orthonormal(applied, gram_matrix):
    lower_factor = jnp.linalg.cholesky(gram_matrix)
    return lax.linalg.triangular_solve(
        lower_factor, applied, left_side=False, lower=True, transpose_a=True
    )


def local(prior_cov, snapshots, prior_basis):
    covariance = prior_cov
    subspace = prior_basis
    row_count = covariance.shape[0]
    inv_snap = 1.0 / snapshots.shape[2]
    for window in range(snapshots.shape[0]):
        snapshot_panel = snapshots[window]

        def outer_block(block_rows, first_row, local_panel=snapshot_panel):
            return lax.dot_general(
                local_panel,
                block_rows,
                (((1,), (1,)), ((), ())),
                preferred_element_type=jnp.float32,
            )

        outer_term = outer_block(
            lax.all_gather(snapshot_panel, "row", axis=0, tiled=True), jnp.int32(0)
        )
        updated = forget_factor * covariance + outer_term * inv_snap
        source = updated
        current = subspace

        def add_block(running, block_rows, first_row, matrix=source):
            return jnp.dot(matrix, block_rows, precision=exact, preferred_element_type=jnp.float32)

        start_value = jnp.zeros((row_count, current.shape[1]), jnp.float32)
        applied = add_block(
            start_value, lax.all_gather(current, "row", axis=0, tiled=True), jnp.int32(0)
        )
        gram_matrix = lax.psum(lead_contract(applied, applied, exact), "row")
        subspace = orthonormal(applied, gram_matrix)
        covariance = updated
    return (covariance, subspace)


def solution(mesh):
    return jax.shard_map(
        local,
        mesh=mesh,
        in_specs=(
            P(("band", "row"), None),
            P(None, ("band", "row"), None),
            P(("band", "row"), None),
        ),
        out_specs=(P(("band", "row"), None), P(("band", "row"), None)),
        check_vma=False,
    )
```

profile of v0, /device:TPU:0, one launch (start us, length us, event | category | flops | bytes accessed | tf_op | source)
XLA Modules:
  0.0 456.3 jit_solution(2026473422893676332)
XLA Ops:
  7.2 1.9 fusion.14
  9.1 0.7 all-gather.7.cloned.1.call-update
  9.9 54.1 %all-gather.11.cloned.1.call-done = bf16[1,8192,256]{2,1,0:T(8,128)(2,1)} async-done(((bf16[1,512,256]{2,1,0:T(8,128)(2,1)}), bf16[1,8192,256]{2,1,0:T(8,128)(2,1)}) %all-gather.11.cloned.1.call-update) | async-done | bytes 4194320 | tf_op jit(solution)/shard_map/all_gather | solution.py:44
  64.0 16.2 %multiply_add_fusion.1 = f32[512,8192]{1,0:T(8,128)} fusion(f32[512,8192]{1,0:T(8,128)} %param.6, bf16[1,8192,256]{2,1,0:T(8,128)(2,1)} %all-gather.11.cloned.1.call-done, bf16[2,512,256]{2,1,0:T(8,128)(2,1)} %param.7), kind=kOutput, calls=%fused_computation.1 | convolution fusion | flops 2160066560 | bytes 38010880 | tf_op jit(solution)/shard_map/dot_general | solution.py:36
  80.2 35.0 %all-gather.7.cloned.1.call-done = f32[8192,128]{1,0:T(8,128)} async-done(((f32[512,128]{1,0:T(8,128)}), f32[8192,128]{1,0:T(8,128)}) %all-gather.7.cloned.1.call-update) | async-done | bytes 4194320 | tf_op jit(solution)/shard_map/all_gather | solution.py:55
  115.3 16.2 %fusion.15 = f32[512,128]{1,0:T(8,128)S(1)} fusion(f32[512,8192]{1,0:T(8,128)} %multiply_add_fusion.1, f32[8192,128]{1,0:T(8,128)} %all-gather.7.cloned.1.call-done), kind=kOutput, calls=%fused_computation.28 | convolution fusion | flops 6442450944 | bytes 21233664 | tf_op jit(solution)/shard_map/dot_general | solution.py:51
  131.5 1.2 fusion.16
  133.5 82.3 %all-reduce.3.cloned.1.call-done = f32[128,128]{0,1:T(8,128)} async-done(((f32[128,128]{0,1:T(8,128)}), f32[128,128]{0,1:T(8,128)}) %all-reduce.3.cloned.1.call-update) | async-done | bytes 65552 | tf_op jit(solution)/shard_map/psum | solution.py:57
  215.8 0.9 copy.6
  216.8 0.9 fusion.9
  217.6 11.7 %cholesky.44 = f32[128,128]{1,0:T(8,128)S(1)} custom-call(f32[128,128]{1,0:T(8,128)S(1)} %fusion.9), custom_call_target="Cholesky" | custom-call | tf_op jit(solution)/shard_map/jit(cholesky)/cholesky | solution.py:21
  230.6 9.8 %custom-call.6 = f32[1,128,128]{1,2,0:T(8,128)S(1)} custom-call(f32[1,128,128]{2,1,0:T(8,128)S(1)} %fusion.4), custom_call_target="InvertDiagBlocksLowerTriangular" | custom-call | tf_op jit(solution)/shard_map/triangular_solve/custom-call.0 | solution.py:22
  240.4 1.1 convolution_bitcast_fusion.1
  241.6 29.8 %all-gather.13.cloned.1.call-done = bf16[1,8192,256]{2,1,0:T(8,128)(2,1)} async-done(((bf16[1,512,256]{2,1,0:T(8,128)(2,1)}), bf16[1,8192,256]{2,1,0:T(8,128)(2,1)}) %all-gather.13.cloned.1.call-update) | async-done | bytes 4194320 | tf_op jit(solution)/shard_map/all_gather | solution.py:44
  271.4 12.4 %multiply_add_fusion = f32[512,8192]{1,0:T(8,128)} fusion(f32[512,8192]{1,0:T(8,128)} %multiply_add_fusion.1, bf16[1,8192,256]{2,1,0:T(8,128)(2,1)} %all-gather.13.cloned.1.call-done, bf16[2,512,256]{2,1,0:T(8,128)(2,1)S(1)} %copy-done), kind=kOutput, calls=%fused_computation | convolution fusion | flops 2160066560 | bytes 38010880 | tf_op jit(solution)/shard_map/dot_general | solution.py:36
  283.9 39.0 %all-gather.9.cloned.1.call-done = f32[8192,128]{0,1:T(8,128)} async-done(((f32[512,128]{0,1:T(8,128)}), f32[8192,128]{0,1:T(8,128)}) %all-gather.9.cloned.1.call-update) | async-done | bytes 4194320 | tf_op jit(solution)/shard_map/all_gather | solution.py:55
  322.8 16.4 %fusion.17 = f32[512,128]{1,0:T(8,128)S(1)} fusion(f32[512,8192]{1,0:T(8,128)} %multiply_add_fusion, f32[8192,128]{0,1:T(8,128)} %all-gather.9.cloned.1.call-done), kind=kOutput, calls=%fused_computation.30 | convolution fusion | flops 6442450944 | bytes 21233664 | tf_op jit(solution)/shard_map/dot_general | solution.py:51
  339.2 1.2 fusion.18
  340.5 83.1 %all-reduce.5.cloned.1.call-done = f32[128,128]{0,1:T(8,128)} async-done(((f32[128,128]{0,1:T(8,128)}), f32[128,128]{0,1:T(8,128)}) %all-reduce.5.cloned.1.call-update) | async-done | bytes 65552 | tf_op jit(solution)/shard_map/psum | solution.py:57
  423.6 0.9 copy.8
  424.5 0.9 fusion.7
  425.4 11.7 %cholesky.55 = f32[128,128]{1,0:T(8,128)S(1)} custom-call(f32[128,128]{1,0:T(8,128)S(1)} %fusion.7), custom_call_target="Cholesky" | custom-call | tf_op jit(solution)/shard_map/jit(cholesky)/cholesky | solution.py:21
  438.4 9.8 %custom-call.7 = f32[1,128,128]{1,2,0:T(8,128)S(1)} custom-call(f32[1,128,128]{2,1,0:T(8,128)S(1)} %fusion.5), custom_call_target="InvertDiagBlocksLowerTriangular" | custom-call | tf_op jit(solution)/shard_map/triangular_solve/custom-call.0 | solution.py:22
  448.7 0.8 copy.9
  (20 shorter events, 4.0 us)
Async XLA Ops:
  7.2 56.9 %all-gather.11.cloned.1.call-start = ((), (), s32[]{:S(2)}) async-start(), calls=%async_computation.4 | async-start | bytes 4456448 | tf_op jit(solution)/shard_map/all_gather | solution.py:44
  9.1 106.2 %all-gather.7.cloned.1.call-start = ((), (), s32[]{:S(2)}) async-start(), calls=%async_computation | async-start | bytes 4456448 | tf_op jit(solution)/shard_map/all_gather | solution.py:55
  9.8 206.0 %all-reduce.3.cloned.1.call-start = ((), (), s32[]{:S(2)}) async-start(), calls=%async_computation.1 | async-start | bytes 131072 | tf_op jit(solution)/shard_map/psum | solution.py:57
  80.2 191.2 %copy-start = (bf16[2,512,256]{2,1,0:T(8,128)(2,1)S(1)}, bf16[2,512,256]{2,1,0:T(8,128)(2,1)}, u32[]{:S(2)}) copy-start(bf16[2,512,256]{2,1,0:T(8,128)(2,1)} %param.7) | copy-start | bytes 1572868
  132.7 138.7 %all-gather.13.cloned.1.call-start = ((), (), s32[]{:S(2)}) async-start(), calls=%async_computation.5 | async-start | bytes 4456448 | tf_op jit(solution)/shard_map/all_gather | solution.py:44
  133.3 189.5 %all-gather.9.cloned.1.call-start = ((), (), s32[]{:S(2)}) async-start(), calls=%async_computation.2 | async-start | bytes 4456448 | tf_op jit(solution)/shard_map/all_gather | solution.py:55
  241.6 182.0 %all-reduce.5.cloned.1.call-start = ((), (), s32[]{:S(2)}) async-start(), calls=%async_computation.3 | async-start | bytes 131072 | tf_op jit(solution)/shard_map/psum | solution.py:57
Sparse Core Ops, SparseCore 0:
  10.7 53.2 all-gather.10
  66.2 49.0 all-gather.6
  132.8 82.9 all-reduce.2
  218.6 52.7 all-gather.12
  273.7 49.0 all-gather.8
  340.6 82.9 all-reduce.4
where the time goes:
time: 458 us; the launch traced here: 456 us
  waiting for transfers between devices  325 us (71%)
  matrix products  65.3 us (14%)
  other arithmetic  47.3 us (10%)
  between operations  14.2 us (3%)
    psum x2, waiting for transfers between devices, local(): gram_matrix = lax.psum(lead_contract(applied, applied, exact), 'row')  165 us
    all_gather x2, waiting for transfers between devices, local(): lax.all_gather(snapshot_panel, 'row', axis=0, tiled=True)  83.9 us
    all_gather x2, waiting for transfers between devices, local(): lax.all_gather(current, 'row', axis=0, tiled=True)  74 us
    dot_general x2, matrix products, add_block(): jnp.dot(matrix, block_rows, precision=exact, preferred_element_type=jnp.f...  32.6 us
    dot_general x2, matrix products, outer_block(): lax.dot_general(local_panel, block_rows, (((1,), (1,)), ((), ())), prefer...  28.6 us
    another operation x6, other arithmetic, orthonormal(): lower_factor = jnp.linalg.cholesky(gram_matrix)  24.8 us
    another operation x4, other arithmetic, orthonormal(): lax.linalg.triangular_solve(lower_factor, applied, left_side=False, lower...  20.9 us
  transfers between devices with their start and end apart: 6, of which 6 were waited for; matrix products, arithmetic and copies ran while one was open for 12% of the time, Pallas kernels for 0%

commit v1 on v0

v1 whole, which is shorter than its diff:
```python
import functools

import jax
import jax.numpy as jnp
import numpy as np
from jax import lax
from jax.experimental import pallas as pl
from jax.experimental.pallas import tpu as pltpu
from jax.sharding import PartitionSpec as P

forget_factor = 0.9
code_span = 240.0
code_middle = 120.0
scale_rows = 16
ln2 = 0.6931471805599453
in_vmem = pl.BlockSpec(memory_space=pltpu.VMEM)
anywhere = pl.BlockSpec(memory_space=pl.ANY)
in_hbm = pl.BlockSpec(memory_space=pltpu.HBM)
in_smem = pl.BlockSpec(memory_space=pltpu.SMEM)
params = pltpu.CompilerParams(vmem_limit_bytes=16 * 2**20)

inner = (((1,), (0,)), ((), ()))
lead = (((0,), (0,)), ((), ()))
trail = (((1,), (1,)), ((), ()))


def dot(a, b, dims):
    return lax.dot_general(a, b, dims, preferred_element_type=jnp.float32)


def split(x):
    high = x.astype(jnp.bfloat16)
    return high, (x - high.astype(jnp.float32)).astype(jnp.bfloat16)


def dot3(a, b, dims):
    a_high, a_low = split(a)
    b_high, b_low = split(b)
    return dot(a_high, b_high, dims) + (dot(a_high, b_low, dims) + dot(a_low, b_high, dims))


def dot2(a, b, dims):
    b_high, b_low = split(b)
    return dot(a, b_high, dims) + dot(a, b_low, dims)


def gate(values, events=()):
    count = len(values)

    def kernel(*refs):
        pass

    return list(
        pl.pallas_call(
            kernel,
            out_shape=tuple(jax.ShapeDtypeStruct(v.shape, v.dtype) for v in values),
            in_specs=[anywhere] * (count + len(events)),
            out_specs=(anywhere,) * count,
            input_output_aliases={i: i for i in range(count)},
            compiler_params=params,
            name="gate",
        )(*values, *events)
    )


def ring_order(devices):
    chips = devices // 2
    return list(range(0, chips, 2)) + list(range(chips - 1, 0, -2))


def ring_pairs(devices, way):
    order = ring_order(devices)
    chips = len(order)
    pairs = []
    for at in range(chips):
        for core in range(2):
            pairs.append((2 * order[at] + core, 2 * order[(at + way) % chips] + core))
    return pairs


def partner_pairs(devices, mask):
    return [(i, i ^ mask) for i in range(devices)]


def ring_table(devices, rows):
    order = ring_order(devices)
    chips = len(order)
    table = []
    for me in range(devices):
        at, core = order.index(me // 2), me % 2
        line = [me * rows, (me ^ 1) * rows]
        for step in range(1, chips // 2):
            for there in (at - step, at + step):
                chip = order[there % chips]
                line += [(2 * chip + core) * rows, (2 * chip + 1 - core) * rows]
        chip = order[(at + chips // 2) % chips]
        own, other = (2 * chip + core) * rows, (2 * chip + 1 - core) * rows
        line += [own, other, own + rows // 2, other + rows // 2]
        line += [core, (me // 2) % 2]
        table.append(line)
    return np.array(table, np.int32)


class Ring:
    def __init__(self, block, devices, axis):
        self.axis = axis
        self.forth, self.back = ring_pairs(devices, 1), ring_pairs(devices, -1)
        self.swap = partner_pairs(devices, 1)
        self.steps = devices // 4
        self.done = 0
        self.ahead = self.behind = block
        self.groups = []

    def pass_on(self):
        mine = [self.ahead] if self.done == 0 else [self.ahead, self.behind]
        group = []
        for block in mine:
            group += [block, lax.ppermute(block, "row", self.swap)]
        self.groups.append(group)

    def step(self):
        self.done += 1
        ahead, behind = self.ahead, self.behind
        if self.done == self.steps:
            half = ahead.shape[self.axis] // 2
            ahead = lax.slice_in_dim(ahead, 0, half, axis=self.axis)
            behind = lax.slice_in_dim(behind, half, 2 * half, axis=self.axis)
        self.ahead = lax.ppermute(ahead, "row", self.forth)
        self.behind = lax.ppermute(behind, "row", self.back)

    def held(self):
        received = [self.groups[-1][1::2]] if self.groups else []
        return [self.ahead, self.behind] + [v for r in received for v in r]

    def hold(self, values):
        values = list(values)
        self.ahead, self.behind = values[:2]
        if self.groups:
            self.groups[-1][1::2] = values[2:]


def small_kernel(kernel, out_shape, args, name):
    multiple = isinstance(out_shape, tuple)
    return pl.pallas_call(
        kernel,
        out_shape=out_shape,
        in_specs=[in_smem] + [in_vmem] * (len(args) - 1),
        out_specs=tuple(in_vmem for _ in out_shape) if multiple else in_vmem,
        compiler_params=params,
        name=name,
    )(*args)


def f32(*shape):
    return jax.ShapeDtypeStruct(shape, jnp.float32)


def store_halves(line_ref, bit, value_ref, mine_ref, theirs_ref):
    half = mine_ref.shape[0]
    side = line_ref[0, bit]
    mine_ref[...] = value_ref[pl.ds(pl.multiple_of(side * half, 8), half), :]
    theirs_ref[...] = value_ref[pl.ds(pl.multiple_of((1 - side) * half, 8), half), :]


def add_two(line, a, b):
    def kernel(line_ref, a_ref, b_ref, out_ref):
        out_ref[...] = a_ref[...] + b_ref[...]

    return small_kernel(kernel, f32(*a.shape), (line, a, b), "add_two")


def add_and_halve(line, bit, a, b):
    half = f32(a.shape[0] // 2, a.shape[1])

    def kernel(line_ref, a_ref, b_ref, mine_ref, theirs_ref):
        size = mine_ref.shape[0]
        side = line_ref[0, bit]
        for out_ref, which in ((mine_ref, side), (theirs_ref, 1 - side)):
            rows = pl.ds(pl.multiple_of(which * size, 8), size)
            out_ref[...] = a_ref[rows, :] + b_ref[rows, :]

    return small_kernel(kernel, (half, half), (line, a, b), "add_and_halve")


def join_halves(line, bit, mine, theirs):
    def kernel(line_ref, mine_ref, theirs_ref, out_ref):
        size = mine_ref.shape[0]
        side = line_ref[0, bit]
        out_ref[pl.ds(pl.multiple_of(side * size, 8), size), :] = mine_ref[...]
        out_ref[pl.ds(pl.multiple_of((1 - side) * size, 8), size), :] = theirs_ref[...]

    shape = f32(2 * mine.shape[0], mine.shape[1])
    return small_kernel(kernel, shape, (line, mine, theirs), "join_halves")


class Total:
    def __init__(self, line, bits, mine, theirs, devices, halve_chips):
        self.line, self.bits, self.devices = line, bits, devices
        self.mine, self.theirs = mine, theirs
        first = 4 if halve_chips else 2
        self.rounds = ["core"] + ["halve"] * halve_chips
        while first < devices:
            self.rounds.append(first)
            first *= 2
        self.rounds += ["join"] * halve_chips + ["last"]

    def pass_on(self, value, mask):
        return lax.ppermute(value, "row", partner_pairs(self.devices, mask))

    def round(self, count=1):
        for _ in range(count):
            if not self.rounds:
                return
            kind = self.rounds.pop(0)
            line, (core_bit, chip_bit) = self.line, self.bits
            if kind == "core":
                got = self.pass_on(self.theirs, 1)
                if self.rounds[0] == "halve":
                    self.mine, self.theirs = add_and_halve(line, chip_bit, self.mine, got)
                else:
                    self.mine, self.theirs = add_two(line, self.mine, got), None
            elif kind == "halve":
                self.mine = add_two(line, self.mine, self.pass_on(self.theirs, 2))
                self.theirs = None
            elif kind == "join":
                self.mine = join_halves(line, chip_bit, self.mine, self.pass_on(self.mine, 2))
            elif kind == "last":
                self.mine = join_halves(line, core_bit, self.mine, self.pass_on(self.mine, 1))
            else:
                self.mine = add_two(line, self.mine, self.pass_on(self.mine, kind))

    def held(self):
        return [self.mine] if self.theirs is None else [self.mine, self.theirs]

    def hold(self, values):
        self.mine = values[0]
        if self.theirs is not None:
            self.theirs = values[1]


def gate_all(parts, extra=(), events=()):
    lists = [p.held() for p in parts]
    flat = [v for values in lists for v in values] + list(extra)
    flat = gate(flat, events)
    at = 0
    for p, values in zip(parts, lists):
        p.hold(flat[at : at + len(values)])
        at += len(values)
    return flat[at:]


def encode(values):
    size = jnp.abs(values)
    most = jnp.max(size, axis=0, keepdims=True)
    level = size / jnp.maximum(most, 1e-37)
    power = jnp.exp((level * code_span - code_middle) * ln2)
    return jnp.where(values < 0.0, -power, power).astype(jnp.bfloat16), most


def decode(code, most):
    code = code.astype(jnp.float32)
    level = (jnp.log(jnp.abs(code)) * (1.0 / ln2) + code_middle) * (1.0 / code_span)
    return jnp.where(code < 0.0, -level, level) * most


def write_rows(rows):
    at = lax.broadcasted_iota(jnp.int32, (scale_rows, rows[0].shape[1]), 0)
    block = jnp.zeros(at.shape, jnp.float32)
    for i, row in enumerate(rows):
        high = row.astype(jnp.bfloat16).astype(jnp.float32)
        block = jnp.where(at == 2 * i, high, block)
        block = jnp.where(at == 2 * i + 1, row - high, block)
    return block.astype(jnp.bfloat16)


def read_row(block, i):
    block = block.astype(jnp.float32)
    return block[2 * i : 2 * i + 1] + block[2 * i + 1 : 2 * i + 2]


def pack(line, values, mine, got, extra):
    rows, rank = values.shape
    sum_rows = mine.shape[0]
    half, sum_half = rows // 2, sum_rows // 2
    size = half + scale_rows + sum_half
    more = [] if extra is None else [extra]

    def kernel(line_ref, values_ref, mine_ref, got_ref, *refs):
        out_ref = refs[-1]
        sums = mine_ref[...] + got_ref[...]
        for h in range(2):
            code, most = encode(values_ref[h * half : (h + 1) * half, :])
            sum_code, sum_most = encode(sums[h * sum_half : (h + 1) * sum_half])
            scales = [most, sum_most]
            if more:
                scales += [refs[0][w : w + 1, :] for w in range(2)]
            at = h * size
            out_ref[at : at + half, :] = code
            out_ref[at + half : at + half + scale_rows, :] = write_rows(scales)
            out_ref[at + half + scale_rows : at + size, :] = sum_code

    return small_kernel(
        kernel,
        jax.ShapeDtypeStruct((2 * size, rank), jnp.bfloat16),
        (line, values, mine, got, *more),
        "pack",
    )


def prepare(line, bits, prior_cov, snapshots, basis):
    windows, rows, count = snapshots.shape
    rank = basis.shape[1]
    pieces = rows // 128
    half = f32(count // 2, rank)

    def total(x):
        return jnp.sum(jnp.sum(x, axis=0, keepdims=True), axis=1, keepdims=True)

    def kernel(line_ref, cov_ref, snap_ref, basis_ref, mine_ref, theirs_ref, share_ref, corner, part, sem):
        copies = []
        for at in range(pieces):
            first = pl.multiple_of(line_ref[0, 0] + at * 128, 128)
            copies.append(
                pltpu.make_async_copy(
                    cov_ref.at[pl.ds(at * 128, 128), pl.ds(first, 128)], corner.at[at], sem.at[at]
                )
            )
        for copy in copies:
            copy.start()
        part[...] = dot2(snap_ref[0], basis_ref[...], lead)
        store_halves(line_ref, bits[0], part, mine_ref, theirs_ref)
        energies = []
        for w in range(windows):
            snap = snap_ref[w].astype(jnp.float32)
            energies.append(total(snap * snap) * (1.0 / count))
        row_at = lax.broadcasted_iota(jnp.int32, (128, 128), 0)
        col_at = lax.broadcasted_iota(jnp.int32, (128, 128), 1)
        diagonal = jnp.zeros((128, 128), jnp.float32)
        for at in range(pieces):
            copies[at].wait()
            diagonal = diagonal + jnp.where(row_at == col_at, corner[at], 0.0)
        trace = total(diagonal)
        for w in range(windows):
            trace = forget_factor * trace + energies[w]
            share_ref[w : w + 1, :] = jnp.broadcast_to(trace, (1, rank))
        share_ref[windows:, :] = jnp.zeros((8 - windows, rank), jnp.float32)

    return pl.pallas_call(
        kernel,
        out_shape=(half, half, f32(8, rank)),
        in_specs=[in_smem, anywhere, in_vmem, in_vmem],
        out_specs=(in_vmem, in_vmem, in_vmem),
        scratch_shapes=[
            pltpu.VMEM((pieces, 128, 128), jnp.float32),
            pltpu.VMEM((count, rank), jnp.float32),
            pltpu.SemaphoreType.DMA((pieces,)),
        ],
        compiler_params=pltpu.CompilerParams(vmem_limit_bytes=50 * 2**20),
        name="prepare",
    )(line, prior_cov, snapshots, basis)


def add_products(line_ref, base, cov_ref, block_refs, state, first_window):
    running, own, other, misc, gram = state
    rows = cov_ref.shape[0]
    rank = running.shape[1]
    half = rows // 2
    sum_half = own.shape[0] // 2
    size = half + scale_rows + sum_half
    for at, block_ref in enumerate(block_refs):
        whole = block_ref.shape[0] == 2 * size
        first = pl.multiple_of(line_ref[0, base + at], 128)
        pieces, sums = [], []
        for h in (0, 1) if whole else (at // 2,):
            start = h * size if whole else 0
            scales = block_ref[start + half : start + half + scale_rows, :]
            most = read_row(scales, 0)
            pieces.append(decode(block_ref[start : start + half, :], most))
            coded = block_ref[start + half + scale_rows : start + size, :]
            sums.append(decode(coded, read_row(scales, 1)))
            if first_window:
                peak = jnp.maximum(misc[2:3], most)
                traces = [misc[w : w + 1] for w in range(2)]
                if h == 0:
                    traces = [t + read_row(scales, 2 + w) for w, t in enumerate(traces)]
                misc = jnp.concatenate(traces + [peak, misc[3:]], axis=0)
        block = jnp.concatenate(pieces, axis=0) if whole else pieces[0]
        if whole:
            piece = jnp.concatenate(sums, axis=0)
        else:
            nothing = jnp.zeros((sum_half, rank), jnp.float32)
            piece = jnp.concatenate(
                [sums[0], nothing] if at // 2 == 0 else [nothing, sums[0]], axis=0
            )
        if at % 2 == 0:
            own = own + piece
        else:
            other = other + piece
        high, low = split(block)
        both = jnp.concatenate([high, low], axis=1)
        cov_high, cov_low = split(cov_ref[:, pl.ds(first, block.shape[0])])
        wide = dot(cov_high, both, inner)
        running = running + (wide[:, :rank] + (wide[:, rank:] + dot(cov_low, high, inner)))
        if gram is not None:
            square = dot(high, both, lead)
            gram = gram + (square[:, :rank] + (square[:, rank:] + dot(low, high, lead)))
    return running, own, other, misc, gram


def empty_state(rows, rank, sum_rows, first_window):
    state = [jnp.zeros((n, rank), jnp.float32) for n in (rows, sum_rows, sum_rows, 8)]
    return state + [None if first_window else jnp.zeros((rank, rank), jnp.float32)]


def product_part(line, base, prior_cov, blocks, state, sum_rows, first_window):
    count = len(blocks)
    rows, rank = prior_cov.shape[0], blocks[0].shape[1]
    shapes = [f32(n, rank) for n in (rows, sum_rows, sum_rows, 8)]
    if not first_window:
        shapes.append(f32(rank, rank))
    outs = len(shapes)
    more = [] if state is None else list(state)

    def kernel(line_ref, cov_ref, *refs):
        old = empty_state(rows, rank, sum_rows, first_window)
        for i in range(len(more)):
            old[i] = refs[count + i][...]
        new = add_products(line_ref, base, cov_ref, refs[:count], old, first_window)
        for out_ref, value in zip(refs[-outs:], new):
            out_ref[...] = value

    return list(
        small_kernel(kernel, tuple(shapes), (line, prior_cov, *blocks, *more), "product_part")
    )


def product_end(line, bits, base, prior_cov, blocks, state, misc, snapshots, window):
    rows, order = prior_cov.shape
    rank = blocks[0].shape[1]
    windows, _, snap_count = snapshots.shape
    count = len(blocks)
    last = window == windows - 1
    first_window = window == 0
    sum_rows = state[1].shape[0]
    inv_snap = 1.0 / snap_count
    parts = len(state)
    more = [] if misc is None else [misc]
    if last:
        shapes = (f32(rows, rank), f32(rank // 2, rank), f32(rank // 2, rank), f32(rank, rank))
    else:
        shapes = (f32(rows, rank), f32(8, rank))

    def kernel(line_ref, cov_ref, *refs):
        block_refs, refs = refs[:count], refs[count:]
        old = [r[...] for r in refs[:parts]] + [None] * (5 - parts)
        snap_ref, refs = refs[parts], refs[parts + 1 :]
        if more:
            misc_ref, refs = refs[0], refs[1:]
        outs, sums_buf, gram_buf = refs[: len(shapes)], refs[-2], refs[-1]
        product, own, other, new_misc, gram = add_products(
            line_ref, base, cov_ref, block_refs, old, first_window
        )
        side = line_ref[0, bits[0]]
        sums_buf[pl.ds(pl.multiple_of(side * sum_rows, 8), sum_rows), :] = own
        sums_buf[pl.ds(pl.multiple_of((1 - side) * sum_rows, 8), sum_rows), :] = other
        applied = product * forget_factor ** (window + 1)
        for w in range(window + 1):
            at = w * snap_count
            weight = forget_factor ** (window - w) * inv_snap
            applied = applied + weight * dot2(
                snap_ref[w], sums_buf[at : at + snap_count, :], inner
            )
        if more:
            new_misc = misc_ref[...]
        factor = float(order) / new_misc[window : window + 1]
        if first_window:
            factor = factor / jnp.maximum(new_misc[2:3], 1e-37)
        applied = applied * factor
        outs[0][...] = applied
        if last:
            gram_buf[...] = lax.dot_general(
                applied,
                applied,
                lead,
                precision=lax.Precision.HIGHEST,
                preferred_element_type=jnp.float32,
            )
            store_halves(line_ref, bits[0], gram_buf, outs[1], outs[2])
            outs[3][...] = gram
        else:
            outs[1][...] = new_misc

    return pl.pallas_call(
        kernel,
        out_shape=shapes,
        in_specs=[in_smem] + [in_vmem] * (2 + count + parts + len(more)),
        out_specs=tuple(in_vmem for _ in shapes),
        scratch_shapes=[
            pltpu.VMEM((2 * sum_rows, rank), jnp.float32),
            pltpu.VMEM((rank, rank), jnp.float32),
        ],
        compiler_params=params,
        name="product_end",
    )(line, prior_cov, *blocks, *state, snapshots, *more)


def window_sums(line, bits, applied, snapshots):
    windows, _, snap_count = snapshots.shape
    rank = applied.shape[1]
    total = windows * snap_count
    half = f32(total // 2, rank)

    def kernel(line_ref, applied_ref, snap_ref, mine_ref, theirs_ref, part):
        for w in range(windows):
            at = w * snap_count
            part[at : at + snap_count, :] = dot2(snap_ref[w], applied_ref[...], lead)
        store_halves(line_ref, bits[0], part, mine_ref, theirs_ref)

    return pl.pallas_call(
        kernel,
        out_shape=(half, half),
        in_specs=[in_smem] + [in_vmem] * 2,
        out_specs=(in_vmem, in_vmem),
        scratch_shapes=[pltpu.VMEM((total, rank), jnp.float32)],
        compiler_params=params,
        name="window_sums",
    )(line, applied, snapshots)


panel = 8


def factor_panel(gram, inverse, first):
    rank = gram.shape[1]
    sub = lax.broadcasted_iota(jnp.int32, (panel, rank), 0)
    top, top_inverse = gram[:panel], inverse[:panel]
    columns = [
        jnp.broadcast_to(top[:, first + k : first + k + 1], (panel, rank)) for k in range(panel)
    ]
    roots = jnp.zeros((panel, rank), jnp.float32)
    for k in range(panel):
        root = lax.rsqrt(columns[k][k : k + 1])
        roots = jnp.where(sub == k, root, roots)
        scaled = jnp.where(sub > k, columns[k] * (root * root), 0.0)
        top = top - scaled * top[k : k + 1]
        top_inverse = top_inverse - scaled * top_inverse[k : k + 1]
        for m in range(k + 1, panel):
            columns[m] = columns[m] - scaled * columns[m][k : k + 1]
    top, top_inverse = top * roots, top_inverse * roots
    rest, rest_inverse = gram[panel:], inverse[panel:]
    if rest.shape[0]:
        change = lax.dot_general(
            top,
            jnp.concatenate([top, top_inverse], axis=1),
            lead,
            precision=lax.Precision.HIGHEST,
            preferred_element_type=jnp.float32,
        )[first + panel :]
        rest = rest - change[:, :rank]
        rest_inverse = rest_inverse - change[:, rank:]
    return top_inverse, rest, rest_inverse


def factor_rows(gram, inverse, first, end):
    done = []
    for at in range(first, end, panel):
        rows, gram, inverse = factor_panel(gram, inverse, at)
        done.append(rows)
    return jnp.concatenate(done, axis=0), gram, inverse


def identity(rank):
    return (
        lax.broadcasted_iota(jnp.int32, (rank, rank), 0)
        == lax.broadcasted_iota(jnp.int32, (rank, rank), 1)
    ).astype(jnp.float32)


def factor_some(line, state, first, end):
    rank = state[0].shape[1]
    left = rank - end
    begin = len(state) == 1
    shapes = (f32(end - first, rank),) + ((f32(left, rank),) * 2 if left else ())

    def kernel(line_ref, *refs):
        inverse = identity(rank) if begin else refs[1][...]
        new = factor_rows(refs[0][...], inverse, first, end)
        for out_ref, value in zip(refs[len(state) :], new):
            out_ref[...] = value

    return list(small_kernel(kernel, shapes, (line, *state), "factor_some"))


def finish(line, bits, gram, theirs, previous, applied):
    rank = applied.shape[1]
    half = rank // 2

    def kernel(line_ref, gram_ref, theirs_ref, *refs):
        applied_ref, out_ref, buf = refs[-3:]
        side = line_ref[0, bits[0]]
        buf[pl.ds(pl.multiple_of(side * half, 8), half), :] = gram_ref[...]
        buf[pl.ds(pl.multiple_of((1 - side) * half, 8), half), :] = theirs_ref[...]
        first = jnp.concatenate([r[...] for r in refs[:-3]], axis=0)

        def exact(a, b, dims):
            return lax.dot_general(
                a,
                b,
                dims,
                precision=lax.Precision.HIGHEST,
                preferred_element_type=jnp.float32,
            )

        second_gram = exact(exact(first, buf[...], inner), first, trail)
        second, _, _ = factor_rows(second_gram, identity(rank), 0, rank)
        out_ref[...] = dot3(applied_ref[...], exact(second, first, inner), trail)

    return pl.pallas_call(
        kernel,
        out_shape=f32(*applied.shape),
        in_specs=[in_smem] + [in_vmem] * (3 + len(previous)),
        out_specs=in_vmem,
        scratch_shapes=[pltpu.VMEM((rank, rank), jnp.float32)],
        compiler_params=params,
        name="finish",
    )(line, gram, theirs, *previous, applied)


def covariance_part(line, base, prior_cov, snapshots, blocks, filled):
    rows, _ = prior_cov.shape
    windows, _, snap_count = snapshots.shape
    count = len(blocks)
    more = [] if filled is None else [filled]
    inv_snap = 1.0 / snap_count

    def kernel(line_ref, cov_ref, snap_ref, *refs):
        block_refs, refs = refs[:count], refs[count + len(more) :]
        out_ref, out_bufs, sems = refs[0], refs[1:-1], refs[-1]
        copies = []
        for at in range(count):
            width = block_refs[at].shape[1]
            first = pl.multiple_of(line_ref[0, base + at], 128)
            columns = pl.ds(first, width)
            total = cov_ref[:, columns] * forget_factor**windows
            for w in range(windows):
                weight = forget_factor ** (windows - 1 - w) * inv_snap
                total = total + weight * dot(snap_ref[w], block_refs[at][w], trail)
            out_bufs[at][...] = total
            copy = pltpu.make_async_copy(out_bufs[at], out_ref.at[:, columns], sems.at[at])
            copy.start()
            copies.append(copy)
        for copy in copies:
            copy.wait()

    return pl.pallas_call(
        kernel,
        out_shape=f32(*prior_cov.shape),
        in_specs=[in_smem] + [in_vmem] * (2 + count) + [in_hbm] * len(more),
        out_specs=in_hbm,
        scratch_shapes=[pltpu.VMEM((rows, b.shape[1]), jnp.float32) for b in blocks]
        + [pltpu.SemaphoreType.DMA((count,))],
        input_output_aliases={3 + count: 0} if more else {},
        compiler_params=params,
        name="covariance_part",
    )(line, prior_cov, snapshots, *blocks, *more)


def local(devices, prior_cov, snapshots, prior_basis):
    rows = prior_cov.shape[0]
    rank = prior_basis.shape[1]
    windows, _, snap_count = snapshots.shape
    table = ring_table(devices, rows)
    me = lax.axis_index("row")
    line = lax.dynamic_slice_in_dim(jnp.asarray(table), me, 1, axis=0)
    entries = table.shape[1]
    bits = (entries - 2, entries - 1)
    steps = devices // 4
    starts = [0] + [2 + 4 * at for at in range(steps)]
    swap = partner_pairs(devices, 1)
    snap_ring = Ring(snapshots, devices, 1)

    def fill(filled, first, end):
        blocks = [b for group in snap_ring.groups[first:end] for b in group]
        return covariance_part(line, starts[first], prior_cov, snapshots, blocks, filled)

    mine, theirs, share = prepare(line, bits, prior_cov, snapshots, prior_basis)
    values, misc = prior_basis, None
    for window in range(windows):
        first_window = window == 0
        got = lax.ppermute(theirs, "row", swap)
        ring = Ring(pack(line, values, mine, got, share if first_window else None), devices, 0)
        sum_rows = mine.shape[0]
        state = None
        for phase in range(1, steps + 1):
            ring.pass_on()
            ring.step()
            if phase >= 2:
                group = phase - 2
                state = product_part(
                    line,
                    starts[group],
                    prior_cov,
                    ring.groups[group],
                    state,
                    sum_rows,
                    first_window,
                )
            collect = not first_window and phase == 2
            state = gate_all([ring, snap_ring] if collect else [ring], state or []) or None
            if collect:
                snap_ring.pass_on()
                snap_ring.step()
        ring.pass_on()
        if first_window:
            snap_ring.ahead = snap_ring.behind = gate([snapshots], [ring.ahead])[0]
            snap_ring.pass_on()
            snap_ring.step()
        state = product_part(
            line,
            starts[steps - 1],
            prior_cov,
            ring.groups[steps - 1],
            state,
            sum_rows,
            first_window,
        )
        result = product_end(
            line,
            bits,
            starts[steps],
            prior_cov,
            ring.groups[steps],
            state,
            misc,
            snapshots,
            window,
        )
        if first_window:
            values, misc = result
            mine, theirs = window_sums(line, bits, values, snapshots)
    applied, mine, theirs, first_gram = result
    total = Total(line, bits, mine, theirs, devices, False)
    total.rounds.pop()
    pieces, left = [], [first_gram]
    count = len(total.rounds)
    at = 0
    while total.rounds:
        total.round()
        end = rank if not total.rounds else min(rank, at + rank // (panel * count) * panel)
        done, *left = factor_some(line, left, at, end)
        pieces.append(done)
        at = end
        (pieces[-1], *left) = gate_all([total], [pieces[-1]] + left)
    new_cov = fill(None, 0, 2)
    theirs = lax.ppermute(total.mine, "row", swap)
    while snap_ring.done < steps:
        snap_ring.pass_on()
        snap_ring.step()
    new_basis = finish(line, bits, total.mine, theirs, pieces, applied)
    snap_ring.pass_on()
    for at in range(2, steps + 1):
        new_cov = fill(new_cov, at, at + 1)
    return (new_cov, new_basis)


def solution(mesh):
    return jax.shard_map(
        functools.partial(local, mesh.shape["row"]),
        mesh=mesh,
        in_specs=(
            P(("band", "row"), None),
            P(None, ("band", "row"), None),
            P(("band", "row"), None),
        ),
        out_specs=(P(("band", "row"), None), P(("band", "row"), None)),
        check_vma=False,
    )
```

time: 458 us -> 172 us (0.38)
  waiting for transfers between devices: 325 us -> 61.1 us
  matrix products: 65.3 us -> 0 us
  Pallas kernels: 0 us -> 64 us
  other arithmetic: 47.3 us -> 0 us
  starting transfers between devices: 0.42 us -> 34.4 us
  between operations: 14.2 us -> 1.32 us
  local copies, waits for them, and re-layouts: 4.55 us -> 10.4 us
    psum x2 -> x0, waiting for transfers between devices: 165 us -> none  [local(): gram_matrix = lax.psum(lead_contract(applied, applied, exact), 'row')]
    all_gather x4 -> x0, waiting for transfers between devices: 158 us -> none  [the longest x2 83.9 us: local(): lax.all_gather(snapshot_panel, 'row', axis=0, tiled=True)]
    pallas_call x0 -> x40, Pallas kernels: none -> 64 us  [the longest x18 30 us: small_kernel(): pl.pallas_call(kernel, out_shape=out_shape, in_specs=[in_smem] + [in_vmem...]
    dot_general x6 -> x0, matrix products: 63.7 us -> none  [the longest x2 32.6 us: add_block(): jnp.dot(matrix, block_rows, precision=exact, preferred_element_type=jnp.f...]
    ppermute x0 -> x58, waiting for transfers between devices: none -> 61.1 us  [the longest x12 41 us: step(): self.ahead = lax.ppermute(ahead, 'row', self.forth)]
    another operation x10 -> x0, other arithmetic: 45.6 us -> none  [the longest x6 24.8 us: orthonormal(): lower_factor = jnp.linalg.cholesky(gram_matrix)]
    ppermute x0 -> x58, starting transfers between devices: none -> 34.4 us  [the longest x12 18.3 us: step(): self.ahead = lax.ppermute(ahead, 'row', self.forth)]
    unnamed x3 -> x11, local copies, waits for them, and re-layouts: 0.84 us -> 9.59 us
  transfers between devices with their start and end apart: 6 -> 58, of which waited for: 6 -> 20; matrix products, arithmetic and copies ran while one was open for 12% -> 0% of each run, Pallas kernels for 0% -> 33%
where the time goes in v1:
time: 172 us; the launch traced here: 171 us
  Pallas kernels  64 us (37%)
  waiting for transfers between devices  61.1 us (36%)
  starting transfers between devices  34.4 us (20%)
  local copies, waits for them, and re-layouts  10.4 us (6%)
    ppermute x12, waiting for transfers between devices, step(): self.ahead = lax.ppermute(ahead, 'row', self.forth)  41 us
    pallas_call x18, Pallas kernels, small_kernel(): pl.pallas_call(kernel, out_shape=out_shape, in_specs=[in_smem] + [in_vmem...  30 us
    ppermute x12, starting transfers between devices, step(): self.ahead = lax.ppermute(ahead, 'row', self.forth)  18.3 us
    pallas_call x4, Pallas kernels, covariance_part(): pl.pallas_call(kernel, out_shape=f32(*prior_cov.shape), in_specs=[in_smem...  16.5 us
    ppermute x12, waiting for transfers between devices, step(): self.behind = lax.ppermute(behind, 'row', self.back)  13 us
    pallas_call x1, Pallas kernels, finish(): pl.pallas_call(kernel, out_shape=f32(*applied.shape), in_specs=[in_smem]...  10.8 us
    unnamed x11, local copies, waits for them, and re-layouts  9.59 us
    ppermute x12, starting transfers between devices, step(): self.behind = lax.ppermute(behind, 'row', self.back)  8.22 us
  transfers between devices with their start and end apart: 58, of which 20 were waited for; matrix products, arithmetic and copies ran while one was open for 0% of the time, Pallas kernels for 33%

profile of v1, /device:TPU:0, one launch (start us, length us, event | category | flops | bytes accessed | tf_op | source)
XLA Modules:
  0.0 171.2 jit_solution(11864842090965295824)
XLA Ops:
  7.3 3.0 %collective-permute-start.1 = (bf16[672,128]{1,0:T(8,128)(2,1)S(1)}, bf16[672,128]{1,0:T(8,128)(2,1)S(1)}, u32[]{:S(2)}, u32[]{:S(2)}) collective-permute-start(bf16[672,128]{1,0:T(8,128)(2,1)S(1)} %pack.2.refs_0_), channel_id=1, source_target_pairs={{0,4},{1,5},{4,8},{5,9},{8,12},{9,13},{12,14},{13,15},{14,10},{15,... | collective-permute-start | bytes 516104 | tf_op jit(solution)/shard_map/ppermute | solution.py:128
  10.3 4.6 %collective-permute-done.1.refs_0_ = bf16[672,128]{1,0:T(8,128)(2,1)S(1)} collective-permute-done((bf16[672,128]{1,0:T(8,128)(2,1)S(1)}, bf16[672,128]{1,0:T(8,128)(2,1)S(1)}, u32[]{:S(2)}, u32[]{:S(2)}) %collective-permute-start.1) | collective-permute-done | bytes 172064 | tf_op jit(solution)/shard_map/ppermute | solution.py:128
  18.9 5.8 %copy-done = f32[512,8192]{1,0:T(8,128)S(1)} copy-done((f32[512,8192]{1,0:T(8,128)S(1)}, f32[512,8192]{1,0:T(8,128)}, u32[]{:S(2)}) %copy-start) | copy-done | bytes 16777240
  30.5 1.9 %product_part.9 = (f32[512,128]{1,0:T(8,128)S(1)}, f32[128,128]{1,0:T(8,128)S(1)}, f32[128,128]{1,0:T(8,128)S(1)}, f32[8,128]{1,0:T(8,128)S(1)}) custom-call(s32[1,20]{1,0:T(1,128)S(1)} %constant_dynamic-slice_fusion.line_ref, f32[512,8192]{1,0:T(8,128)S(1)} %copy-done.1, bf16[672,128]{1,0:T(8,128)(2,1)S(1)} %get-tuple-element.135.refs_0_, ...), custom_call_target="tpu_custom_call" | custom-call | tf_op jit(solution)/shard_map/product_part/pallas_call | solution.py:144
  51.3 13.8 %collective-permute-done.19.refs_0_ = bf16[800,128]{1,0:T(8,128)(2,1)S(1)} collective-permute-done((bf16[800,128]{1,0:T(8,128)(2,1)S(1)}, bf16[800,128]{1,0:T(8,128)(2,1)S(1)}, u32[]{:S(2)}, u32[]{:S(2)}) %collective-permute-start.19) | collective-permute-done | bytes 204832 | tf_op jit(solution)/shard_map/ppermute | solution.py:128
  70.4 3.3 %collective-permute-done.22.refs_0_ = bf16[800,128]{1,0:T(8,128)(2,1)S(1)} collective-permute-done((bf16[800,128]{1,0:T(8,128)(2,1)S(1)}, bf16[800,128]{1,0:T(8,128)(2,1)S(1)}, u32[]{:S(2)}, u32[]{:S(2)}) %collective-permute-start.22) | collective-permute-done | bytes 204832 | tf_op jit(solution)/shard_map/ppermute | solution.py:128
  78.6 5.0 %collective-permute-done.43.refs_0_ = bf16[800,128]{1,0:T(8,128)(2,1)S(1)} collective-permute-done((bf16[800,128]{1,0:T(8,128)(2,1)S(1)}, bf16[800,128]{1,0:T(8,128)(2,1)S(1)}, u32[]{:S(2)}, u32[]{:S(2)}) %collective-permute-start.43) | collective-permute-done | bytes 204832 | tf_op jit(solution)/shard_map/ppermute | solution.py:128
  84.1 2.3 %product_part.13 = (f32[512,128]{1,0:T(8,128)S(1)}, f32[256,128]{1,0:T(8,128)S(1)}, f32[256,128]{1,0:T(8,128)S(1)}, f32[8,128]{1,0:T(8,128)S(1)}, f32[128,128]{1,0:T(8,128)S(1)}) custom-call(s32[1,20]{1,0:T(1,128)S(1)} %constant_dynamic-slice_fusion.line_ref, f32[512,8192]{1,0:T(8,128)S(1)} %copy-done.1, bf16[800,128]{1,0:T(8,128)(2,1)S(1)} %get-tuple-element.181.refs_0_, ...), custom_call_target="tpu_custom_call" | custom-call | tf_op jit(solution)/shard_map/product_part/pallas_call | solution.py:144
  88.6 7.1 %collective-permute-done.47.refs_0_ = bf16[400,128]{1,0:T(8,128)(2,1)S(1)} collective-permute-done((bf16[400,128]{1,0:T(8,128)(2,1)S(1)}, bf16[400,128]{1,0:T(8,128)(2,1)S(1)}, u32[]{:S(2)}, u32[]{:S(2)}) %collective-permute-start.47) | collective-permute-done | bytes 102432 | tf_op jit(solution)/shard_map/ppermute | solution.py:128
  96.3 2.4 %product_part.14 = (f32[512,128]{1,0:T(8,128)S(1)}, f32[256,128]{1,0:T(8,128)S(1)}, f32[256,128]{1,0:T(8,128)S(1)}, f32[8,128]{1,0:T(8,128)S(1)}, f32[128,128]{1,0:T(8,128)S(1)}) custom-call(s32[1,20]{1,0:T(1,128)S(1)} %constant_dynamic-slice_fusion.line_ref, f32[512,8192]{1,0:T(8,128)S(1)} %copy-done.1, bf16[800,128]{1,0:T(8,128)(2,1)S(1)} %get-tuple-element.192.refs_0_, ...), custom_call_target="tpu_custom_call" | custom-call | tf_op jit(solution)/shard_map/product_part/pallas_call | solution.py:144
  101.0 2.4 %product_part.15 = (f32[512,128]{1,0:T(8,128)S(1)}, f32[256,128]{1,0:T(8,128)S(1)}, f32[256,128]{1,0:T(8,128)S(1)}, f32[8,128]{1,0:T(8,128)S(1)}, f32[128,128]{1,0:T(8,128)S(1)}) custom-call(s32[1,20]{1,0:T(1,128)S(1)} %constant_dynamic-slice_fusion.line_ref, f32[512,8192]{1,0:T(8,128)S(1)} %copy-done.1, bf16[800,128]{1,0:T(8,128)(2,1)S(1)} %get-tuple-element.206.refs_0_, ...), custom_call_target="tpu_custom_call" | custom-call | tf_op jit(solution)/shard_map/product_part/pallas_call | solution.py:144
  103.4 2.2 %product_end.3 = (f32[512,128]{1,0:T(8,128)S(1)}, f32[64,128]{1,0:T(8,128)S(1)}, f32[64,128]{1,0:T(8,128)S(1)}, f32[128,128]{1,0:T(8,128)S(1)}) custom-call(s32[1,20]{1,0:T(1,128)S(1)} %constant_dynamic-slice_fusion.line_ref, f32[512,8192]{1,0:T(8,128)S(1)} %copy-done.1, bf16[400,128]{1,0:T(8,128)(2,1)S(1)} %get-tuple-element.220.refs_0_, ...), custom_call_target="tpu_custom_call" | custom-call | tf_op jit(solution)/shard_map/product_end/pallas_call | solution.py:493
  105.7 2.7 %factor_some.4 = (f32[32,128]{1,0:T(8,128)S(1)}, f32[96,128]{1,0:T(8,128)S(1)}, f32[96,128]{1,0:T(8,128)S(1)}) custom-call(s32[1,20]{1,0:T(1,128)S(1)} %constant_dynamic-slice_fusion.line_ref, f32[128,128]{1,0:T(8,128)S(1)} %get-tuple-element.237.refs_0_), custom_call_target="tpu_custom_call" | custom-call | tf_op jit(solution)/shard_map/factor_some/pallas_call | solution.py:144
  109.6 2.8 %factor_some.5 = (f32[32,128]{1,0:T(8,128)S(1)}, f32[64,128]{1,0:T(8,128)S(1)}, f32[64,128]{1,0:T(8,128)S(1)}) custom-call(s32[1,20]{1,0:T(1,128)S(1)} %constant_dynamic-slice_fusion.line_ref, f32[96,128]{1,0:T(8,128)S(1)} %get-tuple-element.242.refs_0_, f32[96,128]{1,0:T(8,128)S(1)} %get-tuple-element.243.refs_1_), custom_call_target="tpu_custom_call" | custom-call | tf_op jit(solution)/shard_map/factor_some/pallas_call | solution.py:144
  115.7 2.8 %factor_some.6 = (f32[32,128]{1,0:T(8,128)S(1)}, f32[32,128]{1,0:T(8,128)S(1)}, f32[32,128]{1,0:T(8,128)S(1)}) custom-call(s32[1,20]{1,0:T(1,128)S(1)} %constant_dynamic-slice_fusion.line_ref, f32[64,128]{1,0:T(8,128)S(1)} %get-tuple-element.248.refs_0_, f32[64,128]{1,0:T(8,128)S(1)} %get-tuple-element.249.refs_1_), custom_call_target="tpu_custom_call" | custom-call | tf_op jit(solution)/shard_map/factor_some/pallas_call | solution.py:144
  119.5 2.0 %collective-permute-start.34 = (bf16[2,512,256]{2,1,0:T(8,128)(2,1)S(1)}, bf16[2,512,256]{2,1,0:T(8,128)(2,1)S(1)}, u32[]{:S(2)}, u32[]{:S(2)}) collective-permute-start(bf16[2,512,256]{2,1,0:T(8,128)(2,1)S(1)} %collective-permute-done.33.refs_2_), channel_id=1, source_target_pairs={{0,2},{1,3},{4,0},{5,1},{8,4},{9,5},{12,8},{13,9},{14,12},{15,13},... | collective-permute-start | bytes 1572872 | tf_op jit(solution)/shard_map/ppermute | solution.py:129
  122.0 5.4 %collective-permute-done.56.b_ref = f32[64,128]{1,0:T(8,128)S(1)} collective-permute-done((f32[64,128]{1,0:T(8,128)S(1)}, f32[64,128]{1,0:T(8,128)S(1)}, u32[]{:S(2)}, u32[]{:S(2)}) %collective-permute-start.56) | collective-permute-done | bytes 32800 | tf_op jit(solution)/shard_map/ppermute | solution.py:208
  127.4 2.3 %factor_some.7.refs_1_ = f32[32,128]{1,0:T(8,128)S(1)} custom-call(s32[1,20]{1,0:T(1,128)S(1)} %constant_dynamic-slice_fusion.line_ref, f32[32,128]{1,0:T(8,128)S(1)} %get-tuple-element.254.refs_0_, f32[32,128]{1,0:T(8,128)S(1)} %get-tuple-element.255.refs_1_), custom_call_target="tpu_custom_call" | custom-call | tf_op jit(solution)/shard_map/factor_some/pallas_call | solution.py:144
  135.9 5.9 %collective-permute-done.31.refs_0_ = bf16[2,256,256]{2,1,0:T(8,128)(2,1)S(1)} collective-permute-done((bf16[2,256,256]{2,1,0:T(8,128)(2,1)S(1)}, bf16[2,256,256]{2,1,0:T(8,128)(2,1)S(1)}, u32[]{:S(2)}, u32[]{:S(2)}) %collective-permute-start.31) | collective-permute-done | bytes 262176 | tf_op jit(solution)/shard_map/ppermute | solution.py:128
  143.6 5.6 %covariance_part.4.refs_4_ = f32[512,8192]{1,0:T(8,128)} custom-call(s32[1,20]{1,0:T(1,128)S(1)} %constant_dynamic-slice_fusion.line_ref, f32[512,8192]{1,0:T(8,128)S(1)} %copy-done.1, bf16[2,512,256]{2,1,0:T(8,128)(2,1)S(1)} %copy-done.3, bf16[2,512,256]{2,1,0:T(8,128)(2,1)S(1)} %gate.18.refs_0_, bf16[2,512,256]{2,1,0:T(8,128)(2,1)S(1)} %get-tuple-element.191.refs_1_, ...), custom_call_target="tpu_custom_call" | custom-call | tf_op jit(solution)/shard_map/covariance_part/pallas_call | solution.py:655
  149.2 10.8 %finish.1 = f32[512,128]{1,0:T(8,128)} custom-call(s32[1,20]{1,0:T(1,128)S(1)} %constant_dynamic-slice_fusion.line_ref, f32[64,128]{1,0:T(8,128)S(1)} %get-tuple-element.256.gram_ref, f32[64,128]{1,0:T(8,128)S(1)} %collective-permute-done.57.theirs_ref, f32[32,128]{1,0:T(8,128)S(1)} %get-tuple-element.257.refs_0_, f32[32,128]{1,0:T(8,128)S(1)} %get-tuple-element.258.refs_1_, ...), custom_call_target="tpu_custom_call" | custom-call | tf_op jit(solution)/shard_map/finish/pallas_call | solution.py:618
  160.0 4.2 %covariance_part.5.refs_4_ = f32[512,8192]{1,0:T(8,128)} custom-call(s32[1,20]{1,0:T(1,128)S(1)} %constant_dynamic-slice_fusion.line_ref, f32[512,8192]{1,0:T(8,128)S(1)} %copy-done.1, bf16[2,512,256]{2,1,0:T(8,128)(2,1)S(1)} %copy-done.3, bf16[2,512,256]{2,1,0:T(8,128)(2,1)S(1)} %collective-permute-done.29.refs_0_, ...), custom_call_target="tpu_custom_call", output_to_operand_aliasing={{}: (7, {})} | custom-call | tf_op jit(solution)/shard_map/covariance_part/pallas_call | solution.py:655
  164.3 4.2 %covariance_part.6.refs_4_ = f32[512,8192]{1,0:T(8,128)} custom-call(s32[1,20]{1,0:T(1,128)S(1)} %constant_dynamic-slice_fusion.line_ref, f32[512,8192]{1,0:T(8,128)S(1)} %copy-done.1, bf16[2,512,256]{2,1,0:T(8,128)(2,1)S(1)} %copy-done.3, bf16[2,512,256]{2,1,0:T(8,128)(2,1)S(1)} %collective-permute-done.30.refs_0_, ...), custom_call_target="tpu_custom_call", output_to_operand_aliasing={{}: (7, {})} | custom-call | tf_op jit(solution)/shard_map/covariance_part/pallas_call | solution.py:655
  168.5 2.5 %covariance_part.7 = f32[512,8192]{1,0:T(8,128)} custom-call(s32[1,20]{1,0:T(1,128)S(1)} %constant_dynamic-slice_fusion.line_ref, f32[512,8192]{1,0:T(8,128)S(1)} %copy-done.1, bf16[2,512,256]{2,1,0:T(8,128)(2,1)S(1)} %copy-done.3, bf16[2,256,256]{2,1,0:T(8,128)(2,1)S(1)} %collective-permute-done.31.refs_0_, ...), custom_call_target="tpu_custom_call", output_to_operand_aliasing={{}: (7, {})} | custom-call | tf_op jit(solution)/shard_map/covariance_part/pallas_call | solution.py:655
  (150 shorter events, 64.8 us)
Async XLA Ops:
  16.4 9.6 %collective-permute-start.4 = (bf16[672,128]{1,0:T(8,128)(2,1)S(1)}, bf16[672,128]{1,0:T(8,128)(2,1)S(1)}, u32[]{:S(2)}, u32[]{:S(2)}) collective-permute-start(bf16[672,128]{1,0:T(8,128)(2,1)S(1)} %get-tuple-element.135.refs_0_), channel_id=1, source_target_pairs={{0,4},{1,5},{4,8},{5,9},{8,12},{9,13},{12,14},{13,15},{14,10},{15,... | collective-permute-start | bytes 516104 | tf_op jit(solution)/shard_map/ppermute | solution.py:128
  46.4 21.7 %collective-permute-start.26 = (bf16[2,512,256]{2,1,0:T(8,128)(2,1)S(1)}, bf16[2,512,256]{2,1,0:T(8,128)(2,1)S(1)}, u32[]{:S(2)}, u32[]{:S(2)}) collective-permute-start(bf16[2,512,256]{2,1,0:T(8,128)(2,1)S(1)} %gate.18.refs_0_), channel_id=1, source_target_pairs={{0,4},{1,5},{4,8},{5,9},{8,12},{9,13},{12,14},{13,15},{14,10},{15,... | collective-permute-start | bytes 1572872 | tf_op jit(solution)/shard_map/ppermute | solution.py:128
  47.9 20.6 %collective-permute-start.27 = (bf16[2,512,256]{2,1,0:T(8,128)(2,1)S(1)}, bf16[2,512,256]{2,1,0:T(8,128)(2,1)S(1)}, u32[]{:S(2)}, u32[]{:S(2)}) collective-permute-start(bf16[2,512,256]{2,1,0:T(8,128)(2,1)S(1)} %gate.18.refs_0_), channel_id=1, source_target_pairs={{0,2},{1,3},{4,0},{5,1},{8,4},{9,5},{12,8},{13,9},{14,12},{15,13},... | collective-permute-start | bytes 1572872 | tf_op jit(solution)/shard_map/ppermute | solution.py:129
  49.2 15.9 %collective-permute-start.19 = (bf16[800,128]{1,0:T(8,128)(2,1)S(1)}, bf16[800,128]{1,0:T(8,128)(2,1)S(1)}, u32[]{:S(2)}, u32[]{:S(2)}) collective-permute-start(bf16[800,128]{1,0:T(8,128)(2,1)S(1)} %pack.3.refs_0_), channel_id=1, source_target_pairs={{0,4},{1,5},{4,8},{5,9},{8,12},{9,13},{12,14},{13,15},{14,10},{15,... | collective-permute-start | bytes 614408 | tf_op jit(solution)/shard_map/ppermute | solution.py:128
  50.8 19.6 %collective-permute-start.28 = (bf16[2,512,256]{2,1,0:T(8,128)(2,1)S(1)}, bf16[2,512,256]{2,1,0:T(8,128)(2,1)S(1)}, u32[]{:S(2)}, u32[]{:S(2)}) collective-permute-start(bf16[2,512,256]{2,1,0:T(8,128)(2,1)S(1)} %gate.18.refs_0_), channel_id=1, source_target_pairs={{0,1},{1,0},{2,3},{3,2},{4,5},{5,4},{6,7},{7,6},{8,9},{9,8},{10,11... | collective-permute-start | bytes 1572872 | tf_op jit(solution)/shard_map/ppermute | solution.py:118
  50.8 15.6 %collective-permute-start.20 = (bf16[800,128]{1,0:T(8,128)(2,1)S(1)}, bf16[800,128]{1,0:T(8,128)(2,1)S(1)}, u32[]{:S(2)}, u32[]{:S(2)}) collective-permute-start(bf16[800,128]{1,0:T(8,128)(2,1)S(1)} %pack.3.refs_0_), channel_id=1, source_target_pairs={{0,2},{1,3},{4,0},{5,1},{8,4},{9,5},{12,8},{13,9},{14,12},{15,13},... | collective-permute-start | bytes 614408 | tf_op jit(solution)/shard_map/ppermute | solution.py:129
  76.1 10.4 %collective-permute-start.44 = (bf16[800,128]{1,0:T(8,128)(2,1)S(1)}, bf16[800,128]{1,0:T(8,128)(2,1)S(1)}, u32[]{:S(2)}, u32[]{:S(2)}) collective-permute-start(bf16[800,128]{1,0:T(8,128)(2,1)S(1)} %get-tuple-element.193.refs_2_), channel_id=1, source_target_pairs={{0,2},{1,3},{4,0},{5,1},{8,4},{9,5},{12,8},{13,9},{14,12},{15,13},... | collective-permute-start | bytes 614408 | tf_op jit(solution)/shard_map/ppermute | solution.py:129
  77.6 8.8 %collective-permute-start.45 = (bf16[800,128]{1,0:T(8,128)(2,1)S(1)}, bf16[800,128]{1,0:T(8,128)(2,1)S(1)}, u32[]{:S(2)}, u32[]{:S(2)}) collective-permute-start(bf16[800,128]{1,0:T(8,128)(2,1)S(1)} %get-tuple-element.192.refs_0_), channel_id=1, source_target_pairs={{0,1},{1,0},{2,3},{3,2},{4,5},{5,4},{6,7},{7,6},{8,9},{9,8},{10,11... | collective-permute-start | bytes 614408 | tf_op jit(solution)/shard_map/ppermute | solution.py:118
  77.6 8.8 %collective-permute-start.46 = (bf16[800,128]{1,0:T(8,128)(2,1)S(1)}, bf16[800,128]{1,0:T(8,128)(2,1)S(1)}, u32[]{:S(2)}, u32[]{:S(2)}) collective-permute-start(bf16[800,128]{1,0:T(8,128)(2,1)S(1)} %get-tuple-element.193.refs_2_), channel_id=1, source_target_pairs={{0,1},{1,0},{2,3},{3,2},{4,5},{5,4},{6,7},{7,6},{8,9},{9,8},{10,11... | collective-permute-start | bytes 614408 | tf_op jit(solution)/shard_map/ppermute | solution.py:118
  78.1 36.0 %collective-permute-start.29 = (bf16[2,512,256]{2,1,0:T(8,128)(2,1)S(1)}, bf16[2,512,256]{2,1,0:T(8,128)(2,1)S(1)}, u32[]{:S(2)}, u32[]{:S(2)}) collective-permute-start(bf16[2,512,256]{2,1,0:T(8,128)(2,1)S(1)} %get-tuple-element.189.refs_2_), channel_id=1, source_target_pairs={{0,4},{1,5},{4,8},{5,9},{8,12},{9,13},{12,14},{13,15},{14,10},{15,... | collective-permute-start | bytes 1572872 | tf_op jit(solution)/shard_map/ppermute | solution.py:128
  83.6 35.9 %collective-permute-start.33 = (bf16[2,512,256]{2,1,0:T(8,128)(2,1)S(1)}, bf16[2,512,256]{2,1,0:T(8,128)(2,1)S(1)}, u32[]{:S(2)}, u32[]{:S(2)}) collective-permute-start(bf16[2,512,256]{2,1,0:T(8,128)(2,1)S(1)} %get-tuple-element.190.refs_4_), channel_id=1, source_target_pairs={{0,2},{1,3},{4,0},{5,1},{8,4},{9,5},{12,8},{13,9},{14,12},{15,13},... | collective-permute-start | bytes 1572872 | tf_op jit(solution)/shard_map/ppermute | solution.py:129
  86.5 9.2 %collective-permute-start.47 = (bf16[400,128]{1,0:T(8,128)(2,1)S(1)}, bf16[400,128]{1,0:T(8,128)(2,1)S(1)}, u32[]{:S(2)}, u32[]{:S(2)}) collective-permute-start(bf16[400,128]{1,0:T(8,128)(2,1)S(1)} %slice.22), channel_id=1, source_target_pairs={{0,4},{1,5},{4,8},{5,9},{8,12},{9,13},{12,14},{13,15},{14,10},{15,... | collective-permute-start | bytes 307208 | tf_op jit(solution)/shard_map/ppermute | solution.py:128
  88.1 12.3 %collective-permute-start.49 = (bf16[800,128]{1,0:T(8,128)(2,1)S(1)}, bf16[800,128]{1,0:T(8,128)(2,1)S(1)}, u32[]{:S(2)}, u32[]{:S(2)}) collective-permute-start(bf16[800,128]{1,0:T(8,128)(2,1)S(1)} %get-tuple-element.206.refs_0_), channel_id=1, source_target_pairs={{0,1},{1,0},{2,3},{3,2},{4,5},{5,4},{6,7},{7,6},{8,9},{9,8},{10,11... | collective-permute-start | bytes 614408 | tf_op jit(solution)/shard_map/ppermute | solution.py:118
  88.1 12.3 %collective-permute-start.50 = (bf16[800,128]{1,0:T(8,128)(2,1)S(1)}, bf16[800,128]{1,0:T(8,128)(2,1)S(1)}, u32[]{:S(2)}, u32[]{:S(2)}) collective-permute-start(bf16[800,128]{1,0:T(8,128)(2,1)S(1)} %get-tuple-element.207.refs_2_), channel_id=1, source_target_pairs={{0,1},{1,0},{2,3},{3,2},{4,5},{5,4},{6,7},{7,6},{8,9},{9,8},{10,11... | collective-permute-start | bytes 614408 | tf_op jit(solution)/shard_map/ppermute | solution.py:118
  114.1 16.2 %collective-permute-start.30 = (bf16[2,512,256]{2,1,0:T(8,128)(2,1)S(1)}, bf16[2,512,256]{2,1,0:T(8,128)(2,1)S(1)}, u32[]{:S(2)}, u32[]{:S(2)}) collective-permute-start(bf16[2,512,256]{2,1,0:T(8,128)(2,1)S(1)} %collective-permute-done.29.refs_0_), channel_id=1, source_target_pairs={{0,4},{1,5},{4,8},{5,9},{8,12},{9,13},{12,14},{13,15},{14,10},{15,... | collective-permute-start | bytes 1572872 | tf_op jit(solution)/shard_map/ppermute | solution.py:128
  119.5 13.3 %collective-permute-start.34 = (bf16[2,512,256]{2,1,0:T(8,128)(2,1)S(1)}, bf16[2,512,256]{2,1,0:T(8,128)(2,1)S(1)}, u32[]{:S(2)}, u32[]{:S(2)}) collective-permute-start(bf16[2,512,256]{2,1,0:T(8,128)(2,1)S(1)} %collective-permute-done.33.refs_2_), channel_id=1, source_target_pairs={{0,2},{1,3},{4,0},{5,1},{8,4},{9,5},{12,8},{13,9},{14,12},{15,13},... | collective-permute-start | bytes 1572872 | tf_op jit(solution)/shard_map/ppermute | solution.py:129
  121.5 11.3 %collective-permute-start.41 = (bf16[2,512,256]{2,1,0:T(8,128)(2,1)S(1)}, bf16[2,512,256]{2,1,0:T(8,128)(2,1)S(1)}, u32[]{:S(2)}, u32[]{:S(2)}) collective-permute-start(bf16[2,512,256]{2,1,0:T(8,128)(2,1)S(1)} %get-tuple-element.189.refs_2_), channel_id=1, source_target_pairs={{0,1},{1,0},{2,3},{3,2},{4,5},{5,4},{6,7},{7,6},{8,9},{9,8},{10,11... | collective-permute-start | bytes 1572872 | tf_op jit(solution)/shard_map/ppermute | solution.py:118
  121.5 13.1 %collective-permute-start.42 = (bf16[2,512,256]{2,1,0:T(8,128)(2,1)S(1)}, bf16[2,512,256]{2,1,0:T(8,128)(2,1)S(1)}, u32[]{:S(2)}, u32[]{:S(2)}) collective-permute-start(bf16[2,512,256]{2,1,0:T(8,128)(2,1)S(1)} %get-tuple-element.190.refs_4_), channel_id=1, source_target_pairs={{0,1},{1,0},{2,3},{3,2},{4,5},{5,4},{6,7},{7,6},{8,9},{9,8},{10,11... | collective-permute-start | bytes 1572872 | tf_op jit(solution)/shard_map/ppermute | solution.py:118
  132.7 27.3 %collective-permute-start.40 = (bf16[2,512,256]{2,1,0:T(8,128)(2,1)S(1)}, bf16[2,512,256]{2,1,0:T(8,128)(2,1)S(1)}, u32[]{:S(2)}, u32[]{:S(2)}) collective-permute-start(bf16[2,512,256]{2,1,0:T(8,128)(2,1)S(1)} %collective-permute-done.33.refs_2_), channel_id=1, source_target_pairs={{0,1},{1,0},{2,3},{3,2},{4,5},{5,4},{6,7},{7,6},{8,9},{9,8},{10,11... | collective-permute-start | bytes 1572872 | tf_op jit(solution)/shard_map/ppermute | solution.py:118
  132.8 9.0 %collective-permute-start.31 = (bf16[2,256,256]{2,1,0:T(8,128)(2,1)S(1)}, bf16[2,256,256]{2,1,0:T(8,128)(2,1)S(1)}, u32[]{:S(2)}, u32[]{:S(2)}) collective-permute-start(bf16[2,256,256]{2,1,0:T(8,128)(2,1)S(1)} %slice.24), channel_id=1, source_target_pairs={{0,4},{1,5},{4,8},{5,9},{8,12},{9,13},{12,14},{13,15},{14,10},{15,... | collective-permute-start | bytes 786440 | tf_op jit(solution)/shard_map/ppermute | solution.py:128
  134.6 29.6 %collective-permute-start.37 = (bf16[2,512,256]{2,1,0:T(8,128)(2,1)S(1)}, bf16[2,512,256]{2,1,0:T(8,128)(2,1)S(1)}, u32[]{:S(2)}, u32[]{:S(2)}) collective-permute-start(bf16[2,512,256]{2,1,0:T(8,128)(2,1)S(1)} %collective-permute-done.30.refs_0_), channel_id=1, source_target_pairs={{0,1},{1,0},{2,3},{3,2},{4,5},{5,4},{6,7},{7,6},{8,9},{9,8},{10,11... | collective-permute-start | bytes 1572872 | tf_op jit(solution)/shard_map/ppermute | solution.py:118
  134.9 29.4 %collective-permute-start.38 = (bf16[2,512,256]{2,1,0:T(8,128)(2,1)S(1)}, bf16[2,512,256]{2,1,0:T(8,128)(2,1)S(1)}, u32[]{:S(2)}, u32[]{:S(2)}) collective-permute-start(bf16[2,512,256]{2,1,0:T(8,128)(2,1)S(1)} %collective-permute-done.34.refs_2_), channel_id=1, source_target_pairs={{0,1},{1,0},{2,3},{3,2},{4,5},{5,4},{6,7},{7,6},{8,9},{9,8},{10,11... | collective-permute-start | bytes 1572872 | tf_op jit(solution)/shard_map/ppermute | solution.py:118
  141.8 26.7 %collective-permute-start.32 = (bf16[2,256,256]{2,1,0:T(8,128)(2,1)S(1)}, bf16[2,256,256]{2,1,0:T(8,128)(2,1)S(1)}, u32[]{:S(2)}, u32[]{:S(2)}) collective-permute-start(bf16[2,256,256]{2,1,0:T(8,128)(2,1)S(1)} %collective-permute-done.31.refs_0_), channel_id=1, source_target_pairs={{0,1},{1,0},{2,3},{3,2},{4,5},{5,4},{6,7},{7,6},{8,9},{9,8},{10,11... | collective-permute-start | bytes 786440 | tf_op jit(solution)/shard_map/ppermute | solution.py:118
  143.6 24.9 %collective-permute-start.36 = (bf16[2,256,256]{2,1,0:T(8,128)(2,1)S(1)}, bf16[2,256,256]{2,1,0:T(8,128)(2,1)S(1)}, u32[]{:S(2)}, u32[]{:S(2)}) collective-permute-start(bf16[2,256,256]{2,1,0:T(8,128)(2,1)S(1)} %collective-permute-done.35.refs_2_), channel_id=1, source_target_pairs={{0,1},{1,0},{2,3},{3,2},{4,5},{5,4},{6,7},{7,6},{8,9},{9,8},{10,11... | collective-permute-start | bytes 786440 | tf_op jit(solution)/shard_map/ppermute | solution.py:118
  (39 other events, 209.3 us)

commit v2 on v1

v2 whole, which is shorter than its diff:
```python
import functools

import jax
import jax.numpy as jnp
import numpy as np
from jax import lax
from jax.experimental import pallas as pl
from jax.experimental.pallas import tpu as pltpu
from jax.sharding import PartitionSpec as P

forget_factor = 0.9
code_span = 240.0
code_middle = 120.0
scale_rows = 16
ln2 = 0.6931471805599453
in_vmem = pl.BlockSpec(memory_space=pltpu.VMEM)
anywhere = pl.BlockSpec(memory_space=pl.ANY)
in_hbm = pl.BlockSpec(memory_space=pltpu.HBM)
in_smem = pl.BlockSpec(memory_space=pltpu.SMEM)
params = pltpu.CompilerParams(vmem_limit_bytes=16 * 2**20)

inner = (((1,), (0,)), ((), ()))
lead = (((0,), (0,)), ((), ()))
trail = (((1,), (1,)), ((), ()))


def dot(a, b, dims):
    return lax.dot_general(a, b, dims, preferred_element_type=jnp.float32)


def split(x):
    high = x.astype(jnp.bfloat16)
    return high, (x - high.astype(jnp.float32)).astype(jnp.bfloat16)


def dot3(a, b, dims):
    a_high, a_low = split(a)
    b_high, b_low = split(b)
    return dot(a_high, b_high, dims) + (dot(a_high, b_low, dims) + dot(a_low, b_high, dims))


def dot2(a, b, dims):
    b_high, b_low = split(b)
    return dot(a, b_high, dims) + dot(a, b_low, dims)


def gate(values, events=()):
    count = len(values)

    def kernel(*refs):
        pass

    return list(
        pl.pallas_call(
            kernel,
            out_shape=tuple(jax.ShapeDtypeStruct(v.shape, v.dtype) for v in values),
            in_specs=[anywhere] * (count + len(events)),
            out_specs=(anywhere,) * count,
            input_output_aliases={i: i for i in range(count)},
            compiler_params=params,
            name="gate",
        )(*values, *events)
    )


def ring_order(devices):
    chips = devices // 2
    return list(range(0, chips, 2)) + list(range(chips - 1, 0, -2))


def ring_pairs(devices, way):
    order = ring_order(devices)
    chips = len(order)
    pairs = []
    for at in range(chips):
        for core in range(2):
            pairs.append((2 * order[at] + core, 2 * order[(at + way) % chips] + core))
    return pairs


def partner_pairs(devices, mask):
    return [(i, i ^ mask) for i in range(devices)]


def ring_table(devices, rows):
    order = ring_order(devices)
    chips = len(order)
    table = []
    for me in range(devices):
        at, core = order.index(me // 2), me % 2
        line = [me * rows, (me ^ 1) * rows]
        for step in range(1, chips // 2):
            for there in (at - step, at + step):
                chip = order[there % chips]
                line += [(2 * chip + core) * rows, (2 * chip + 1 - core) * rows]
        chip = order[(at + chips // 2) % chips]
        line += [(2 * chip + core) * rows, (2 * chip + 1 - core) * rows]
        line += [core, (me // 2) % 2]
        table.append(line)
    return np.array(table, np.int32)


class Ring:
    def __init__(self, line, bits, block, devices):
        self.line, self.bits = line, bits
        self.forth, self.back = ring_pairs(devices, 1), ring_pairs(devices, -1)
        self.apart = [p for p in self.forth if p[0] % 2 == 0] + [
            p for p in self.back if p[0] % 2 == 1
        ]
        self.swap = partner_pairs(devices, 1)
        self.steps = devices // 4
        self.done = 0
        self.recent = [block]
        self.groups = []
        self.new_recent = self.new_swapped = False

    def pass_on(self, copies=None):
        group = []
        for block, copy in zip(self.recent, copies or self.recent):
            group += [block, lax.ppermute(copy, "row", self.swap)]
        self.groups.append(group)
        self.new_swapped = True

    def step(self):
        self.done += 1
        self.new_recent = True
        ahead, behind = self.recent[0], self.recent[-1]
        self.full = self.recent
        if self.done == self.steps:
            block = ahead
            if len(self.recent) == 2:
                block = choose(self.line, self.bits[0], ahead, behind)
            self.recent = [lax.ppermute(block, "row", self.apart)]
        else:
            self.recent = [
                lax.ppermute(ahead, "row", self.forth),
                lax.ppermute(behind, "row", self.back),
            ]

    def held(self):
        return (self.recent if self.new_recent else []) + (
            self.groups[-1][1::2] if self.new_swapped else []
        )

    def hold(self, values):
        values = list(values)
        if self.new_recent:
            old, count = self.recent, len(self.recent)
            self.recent, values = values[:count], values[count:]
            for group in self.groups:
                for at, block in enumerate(group):
                    for before, now in zip(old, self.recent):
                        if block is before:
                            group[at] = now
        if self.new_swapped:
            self.groups[-1][1::2] = values
        self.new_recent = self.new_swapped = False


def small_kernel(kernel, out_shape, args, name):
    multiple = isinstance(out_shape, tuple)
    return pl.pallas_call(
        kernel,
        out_shape=out_shape,
        in_specs=[in_smem] + [in_vmem] * (len(args) - 1),
        out_specs=tuple(in_vmem for _ in out_shape) if multiple else in_vmem,
        compiler_params=params,
        name=name,
    )(*args)


def f32(*shape):
    return jax.ShapeDtypeStruct(shape, jnp.float32)


def choose(line, bit, first, second):
    def kernel(line_ref, first_ref, second_ref, out_ref):
        @pl.when(line_ref[0, bit] == 0)
        def _():
            out_ref[...] = first_ref[...]

        @pl.when(line_ref[0, bit] == 1)
        def _():
            out_ref[...] = second_ref[...]

    shape = jax.ShapeDtypeStruct(first.shape, first.dtype)
    return small_kernel(kernel, shape, (line, first, second), "choose")


def store_halves(line_ref, bit, value_ref, mine_ref, theirs_ref):
    half = mine_ref.shape[0]
    side = line_ref[0, bit]
    mine_ref[...] = value_ref[pl.ds(pl.multiple_of(side * half, 8), half), :]
    theirs_ref[...] = value_ref[pl.ds(pl.multiple_of((1 - side) * half, 8), half), :]


def add_two(line, a, b):
    def kernel(line_ref, a_ref, b_ref, out_ref):
        out_ref[...] = a_ref[...] + b_ref[...]

    return small_kernel(kernel, f32(*a.shape), (line, a, b), "add_two")


def add_and_halve(line, bit, a, b):
    half = f32(a.shape[0] // 2, a.shape[1])

    def kernel(line_ref, a_ref, b_ref, mine_ref, theirs_ref):
        size = mine_ref.shape[0]
        side = line_ref[0, bit]
        for out_ref, which in ((mine_ref, side), (theirs_ref, 1 - side)):
            rows = pl.ds(pl.multiple_of(which * size, 8), size)
            out_ref[...] = a_ref[rows, :] + b_ref[rows, :]

    return small_kernel(kernel, (half, half), (line, a, b), "add_and_halve")


def join_halves(line, bit, mine, theirs):
    def kernel(line_ref, mine_ref, theirs_ref, out_ref):
        size = mine_ref.shape[0]
        side = line_ref[0, bit]
        out_ref[pl.ds(pl.multiple_of(side * size, 8), size), :] = mine_ref[...]
        out_ref[pl.ds(pl.multiple_of((1 - side) * size, 8), size), :] = theirs_ref[...]

    shape = f32(2 * mine.shape[0], mine.shape[1])
    return small_kernel(kernel, shape, (line, mine, theirs), "join_halves")


class Total:
    def __init__(self, line, bits, mine, theirs, devices, halve_chips):
        self.line, self.bits, self.devices = line, bits, devices
        self.mine, self.theirs = mine, theirs
        first = 4 if halve_chips else 2
        self.rounds = ["core"] + ["halve"] * halve_chips
        while first < devices:
            self.rounds.append(first)
            first *= 2
        self.rounds += ["join"] * halve_chips + ["last"]

    def pass_on(self, value, mask):
        return lax.ppermute(value, "row", partner_pairs(self.devices, mask))

    def round(self, count=1):
        for _ in range(count):
            if not self.rounds:
                return
            kind = self.rounds.pop(0)
            line, (core_bit, chip_bit) = self.line, self.bits
            if kind == "core":
                got = self.pass_on(self.theirs, 1)
                if self.rounds[0] == "halve":
                    self.mine, self.theirs = add_and_halve(line, chip_bit, self.mine, got)
                else:
                    self.mine, self.theirs = add_two(line, self.mine, got), None
            elif kind == "halve":
                self.mine = add_two(line, self.mine, self.pass_on(self.theirs, 2))
                self.theirs = None
            elif kind == "join":
                self.mine = join_halves(line, chip_bit, self.mine, self.pass_on(self.mine, 2))
            elif kind == "last":
                self.mine = join_halves(line, core_bit, self.mine, self.pass_on(self.mine, 1))
            else:
                self.mine = add_two(line, self.mine, self.pass_on(self.mine, kind))

    def held(self):
        return [self.mine] if self.theirs is None else [self.mine, self.theirs]

    def hold(self, values):
        self.mine = values[0]
        if self.theirs is not None:
            self.theirs = values[1]


def gate_all(parts, extra=(), events=()):
    lists = [p.held() for p in parts]
    flat = [v for values in lists for v in values] + list(extra)
    flat = gate(flat, events)
    at = 0
    for p, values in zip(parts, lists):
        p.hold(flat[at : at + len(values)])
        at += len(values)
    return flat[at:]


def encode(values):
    size = jnp.abs(values)
    most = jnp.max(size, axis=0, keepdims=True)
    level = size / jnp.maximum(most, 1e-37)
    power = jnp.exp((level * code_span - code_middle) * ln2)
    return jnp.where(values < 0.0, -power, power).astype(jnp.bfloat16), most


def decode(code, most):
    code = code.astype(jnp.float32)
    level = (jnp.log(jnp.abs(code)) * (1.0 / ln2) + code_middle) * (1.0 / code_span)
    return jnp.where(code < 0.0, -level, level) * most


def write_rows(rows):
    at = lax.broadcasted_iota(jnp.int32, (scale_rows, rows[0].shape[1]), 0)
    block = jnp.zeros(at.shape, jnp.float32)
    for i, row in enumerate(rows):
        high = row.astype(jnp.bfloat16).astype(jnp.float32)
        block = jnp.where(at == 2 * i, high, block)
        block = jnp.where(at == 2 * i + 1, row - high, block)
    return block.astype(jnp.bfloat16)


def read_row(block, i):
    block = block.astype(jnp.float32)
    return block[2 * i : 2 * i + 1] + block[2 * i + 1 : 2 * i + 2]


def pack(line, values, mine, got, extra):
    rows, rank = values.shape
    sum_rows = mine.shape[0]
    size = rows + scale_rows + sum_rows
    more = [] if extra is None else [extra]

    def kernel(line_ref, values_ref, mine_ref, got_ref, *refs):
        out_ref = refs[-1]
        code, most = encode(values_ref[...])
        sum_code, sum_most = encode(mine_ref[...] + got_ref[...])
        scales = [most, sum_most] + ([refs[0][:1, :]] if more else [])
        out_ref[:rows, :] = code
        out_ref[rows : rows + scale_rows, :] = write_rows(scales)
        out_ref[rows + scale_rows :, :] = sum_code

    return small_kernel(
        kernel,
        jax.ShapeDtypeStruct((size, rank), jnp.bfloat16),
        (line, values, mine, got, *more),
        "pack",
    )


def turn(line, snapshots, basis):
    windows, rows, count = snapshots.shape

    def kernel(line_ref, snap_ref, basis_ref, out_ref, snap_copy_ref, basis_copy_ref):
        for w in range(windows):
            out_ref[w] = snap_ref[w].T
        snap_copy_ref[...] = snap_ref[...]
        basis_copy_ref[...] = basis_ref[...]

    shapes = (
        jax.ShapeDtypeStruct((windows, count, rows), snapshots.dtype),
        jax.ShapeDtypeStruct(snapshots.shape, snapshots.dtype),
        f32(*basis.shape),
    )
    return small_kernel(kernel, shapes, (line, snapshots, basis), "turn")


def first_sums(line, bits, snapshots, basis, share):
    _, _, count = snapshots.shape
    rank = basis.shape[1]
    half = f32(count // 2, rank)

    def kernel(line_ref, snap_ref, basis_ref, share_ref, mine_ref, theirs_ref, part):
        part[...] = dot2(snap_ref[0], basis_ref[...], lead)
        store_halves(line_ref, bits[0], part, mine_ref, theirs_ref)

    return pl.pallas_call(
        kernel,
        out_shape=(half, half),
        in_specs=[in_smem, in_vmem, in_vmem, in_vmem],
        out_specs=(in_vmem, in_vmem),
        scratch_shapes=[pltpu.VMEM((count, rank), jnp.float32)],
        compiler_params=params,
        name="first_sums",
    )(line, snapshots, basis, share)


def local_trace(line, prior_cov, snapshots):
    windows, rows, count = snapshots.shape

    def total(x):
        return jnp.sum(jnp.sum(x, axis=0, keepdims=True), axis=1, keepdims=True)

    def kernel(line_ref, cov_ref, snap_ref, out_ref):
        row_at = lax.broadcasted_iota(jnp.int32, (128, 128), 0)
        col_at = lax.broadcasted_iota(jnp.int32, (128, 128), 1)
        diagonal = jnp.zeros((128, 128), jnp.float32)
        for at in range(0, rows, 128):
            first = pl.multiple_of(line_ref[0, 0] + at, 128)
            corner = cov_ref[at : at + 128, pl.ds(first, 128)]
            diagonal = diagonal + jnp.where(row_at == col_at, corner, 0.0)
        prior = total(diagonal)
        trace = prior
        for w in range(windows):
            snap = snap_ref[w].astype(jnp.float32)
            trace = forget_factor * trace + total(snap * snap) * (1.0 / count)
        at = lax.broadcasted_iota(jnp.int32, out_ref.shape, 0)
        out_ref[...] = jnp.where(at == 0, trace, prior * (1.0 / rows))

    return small_kernel(kernel, f32(8, 128), (line, prior_cov, snapshots), "local_trace")


def add_products(line_ref, base, cov_ref, block_refs, state, mean):
    running, own, other = state[:3]
    rows, rank = running.shape
    for at, block_ref in enumerate(block_refs):
        first = pl.multiple_of(line_ref[0, base + at], 128)
        scales = block_ref[rows : rows + scale_rows, :]
        block = decode(block_ref[:rows, :], read_row(scales, 0))
        piece = decode(block_ref[rows + scale_rows :, :], read_row(scales, 1))
        if at % 2 == 0:
            own = own + piece
        else:
            other = other + piece
        high, low = split(block)
        if mean is not None:
            gram, trace = state[3:]
            both = jnp.concatenate([high, low], axis=1)
            square = dot(high, both, lead)
            gram = gram + (square[:, :rank] + (square[:, rank:] + dot(low, high, lead)))
            trace = trace + read_row(scales, 2)
            state = (running, own, other, gram, trace)
            high, low = split(block * (1.0 / mean))
        both = jnp.concatenate([high, low], axis=1)
        cov_high, cov_low = split(cov_ref[:, pl.ds(first, rows)])
        wide = dot(cov_high, both, inner)
        running = running + (wide[:, :rank] + (wide[:, rank:] + dot(cov_low, high, inner)))
    return (running, own, other) + tuple(state[3:])


def state_shapes(rows, rank, sum_rows, last):
    shapes = [f32(n, rank) for n in (rows, sum_rows, sum_rows)]
    return shapes + ([f32(rank, rank), f32(1, rank)] if last else [])


def product_part(line, base, prior_cov, blocks, state, sum_rows, share, carried):
    count = len(blocks)
    last = share is not None
    shapes = state_shapes(prior_cov.shape[0], blocks[0].shape[1], sum_rows, last)
    outs = len(shapes)
    shapes += [jax.ShapeDtypeStruct(v.shape, v.dtype) for v in carried]
    more = ([share] if last else []) + list(state or [])

    def kernel(line_ref, cov_ref, *refs):
        block_refs, refs = refs[:count], refs[count:]
        carried_refs, refs = refs[: len(carried)], refs[len(carried) :]
        given, out_refs = refs[: -len(shapes)], refs[-len(shapes) :]
        for carried_ref, out_ref in zip(carried_refs, out_refs[outs:]):
            out_ref[...] = carried_ref[...]
        mean = None
        if last:
            mean, given = given[0][1:2, :1], given[1:]
        old = [r[...] for r in given] or [jnp.zeros(v.shape, jnp.float32) for v in shapes[:outs]]
        new = add_products(line_ref, base, cov_ref, block_refs, tuple(old), mean)
        for out_ref, value in zip(out_refs[:outs], new):
            out_ref[...] = value

    results = small_kernel(
        kernel, tuple(shapes), (line, prior_cov, *blocks, *carried, *more), "product_part"
    )
    return list(results[:outs]), list(results[outs:])


def product_end(line, bits, base, prior_cov, blocks, state, snapshots, window, share):
    rows, order = prior_cov.shape
    rank = blocks[0].shape[1]
    windows, _, snap_count = snapshots.shape
    count = len(blocks)
    last = share is not None
    sum_rows = state[1].shape[0]
    inv_snap = 1.0 / snap_count
    parts = len(state)
    more = [share] if last else []
    shapes = (f32(rows, rank),)
    if last:
        shapes += (f32(rank // 2, rank), f32(rank // 2, rank), f32(rank, rank))

    def kernel(line_ref, cov_ref, *refs):
        block_refs, refs = refs[:count], refs[count:]
        old = tuple(r[...] for r in refs[:parts])
        snap_ref, refs = refs[parts], refs[parts + 1 :]
        mean = None
        if last:
            mean, refs = refs[0][1:2, :1], refs[1:]
        outs, sums_buf, gram_buf = refs[: len(shapes)], refs[-2], refs[-1]
        new = add_products(line_ref, base, cov_ref, block_refs, old, mean)
        side = line_ref[0, bits[0]]
        sums_buf[pl.ds(pl.multiple_of(side * sum_rows, 8), sum_rows), :] = new[1]
        sums_buf[pl.ds(pl.multiple_of((1 - side) * sum_rows, 8), sum_rows), :] = new[2]
        applied = new[0] * forget_factor ** (window + 1)
        scale = 1.0
        if last:
            scale = float(order) / new[4]
            applied = applied * (scale * mean)
        for w in range(window + 1):
            at = w * snap_count
            total = sums_buf[at : at + snap_count, :] * scale
            weight = forget_factor ** (window - w) * inv_snap
            applied = applied + weight * dot2(snap_ref[w], total, inner)
        outs[0][...] = applied
        if last:
            gram_buf[...] = lax.dot_general(
                applied,
                applied,
                lead,
                precision=lax.Precision.HIGHEST,
                preferred_element_type=jnp.float32,
            )
            store_halves(line_ref, bits[0], gram_buf, outs[1], outs[2])
            outs[3][...] = new[3]

    return pl.pallas_call(
        kernel,
        out_shape=shapes,
        in_specs=[in_smem] + [in_vmem] * (2 + count + parts + len(more)),
        out_specs=tuple(in_vmem for _ in shapes),
        scratch_shapes=[
            pltpu.VMEM((2 * sum_rows, rank), jnp.float32),
            pltpu.VMEM((rank, rank), jnp.float32),
        ],
        compiler_params=params,
        name="product_end",
    )(line, prior_cov, *blocks, *state, snapshots, *more)


def window_sums(line, bits, applied, snapshots):
    windows, _, snap_count = snapshots.shape
    rank = applied.shape[1]
    total = windows * snap_count
    half = f32(total // 2, rank)

    def kernel(line_ref, applied_ref, snap_ref, mine_ref, theirs_ref, part):
        for w in range(windows):
            at = w * snap_count
            part[at : at + snap_count, :] = dot2(snap_ref[w], applied_ref[...], lead)
        store_halves(line_ref, bits[0], part, mine_ref, theirs_ref)

    return pl.pallas_call(
        kernel,
        out_shape=(half, half),
        in_specs=[in_smem] + [in_vmem] * 2,
        out_specs=(in_vmem, in_vmem),
        scratch_shapes=[pltpu.VMEM((total, rank), jnp.float32)],
        compiler_params=params,
        name="window_sums",
    )(line, applied, snapshots)


panel = 8


def inverse_factor(gram):
    rank = gram.shape[0]
    eye = lax.broadcasted_iota(jnp.int32, (rank, rank), 0) == lax.broadcasted_iota(
        jnp.int32, (rank, rank), 1
    )
    diagonal = jnp.where(eye, gram, 0.0)
    down = lax.rsqrt(jnp.sum(diagonal, axis=1, keepdims=True))
    along = lax.rsqrt(jnp.sum(diagonal, axis=0, keepdims=True))
    gram = gram * down * along
    start = jnp.where(eye, along, 0.0)
    count = rank // panel
    rows = [gram[i * panel : (i + 1) * panel] for i in range(count)]
    sides = [start[i * panel : (i + 1) * panel] for i in range(count)]
    sub = lax.broadcasted_iota(jnp.int32, (panel, rank), 0)
    finished = []
    for top in range(count):
        first = top * panel
        spread = {
            i: [
                jnp.broadcast_to(rows[i][:, first + k : first + k + 1], (panel, rank))
                for k in range(panel)
            ]
            for i in range(top, count)
        }
        done = jnp.zeros((panel, rank), jnp.float32)
        for j in range(0, panel, 2):
            row0, row1 = rows[top][j : j + 1], rows[top][j + 1 : j + 2]
            side0, side1 = sides[top][j : j + 1], sides[top][j + 1 : j + 2]
            lead_columns = spread[top]
            a = lead_columns[j][j : j + 1]
            b = lead_columns[j][j + 1 : j + 2]
            c = lead_columns[j + 1][j + 1 : j + 2]
            over = 1.0 / (a * c - b * b)
            a_over, b_over, c_over = a * over, b * over, c * over
            root = lax.rsqrt(a)
            ratio = b * root * root
            done = jnp.where(sub == j, side0 * root, done)
            done = jnp.where(
                sub == j + 1, (side1 - ratio * side0) * lax.rsqrt(c - ratio * b), done
            )
            heads = [
                (lead_columns[m][j : j + 1], lead_columns[m][j + 1 : j + 2]) for m in range(panel)
            ]
            for i in range(top, count):
                x0, x1 = spread[i][j], spread[i][j + 1]
                m0 = x0 * c_over - x1 * b_over
                m1 = x1 * a_over - x0 * b_over
                rows[i] = rows[i] - (m0 * row0 + m1 * row1)
                sides[i] = sides[i] - (m0 * side0 + m1 * side1)
                for m in range(j + 2, panel):
                    head0, head1 = heads[m]
                    spread[i][m] = spread[i][m] - (m0 * head0 + m1 * head1)
        finished.append(done)
    return jnp.concatenate(finished, axis=0)


def factor(line, gram):
    def kernel(line_ref, gram_ref, out_ref):
        out_ref[...] = inverse_factor(gram_ref[...])

    return small_kernel(kernel, f32(*gram.shape), (line, gram), "factor")


def finish(line, bits, gram, theirs, first, applied):
    rank = applied.shape[1]
    half = rank // 2

    def kernel(line_ref, gram_ref, theirs_ref, first_ref, applied_ref, out_ref, buf):
        side = line_ref[0, bits[0]]
        buf[pl.ds(pl.multiple_of(side * half, 8), half), :] = gram_ref[...]
        buf[pl.ds(pl.multiple_of((1 - side) * half, 8), half), :] = theirs_ref[...]
        first = first_ref[...]

        def exact(a, b, dims):
            return lax.dot_general(
                a,
                b,
                dims,
                precision=lax.Precision.HIGHEST,
                preferred_element_type=jnp.float32,
            )

        second_gram = exact(exact(first, buf[...], inner), first, trail)
        second = inverse_factor(second_gram)
        out_ref[...] = dot3(applied_ref[...], exact(second, first, inner), trail)

    return pl.pallas_call(
        kernel,
        out_shape=f32(*applied.shape),
        in_specs=[in_smem] + [in_vmem] * 4,
        out_specs=in_vmem,
        scratch_shapes=[pltpu.VMEM((rank, rank), jnp.float32)],
        compiler_params=params,
        name="finish",
    )(line, gram, theirs, first, applied)


def covariance_part(line, numbers, prior_cov, snapshots, blocks, filled):
    rows, _ = prior_cov.shape
    windows, _, snap_count = snapshots.shape
    count = len(blocks)
    more = [] if filled is None else [filled]
    inv_snap = 1.0 / snap_count

    def kernel(line_ref, cov_ref, snap_ref, *refs):
        block_refs, refs = refs[:count], refs[count + len(more) :]
        out_ref, out_bufs, sems = refs[0], refs[1:-1], refs[-1]
        copies = []
        for at in range(count):
            width = block_refs[at].shape[2]
            first = pl.multiple_of(line_ref[0, numbers[at]], 128)
            columns = pl.ds(first, width)
            total = cov_ref[:, columns] * forget_factor**windows
            for w in range(windows):
                weight = forget_factor ** (windows - 1 - w) * inv_snap
                total = total + weight * dot(snap_ref[w], block_refs[at][w], inner)
            out_bufs[at][...] = total
            copy = pltpu.make_async_copy(out_bufs[at], out_ref.at[:, columns], sems.at[at])
            copy.start()
            copies.append(copy)
        for copy in copies:
            copy.wait()

    return pl.pallas_call(
        kernel,
        out_shape=f32(*prior_cov.shape),
        in_specs=[in_smem] + [in_vmem] * (2 + count) + [in_hbm] * len(more),
        out_specs=in_hbm,
        scratch_shapes=[pltpu.VMEM((rows, b.shape[2]), jnp.float32) for b in blocks]
        + [pltpu.SemaphoreType.DMA((count,))],
        input_output_aliases={3 + count: 0} if more else {},
        compiler_params=params,
        name="covariance_part",
    )(line, prior_cov, snapshots, *blocks, *more)


def local(devices, prior_cov, snapshots, prior_basis):
    rows = prior_cov.shape[0]
    rank = prior_basis.shape[1]
    windows, _, snap_count = snapshots.shape
    table = ring_table(devices, rows)
    me = lax.axis_index("row")
    line = lax.dynamic_slice_in_dim(jnp.asarray(table), me, 1, axis=0)
    entries = table.shape[1]
    bits = (entries - 2, entries - 1)
    steps = devices // 4
    starts = [0] + [2 + 4 * at for at in range(steps)]
    swap = partner_pairs(devices, 1)

    def fill(filled, numbers):
        blocks = [b for group in snap_ring.groups for b in group]
        chosen = [blocks[n] for n in numbers]
        return covariance_part(line, numbers, prior_cov, snapshots, chosen, filled)

    turned, snapshots, values = turn(line, snapshots, prior_basis)
    snap_ring = Ring(line, bits, turned, devices)
    snap_ring.pass_on()
    snap_ring.step()
    next_share = local_trace(line, prior_cov, snapshots)
    mine, theirs = first_sums(line, bits, snapshots, values, next_share)
    share = new_cov = None
    for window in range(windows):
        got = lax.ppermute(theirs, "row", swap)
        if window == 1:
            (values, new_cov) = gate_all([snap_ring], [values, new_cov])
        ring = Ring(line, bits, pack(line, values, mine, got, share), devices)
        sum_rows = mine.shape[0]
        state = None
        for phase in range(1, steps + 1):
            sent = ring.recent
            ring.step()
            arrived, ring.recent = ring.recent, sent
            extra, waiting = [], [ring]
            if phase == 1:
                ring.pass_on()
                if window == 0:
                    waiting.append(snap_ring)
                else:
                    snap_ring.recent = gate(snap_ring.recent, [sent[0]])
                    snap_ring.pass_on()
                    waiting.append(snap_ring)
                    new_cov = fill(new_cov, [6, 8])
                    extra.append(new_cov)
            else:
                state, _ = product_part(
                    line,
                    starts[phase - 2],
                    prior_cov,
                    ring.groups[phase - 2],
                    state,
                    sum_rows,
                    share,
                    [],
                )
                ring.pass_on()
                arrived = gate(arrived, [state[0]])
                extra += state
                if window == 0 and phase == steps - 1:
                    snap_ring.new_recent = True
                    waiting.append(snap_ring)
                if phase == steps:
                    if window == 0:
                        snap_ring.pass_on()
                    snap_ring.new_recent = True
                    waiting.append(snap_ring)
            ring.recent = arrived
            extra = gate_all(waiting, extra)
            if window == 1 and phase == 1:
                new_cov = extra.pop()
            state = extra or None
        snap_ring.step()
        state, _ = product_part(
            line,
            starts[steps - 1],
            prior_cov,
            ring.groups[steps - 1],
            state,
            sum_rows,
            share,
            [],
        )
        ring.pass_on()
        result = product_end(
            line,
            bits,
            starts[steps],
            prior_cov,
            ring.groups[steps],
            state,
            snapshots,
            window,
            share,
        )
        if window == 0:
            (values,) = result
            share = next_share
            mine, theirs = window_sums(line, bits, values, snapshots)
            new_cov = fill(None, range(6))
    applied, mine, theirs, first_gram = result
    total = Total(line, bits, mine, theirs, devices, False)
    total.rounds.pop()
    total.round()
    first = factor(line, first_gram)
    while snap_ring.done < steps - 1:
        (first,) = gate_all([total, snap_ring], [first])
        snap_ring.pass_on()
        snap_ring.step()
    (first, new_cov) = gate_all([total, snap_ring], [first, new_cov])

    end = 4 * steps
    snap_ring.step()
    arrived, snap_ring.recent = snap_ring.recent, snap_ring.full
    snap_ring.pass_on()
    snap_ring.recent = arrived
    total.round()
    new_cov = fill(new_cov, [7, 9] + list(range(10, end - 6)))
    new_cov = fill(new_cov, [end - 6, end - 4])
    (first, new_cov) = gate_all([total, snap_ring], [first, new_cov])
    snap_ring.pass_on()
    total.round()
    new_cov = fill(new_cov, [end - 5, end - 3])
    (first, new_cov) = gate_all([total, snap_ring], [first, new_cov])
    while total.rounds:
        total.round()
    new_cov = fill(new_cov, [end - 2, end - 1])
    (first, new_cov) = gate_all([total], [first, new_cov])
    theirs = lax.ppermute(total.mine, "row", swap)
    new_basis = finish(line, bits, total.mine, theirs, first, applied)
    return (new_cov, new_basis)


def solution(mesh):
    return jax.shard_map(
        functools.partial(local, mesh.shape["row"]),
        mesh=mesh,
        in_specs=(
            P(("band", "row"), None),
            P(None, ("band", "row"), None),
            P(("band", "row"), None),
        ),
        out_specs=(P(("band", "row"), None), P(("band", "row"), None)),
        check_vma=False,
    )
```

time: 172 us -> 133 us (0.77)
  waiting for transfers between devices: 61.1 us -> 31.8 us
  Pallas kernels: 64 us -> 59.1 us
  starting transfers between devices: 34.4 us -> 32.4 us
  local copies, waits for them, and re-layouts: 10.4 us -> 8.46 us
    ppermute x51 -> x45, waiting for transfers between devices: 54.2 us -> 23.7 us  [the longest x9 13 us: step(): lax.ppermute(behind, 'row', self.back)]
    pallas_call x1, Pallas kernels: 10.8 us -> 6.41 us  [finish(): pl.pallas_call(kernel, out_shape=f32(*applied.shape), in_specs=[in_smem]...]
    pallas_call x4 -> x6, Pallas kernels: 16.5 us -> 18.9 us  [covariance_part(): pl.pallas_call(kernel, out_shape=f32(*prior_cov.shape), in_specs=[in_smem...]
    pallas_call x18 -> x20, Pallas kernels: 30 us -> 27.9 us  [small_kernel(): pl.pallas_call(kernel, out_shape=out_shape, in_specs=[in_smem] + [in_vmem...]
    ppermute x51 -> x45, starting transfers between devices: 31.6 us -> 29.6 us  [the longest x9 11.5 us: step(): lax.ppermute(ahead, 'row', self.forth)]
    unnamed x11 -> x8, local copies, waits for them, and re-layouts: 9.59 us -> 7.76 us
  transfers between devices with their start and end apart: 58 -> 52, of which waited for: 20 -> 21; matrix products, arithmetic and copies ran while one was open for 0% -> 0% of each run, Pallas kernels for 33% -> 37%
where the time goes in v2:
time: 133 us
  Pallas kernels  59.1 us (44%)
  starting transfers between devices  32.4 us (24%)
  waiting for transfers between devices  31.8 us (24%)
  local copies, waits for them, and re-layouts  8.46 us (6%)
    pallas_call x20, Pallas kernels, small_kernel(): pl.pallas_call(kernel, out_shape=out_shape, in_specs=[in_smem] + [in_vmem...  27.9 us
    pallas_call x6, Pallas kernels, covariance_part(): pl.pallas_call(kernel, out_shape=f32(*prior_cov.shape), in_specs=[in_smem...  18.9 us
    ppermute x9, waiting for transfers between devices, step(): lax.ppermute(behind, 'row', self.back)  13 us
    ppermute x9, starting transfers between devices, step(): lax.ppermute(ahead, 'row', self.forth)  11.5 us
    ppermute x9, starting transfers between devices, step(): lax.ppermute(behind, 'row', self.back)  8.85 us
    unnamed x8, local copies, waits for them, and re-layouts  7.76 us
    ppermute x9, waiting for transfers between devices, step(): lax.ppermute(ahead, 'row', self.forth)  7.22 us
    pallas_call x1, Pallas kernels, finish(): pl.pallas_call(kernel, out_shape=f32(*applied.shape), in_specs=[in_smem]...  6.41 us
  transfers between devices with their start and end apart: 52, of which 21 were waited for; matrix products, arithmetic and copies ran while one was open for 0% of the time, Pallas kernels for 37%

profile of v2, /device:TPU:0, one launch (start us, length us, event | category | flops | bytes accessed | tf_op | source)
XLA Modules:
  0.0 132.9 jit_solution(1980256454851092482)
XLA Ops:
  4.6 2.6 %collective-permute-start.5 = (bf16[2,256,512]{2,1,0:T(8,128)(2,1)S(1)}, bf16[2,256,512]{2,1,0:T(8,128)(2,1)S(1)}, u32[]{:S(2)}, u32[]{:S(2)}) collective-permute-start(bf16[2,256,512]{2,1,0:T(8,128)(2,1)S(1)} %get-tuple-element.147.refs_0_), channel_id=1, source_target_pairs={{0,2},{1,3},{4,0},{5,1},{8,4},{9,5},{12,8},{13,9},{14,12},{15,13},... | collective-permute-start | bytes 1572872 | tf_op jit(solution)/shard_map/ppermute | solution.py:137
  7.3 5.8 %copy-done = f32[512,8192]{1,0:T(8,128)S(1)} copy-done((f32[512,8192]{1,0:T(8,128)S(1)}, f32[512,8192]{1,0:T(8,128)}, u32[]{:S(2)}) %copy-start) | copy-done | bytes 16777240
  16.9 1.9 %collective-permute-start.2 = (bf16[656,128]{1,0:T(8,128)(2,1)S(1)}, bf16[656,128]{1,0:T(8,128)(2,1)S(1)}, u32[]{:S(2)}, u32[]{:S(2)}) collective-permute-start(bf16[656,128]{1,0:T(8,128)(2,1)S(1)} %pack.2.refs_0_), channel_id=1, source_target_pairs={{0,2},{1,3},{4,0},{5,1},{8,4},{9,5},{12,8},{13,9},{14,12},{15,13},... | collective-permute-start | bytes 503816 | tf_op jit(solution)/shard_map/ppermute | solution.py:137
  20.1 3.6 %collective-permute-done.2.refs_1_ = bf16[656,128]{1,0:T(8,128)(2,1)S(1)} collective-permute-done((bf16[656,128]{1,0:T(8,128)(2,1)S(1)}, bf16[656,128]{1,0:T(8,128)(2,1)S(1)}, u32[]{:S(2)}, u32[]{:S(2)}) %collective-permute-start.2) | collective-permute-done | bytes 167968 | tf_op jit(solution)/shard_map/ppermute | solution.py:137
  34.5 1.9 %product_part.9 = (f32[512,128]{1,0:T(8,128)S(1)}, f32[128,128]{1,0:T(8,128)S(1)}, f32[128,128]{1,0:T(8,128)S(1)}) custom-call(s32[1,18]{1,0:T(1,128)S(1)} %constant_dynamic-slice_fusion.line_ref, f32[512,8192]{1,0:T(8,128)S(1)} %copy-done.1, bf16[656,128]{1,0:T(8,128)(2,1)S(1)} %get-tuple-element.148.refs_0_, ...), custom_call_target="tpu_custom_call" | custom-call | tf_op jit(solution)/shard_map/product_part/pallas_call | solution.py:162
  42.2 1.9 %product_part.10 = (f32[512,128]{1,0:T(8,128)S(1)}, f32[128,128]{1,0:T(8,128)S(1)}, f32[128,128]{1,0:T(8,128)S(1)}) custom-call(s32[1,18]{1,0:T(1,128)S(1)} %constant_dynamic-slice_fusion.line_ref, f32[512,8192]{1,0:T(8,128)S(1)} %copy-done.1, bf16[656,128]{1,0:T(8,128)(2,1)S(1)} %get-tuple-element.156.refs_0_, ...), custom_call_target="tpu_custom_call" | custom-call | tf_op jit(solution)/shard_map/product_part/pallas_call | solution.py:162
  47.6 1.9 %product_part.11 = (f32[512,128]{1,0:T(8,128)S(1)}, f32[128,128]{1,0:T(8,128)S(1)}, f32[128,128]{1,0:T(8,128)S(1)}) custom-call(s32[1,18]{1,0:T(1,128)S(1)} %constant_dynamic-slice_fusion.line_ref, f32[512,8192]{1,0:T(8,128)S(1)} %copy-done.1, bf16[656,128]{1,0:T(8,128)(2,1)S(1)} %get-tuple-element.170.first_ref.refs_0_, ...), custom_call_target="tpu_custom_call" | custom-call | tf_op jit(solution)/shard_map/product_part/pallas_call | solution.py:162
  52.8 5.6 %covariance_part.6.refs_3_ = f32[512,8192]{1,0:T(8,128)} custom-call(s32[1,18]{1,0:T(1,128)S(1)} %constant_dynamic-slice_fusion.line_ref, f32[512,8192]{1,0:T(8,128)S(1)} %copy-done.1, bf16[2,512,256]{2,1,0:T(8,128)(2,1)S(1)} %get-tuple-element.144.snap_ref.refs_5_.refs_7_, bf16[2,256,512]{2,1,0:T(8,128)(2,1)S(1)} %get-tuple-element.147.refs_0_, ...), custom_call_target="tpu_custom_call" | custom-call | tf_op jit(solution)/shard_map/covariance_part/pallas_call | solution.py:670
  63.3 2.7 %covariance_part.7.refs_5_ = f32[512,8192]{1,0:T(8,128)} custom-call(s32[1,18]{1,0:T(1,128)S(1)} %constant_dynamic-slice_fusion.line_ref, f32[512,8192]{1,0:T(8,128)S(1)} %copy-done.1, bf16[2,512,256]{2,1,0:T(8,128)(2,1)S(1)} %get-tuple-element.144.snap_ref.refs_5_.refs_7_, ...), custom_call_target="tpu_custom_call", output_to_operand_aliasing={{}: (5, {})} | custom-call | tf_op jit(solution)/shard_map/covariance_part/pallas_call | solution.py:670
  66.0 2.6 %collective-permute-done.25.refs_1_ = bf16[784,128]{1,0:T(8,128)(2,1)S(1)} collective-permute-done((bf16[784,128]{1,0:T(8,128)(2,1)S(1)}, bf16[784,128]{1,0:T(8,128)(2,1)S(1)}, u32[]{:S(2)}, u32[]{:S(2)}) %collective-permute-start.25) | collective-permute-done | bytes 200736 | tf_op jit(solution)/shard_map/ppermute | solution.py:137
  73.1 2.2 %collective-permute-done.29.refs_0_ = bf16[784,128]{1,0:T(8,128)(2,1)S(1)} collective-permute-done((bf16[784,128]{1,0:T(8,128)(2,1)S(1)}, bf16[784,128]{1,0:T(8,128)(2,1)S(1)}, u32[]{:S(2)}, u32[]{:S(2)}) %collective-permute-start.29) | collective-permute-done | bytes 200736 | tf_op jit(solution)/shard_map/ppermute | solution.py:136
  79.1 2.5 %product_part.13 = (f32[512,128]{1,0:T(8,128)S(1)}, f32[256,128]{1,0:T(8,128)S(1)}, f32[256,128]{1,0:T(8,128)S(1)}, f32[128,128]{1,0:T(8,128)S(1)}, f32[1,128]{1,0:T(1,128)S(1)}) custom-call(s32[1,18]{1,0:T(1,128)S(1)} %constant_dynamic-slice_fusion.line_ref, f32[512,8192]{1,0:T(8,128)S(1)} %copy-done.1, bf16[784,128]{1,0:T(8,128)(2,1)S(1)} %get-tuple-element.204.refs_0_, ...), custom_call_target="tpu_custom_call" | custom-call | tf_op jit(solution)/shard_map/product_part/pallas_call | solution.py:162
  85.8 2.5 %product_part.14 = (f32[512,128]{1,0:T(8,128)S(1)}, f32[256,128]{1,0:T(8,128)S(1)}, f32[256,128]{1,0:T(8,128)S(1)}, f32[128,128]{1,0:T(8,128)S(1)}, f32[1,128]{1,0:T(1,128)S(1)}) custom-call(s32[1,18]{1,0:T(1,128)S(1)} %constant_dynamic-slice_fusion.line_ref, f32[512,8192]{1,0:T(8,128)S(1)} %copy-done.1, bf16[784,128]{1,0:T(8,128)(2,1)S(1)} %get-tuple-element.214.refs_0_, ...), custom_call_target="tpu_custom_call" | custom-call | tf_op jit(solution)/shard_map/product_part/pallas_call | solution.py:162
  88.3 2.0 %collective-permute-done.37.refs_0_ = bf16[784,128]{1,0:T(8,128)(2,1)S(1)} collective-permute-done((bf16[784,128]{1,0:T(8,128)(2,1)S(1)}, bf16[784,128]{1,0:T(8,128)(2,1)S(1)}, u32[]{:S(2)}, u32[]{:S(2)}) %collective-permute-start.37) | collective-permute-done | bytes 200736 | tf_op jit(solution)/shard_map/ppermute | solution.py:133
  92.4 2.5 %product_part.15 = (f32[512,128]{1,0:T(8,128)S(1)}, f32[256,128]{1,0:T(8,128)S(1)}, f32[256,128]{1,0:T(8,128)S(1)}, f32[128,128]{1,0:T(8,128)S(1)}, f32[1,128]{1,0:T(1,128)S(1)}) custom-call(s32[1,18]{1,0:T(1,128)S(1)} %constant_dynamic-slice_fusion.line_ref, f32[512,8192]{1,0:T(8,128)S(1)} %copy-done.1, ...), custom_call_target="tpu_custom_call" | custom-call | tf_op jit(solution)/shard_map/product_part/pallas_call | solution.py:162
  94.9 2.3 %product_end.3 = (f32[512,128]{1,0:T(8,128)S(1)}, f32[64,128]{1,0:T(8,128)S(1)}, f32[64,128]{1,0:T(8,128)S(1)}, f32[128,128]{1,0:T(8,128)S(1)}) custom-call(s32[1,18]{1,0:T(1,128)S(1)} %constant_dynamic-slice_fusion.line_ref, f32[512,8192]{1,0:T(8,128)S(1)} %copy-done.1, bf16[784,128]{1,0:T(8,128)(2,1)S(1)} %get-tuple-element.244.refs_0_, ...), custom_call_target="tpu_custom_call" | custom-call | tf_op jit(solution)/shard_map/product_end/pallas_call | solution.py:507
  97.8 5.0 %factor.1.refs_3_ = f32[128,128]{1,0:T(8,128)S(1)} custom-call(s32[1,18]{1,0:T(1,128)S(1)} %constant_dynamic-slice_fusion.line_ref, f32[128,128]{1,0:T(8,128)S(1)} %get-tuple-element.261.gram_ref), custom_call_target="tpu_custom_call" | custom-call | tf_op jit(solution)/shard_map/factor/pallas_call | solution.py:162
  106.8 2.7 %covariance_part.8.refs_2_ = f32[512,8192]{1,0:T(8,128)} custom-call(s32[1,18]{1,0:T(1,128)S(1)} %constant_dynamic-slice_fusion.line_ref, f32[512,8192]{1,0:T(8,128)S(1)} %copy-done.1, bf16[2,512,256]{2,1,0:T(8,128)(2,1)S(1)} %get-tuple-element.144.snap_ref.refs_5_.refs_7_, ...), custom_call_target="tpu_custom_call", output_to_operand_aliasing={{}: (5, {})} | custom-call | tf_op jit(solution)/shard_map/covariance_part/pallas_call | solution.py:670
  109.5 2.7 %covariance_part.9.refs_5_ = f32[512,8192]{1,0:T(8,128)} custom-call(s32[1,18]{1,0:T(1,128)S(1)} %constant_dynamic-slice_fusion.line_ref, f32[512,8192]{1,0:T(8,128)S(1)} %copy-done.1, bf16[2,512,256]{2,1,0:T(8,128)(2,1)S(1)} %get-tuple-element.144.snap_ref.refs_5_.refs_7_, ...), custom_call_target="tpu_custom_call", output_to_operand_aliasing={{}: (5, {})} | custom-call | tf_op jit(solution)/shard_map/covariance_part/pallas_call | solution.py:670
  112.2 2.0 %collective-permute-done.44.b_ref = f32[64,128]{1,0:T(8,128)S(1)} collective-permute-done((f32[64,128]{1,0:T(8,128)S(1)}, f32[64,128]{1,0:T(8,128)S(1)}, u32[]{:S(2)}, u32[]{:S(2)}) %collective-permute-start.44) | collective-permute-done | bytes 32800 | tf_op jit(solution)/shard_map/ppermute | solution.py:240
  114.9 2.6 %covariance_part.10.refs_3_ = f32[512,8192]{1,0:T(8,128)} custom-call(s32[1,18]{1,0:T(1,128)S(1)} %constant_dynamic-slice_fusion.line_ref, f32[512,8192]{1,0:T(8,128)S(1)} %copy-done.1, bf16[2,512,256]{2,1,0:T(8,128)(2,1)S(1)} %get-tuple-element.144.snap_ref.refs_5_.refs_7_, ...), custom_call_target="tpu_custom_call", output_to_operand_aliasing={{}: (5, {})} | custom-call | tf_op jit(solution)/shard_map/covariance_part/pallas_call | solution.py:670
  119.5 2.6 %covariance_part.11.refs_2_ = f32[512,8192]{1,0:T(8,128)} custom-call(s32[1,18]{1,0:T(1,128)S(1)} %constant_dynamic-slice_fusion.line_ref, f32[512,8192]{1,0:T(8,128)S(1)} %copy-done.1, bf16[2,512,256]{2,1,0:T(8,128)(2,1)S(1)} %get-tuple-element.144.snap_ref.refs_5_.refs_7_, ...), custom_call_target="tpu_custom_call", output_to_operand_aliasing={{}: (5, {})} | custom-call | tf_op jit(solution)/shard_map/covariance_part/pallas_call | solution.py:670
  122.1 2.5 %collective-permute-done.50.b_ref = f32[64,128]{1,0:T(8,128)S(1)} collective-permute-done((f32[64,128]{1,0:T(8,128)S(1)}, f32[64,128]{1,0:T(8,128)S(1)}, u32[]{:S(2)}, u32[]{:S(2)}) %collective-permute-start.50) | collective-permute-done | bytes 32800 | tf_op jit(solution)/shard_map/ppermute | solution.py:240
  126.5 6.4 %finish.1 = f32[512,128]{1,0:T(8,128)} custom-call(s32[1,18]{1,0:T(1,128)S(1)} %constant_dynamic-slice_fusion.line_ref, f32[64,128]{1,0:T(8,128)S(1)} %get-tuple-element.281.gram_ref, f32[64,128]{1,0:T(8,128)S(1)} %collective-permute-done.51.theirs_ref, f32[128,128]{1,0:T(8,128)S(1)} %get-tuple-element.282.first_ref, ...), custom_call_target="tpu_custom_call" | custom-call | tf_op jit(solution)/shard_map/finish/pallas_call | solution.py:633
  (140 shorter events, 60.8 us)
Async XLA Ops:
  4.1 21.0 %collective-permute-start.6 = (bf16[2,256,512]{2,1,0:T(8,128)(2,1)S(1)}, bf16[2,256,512]{2,1,0:T(8,128)(2,1)S(1)}, u32[]{:S(2)}, u32[]{:S(2)}) collective-permute-start(bf16[2,256,512]{2,1,0:T(8,128)(2,1)S(1)} %get-tuple-element.147.refs_0_), channel_id=1, source_target_pairs={{0,1},{1,0},{2,3},{3,2},{4,5},{5,4},{6,7},{7,6},{8,9},{9,8},{10,11... | collective-permute-start | bytes 1572872 | tf_op jit(solution)/shard_map/ppermute | solution.py:120
  4.6 20.5 %collective-permute-start.5 = (bf16[2,256,512]{2,1,0:T(8,128)(2,1)S(1)}, bf16[2,256,512]{2,1,0:T(8,128)(2,1)S(1)}, u32[]{:S(2)}, u32[]{:S(2)}) collective-permute-start(bf16[2,256,512]{2,1,0:T(8,128)(2,1)S(1)} %get-tuple-element.147.refs_0_), channel_id=1, source_target_pairs={{0,2},{1,3},{4,0},{5,1},{8,4},{9,5},{12,8},{13,9},{14,12},{15,13},... | collective-permute-start | bytes 1572872 | tf_op jit(solution)/shard_map/ppermute | solution.py:137
  7.2 17.9 %collective-permute-start.4 = (bf16[2,256,512]{2,1,0:T(8,128)(2,1)S(1)}, bf16[2,256,512]{2,1,0:T(8,128)(2,1)S(1)}, u32[]{:S(2)}, u32[]{:S(2)}) collective-permute-start(bf16[2,256,512]{2,1,0:T(8,128)(2,1)S(1)} %get-tuple-element.147.refs_0_), channel_id=1, source_target_pairs={{0,4},{1,5},{4,8},{5,9},{8,12},{9,13},{12,14},{13,15},{14,10},{15,... | collective-permute-start | bytes 1572872 | tf_op jit(solution)/shard_map/ppermute | solution.py:136
  16.9 6.7 %collective-permute-start.2 = (bf16[656,128]{1,0:T(8,128)(2,1)S(1)}, bf16[656,128]{1,0:T(8,128)(2,1)S(1)}, u32[]{:S(2)}, u32[]{:S(2)}) collective-permute-start(bf16[656,128]{1,0:T(8,128)(2,1)S(1)} %pack.2.refs_0_), channel_id=1, source_target_pairs={{0,2},{1,3},{4,0},{5,1},{8,4},{9,5},{12,8},{13,9},{14,12},{15,13},... | collective-permute-start | bytes 503816 | tf_op jit(solution)/shard_map/ppermute | solution.py:137
  18.8 6.3 %collective-permute-start.1 = (bf16[656,128]{1,0:T(8,128)(2,1)S(1)}, bf16[656,128]{1,0:T(8,128)(2,1)S(1)}, u32[]{:S(2)}, u32[]{:S(2)}) collective-permute-start(bf16[656,128]{1,0:T(8,128)(2,1)S(1)} %pack.2.refs_0_), channel_id=1, source_target_pairs={{0,4},{1,5},{4,8},{5,9},{8,12},{9,13},{12,14},{13,15},{14,10},{15,... | collective-permute-start | bytes 503816 | tf_op jit(solution)/shard_map/ppermute | solution.py:136
  38.9 6.6 %collective-permute-start.18 = (bf16[2,256,512]{2,1,0:T(8,128)(2,1)S(1)}, bf16[2,256,512]{2,1,0:T(8,128)(2,1)S(1)}, u32[]{:S(2)}, u32[]{:S(2)}) collective-permute-start(bf16[2,256,512]{2,1,0:T(8,128)(2,1)S(1)} %get-tuple-element.178.refs_3_), channel_id=1, source_target_pairs={{0,1},{1,0},{2,3},{3,2},{4,5},{5,4},{6,7},{7,6},{8,9},{9,8},{10,11... | collective-permute-start | bytes 1572872 | tf_op jit(solution)/shard_map/ppermute | solution.py:120
  39.0 6.5 %collective-permute-start.19 = (bf16[2,256,512]{2,1,0:T(8,128)(2,1)S(1)}, bf16[2,256,512]{2,1,0:T(8,128)(2,1)S(1)}, u32[]{:S(2)}, u32[]{:S(2)}) collective-permute-start(bf16[2,256,512]{2,1,0:T(8,128)(2,1)S(1)} %get-tuple-element.179.refs_4_), channel_id=1, source_target_pairs={{0,1},{1,0},{2,3},{3,2},{4,5},{5,4},{6,7},{7,6},{8,9},{9,8},{10,11... | collective-permute-start | bytes 1572872 | tf_op jit(solution)/shard_map/ppermute | solution.py:120
  45.5 13.1 %collective-permute-start.20 = (bf16[2,256,512]{2,1,0:T(8,128)(2,1)S(1)}, bf16[2,256,512]{2,1,0:T(8,128)(2,1)S(1)}, u32[]{:S(2)}, u32[]{:S(2)}) collective-permute-start(bf16[2,256,512]{2,1,0:T(8,128)(2,1)S(1)} %get-tuple-element.182.refs_2_), channel_id=1, source_target_pairs={{0,4},{1,5},{4,8},{5,9},{8,12},{9,13},{12,14},{13,15},{14,10},{15,... | collective-permute-start | bytes 1572872 | tf_op jit(solution)/shard_map/ppermute | solution.py:136
  47.1 12.8 %collective-permute-start.21 = (bf16[2,256,512]{2,1,0:T(8,128)(2,1)S(1)}, bf16[2,256,512]{2,1,0:T(8,128)(2,1)S(1)}, u32[]{:S(2)}, u32[]{:S(2)}) collective-permute-start(bf16[2,256,512]{2,1,0:T(8,128)(2,1)S(1)} %get-tuple-element.183.refs_4_), channel_id=1, source_target_pairs={{0,2},{1,3},{4,0},{5,1},{8,4},{9,5},{12,8},{13,9},{14,12},{15,13},... | collective-permute-start | bytes 1572872 | tf_op jit(solution)/shard_map/ppermute | solution.py:137
  52.2 7.7 %collective-permute-start.23 = (f32[256,128]{1,0:T(8,128)S(1)}, f32[256,128]{1,0:T(8,128)S(1)}, u32[]{:S(2)}, u32[]{:S(2)}) collective-permute-start(f32[256,128]{1,0:T(8,128)S(1)} %get-tuple-element.198), channel_id=1, source_target_pairs={{0,1},{1,0},{2,3},{3,2},{4,5},{5,4},{6,7},{7,6},{8,9},{9,8},{10,11... | collective-permute-start | bytes 393224 | tf_op jit(solution)/shard_map/ppermute | solution.py:709
  60.7 8.2 %collective-permute-start.27 = (bf16[2,256,512]{2,1,0:T(8,128)(2,1)S(1)}, bf16[2,256,512]{2,1,0:T(8,128)(2,1)S(1)}, u32[]{:S(2)}, u32[]{:S(2)}) collective-permute-start(bf16[2,256,512]{2,1,0:T(8,128)(2,1)S(1)} %get-tuple-element.201.refs_0_.refs_3_), channel_id=1, source_target_pairs={{0,1},{1,0},{2,3},{3,2},{4,5},{5,4},{6,7},{7,6},{8,9},{9,8},{10,11... | collective-permute-start | bytes 1572872 | tf_op jit(solution)/shard_map/ppermute | solution.py:120
  60.7 8.1 %collective-permute-start.28 = (bf16[2,256,512]{2,1,0:T(8,128)(2,1)S(1)}, bf16[2,256,512]{2,1,0:T(8,128)(2,1)S(1)}, u32[]{:S(2)}, u32[]{:S(2)}) collective-permute-start(bf16[2,256,512]{2,1,0:T(8,128)(2,1)S(1)} %get-tuple-element.202.refs_1_.refs_4_), channel_id=1, source_target_pairs={{0,1},{1,0},{2,3},{3,2},{4,5},{5,4},{6,7},{7,6},{8,9},{9,8},{10,11... | collective-permute-start | bytes 1572872 | tf_op jit(solution)/shard_map/ppermute | solution.py:120
  61.3 7.3 %collective-permute-start.25 = (bf16[784,128]{1,0:T(8,128)(2,1)S(1)}, bf16[784,128]{1,0:T(8,128)(2,1)S(1)}, u32[]{:S(2)}, u32[]{:S(2)}) collective-permute-start(bf16[784,128]{1,0:T(8,128)(2,1)S(1)} %pack.3.refs_2_.refs_0_), channel_id=1, source_target_pairs={{0,2},{1,3},{4,0},{5,1},{8,4},{9,5},{12,8},{13,9},{14,12},{15,13},... | collective-permute-start | bytes 602120 | tf_op jit(solution)/shard_map/ppermute | solution.py:137
  61.8 7.1 %collective-permute-start.24 = (bf16[784,128]{1,0:T(8,128)(2,1)S(1)}, bf16[784,128]{1,0:T(8,128)(2,1)S(1)}, u32[]{:S(2)}, u32[]{:S(2)}) collective-permute-start(bf16[784,128]{1,0:T(8,128)(2,1)S(1)} %pack.3.refs_2_.refs_0_), channel_id=1, source_target_pairs={{0,4},{1,5},{4,8},{5,9},{8,12},{9,13},{12,14},{13,15},{14,10},{15,... | collective-permute-start | bytes 602120 | tf_op jit(solution)/shard_map/ppermute | solution.py:136
  68.8 6.5 %collective-permute-start.29 = (bf16[784,128]{1,0:T(8,128)(2,1)S(1)}, bf16[784,128]{1,0:T(8,128)(2,1)S(1)}, u32[]{:S(2)}, u32[]{:S(2)}) collective-permute-start(bf16[784,128]{1,0:T(8,128)(2,1)S(1)} %get-tuple-element.204.refs_0_), channel_id=1, source_target_pairs={{0,4},{1,5},{4,8},{5,9},{8,12},{9,13},{12,14},{13,15},{14,10},{15,... | collective-permute-start | bytes 602120 | tf_op jit(solution)/shard_map/ppermute | solution.py:136
  70.5 6.1 %collective-permute-start.30 = (bf16[784,128]{1,0:T(8,128)(2,1)S(1)}, bf16[784,128]{1,0:T(8,128)(2,1)S(1)}, u32[]{:S(2)}, u32[]{:S(2)}) collective-permute-start(bf16[784,128]{1,0:T(8,128)(2,1)S(1)} %get-tuple-element.205.refs_2_), channel_id=1, source_target_pairs={{0,2},{1,3},{4,0},{5,1},{8,4},{9,5},{12,8},{13,9},{14,12},{15,13},... | collective-permute-start | bytes 602120 | tf_op jit(solution)/shard_map/ppermute | solution.py:137
  76.5 5.8 %collective-permute-start.33 = (bf16[784,128]{1,0:T(8,128)(2,1)S(1)}, bf16[784,128]{1,0:T(8,128)(2,1)S(1)}, u32[]{:S(2)}, u32[]{:S(2)}) collective-permute-start(bf16[784,128]{1,0:T(8,128)(2,1)S(1)} %get-tuple-element.214.refs_0_), channel_id=1, source_target_pairs={{0,4},{1,5},{4,8},{5,9},{8,12},{9,13},{12,14},{13,15},{14,10},{15,... | collective-permute-start | bytes 602120 | tf_op jit(solution)/shard_map/ppermute | solution.py:136
  84.3 6.0 %collective-permute-start.37 = (bf16[784,128]{1,0:T(8,128)(2,1)S(1)}, bf16[784,128]{1,0:T(8,128)(2,1)S(1)}, u32[]{:S(2)}, u32[]{:S(2)}) collective-permute-start(bf16[784,128]{1,0:T(8,128)(2,1)S(1)} %choose.4), channel_id=1, source_target_pairs={{0,4},{4,8},{8,12},{12,14},{14,10},{10,6},{6,2},{2,0},{1,3},{5,1},... | collective-permute-start | bytes 602120 | tf_op jit(solution)/shard_map/ppermute | solution.py:133
  90.3 13.0 %collective-permute-start.42 = (bf16[2,256,512]{2,1,0:T(8,128)(2,1)S(1)}, bf16[2,256,512]{2,1,0:T(8,128)(2,1)S(1)}, u32[]{:S(2)}, u32[]{:S(2)}) collective-permute-start(bf16[2,256,512]{2,1,0:T(8,128)(2,1)S(1)} %get-tuple-element.259), channel_id=1, source_target_pairs={{0,4},{1,5},{4,8},{5,9},{8,12},{9,13},{12,14},{13,15},{14,10},{15,... | collective-permute-start | bytes 1572872 | tf_op jit(solution)/shard_map/ppermute | solution.py:136
  91.1 12.3 %collective-permute-start.43 = (bf16[2,256,512]{2,1,0:T(8,128)(2,1)S(1)}, bf16[2,256,512]{2,1,0:T(8,128)(2,1)S(1)}, u32[]{:S(2)}, u32[]{:S(2)}) collective-permute-start(bf16[2,256,512]{2,1,0:T(8,128)(2,1)S(1)} %get-tuple-element.260), channel_id=1, source_target_pairs={{0,2},{1,3},{4,0},{5,1},{8,4},{9,5},{12,8},{13,9},{14,12},{15,13},... | collective-permute-start | bytes 1572872 | tf_op jit(solution)/shard_map/ppermute | solution.py:137
  104.0 10.8 %collective-permute-start.45 = (bf16[2,256,512]{2,1,0:T(8,128)(2,1)S(1)}, bf16[2,256,512]{2,1,0:T(8,128)(2,1)S(1)}, u32[]{:S(2)}, u32[]{:S(2)}) collective-permute-start(bf16[2,256,512]{2,1,0:T(8,128)(2,1)S(1)} %choose.5), channel_id=1, source_target_pairs={{0,4},{4,8},{8,12},{12,14},{14,10},{10,6},{6,2},{2,0},{1,3},{5,1},... | collective-permute-start | bytes 1572872 | tf_op jit(solution)/shard_map/ppermute | solution.py:133
  105.0 9.7 %collective-permute-start.46 = (bf16[2,256,512]{2,1,0:T(8,128)(2,1)S(1)}, bf16[2,256,512]{2,1,0:T(8,128)(2,1)S(1)}, u32[]{:S(2)}, u32[]{:S(2)}) collective-permute-start(bf16[2,256,512]{2,1,0:T(8,128)(2,1)S(1)} %get-tuple-element.264.first_ref.refs_0_), channel_id=1, source_target_pairs={{0,1},{1,0},{2,3},{3,2},{4,5},{5,4},{6,7},{7,6},{8,9},{9,8},{10,11... | collective-permute-start | bytes 1572872 | tf_op jit(solution)/shard_map/ppermute | solution.py:120
  105.0 9.8 %collective-permute-start.47 = (bf16[2,256,512]{2,1,0:T(8,128)(2,1)S(1)}, bf16[2,256,512]{2,1,0:T(8,128)(2,1)S(1)}, u32[]{:S(2)}, u32[]{:S(2)}) collective-permute-start(bf16[2,256,512]{2,1,0:T(8,128)(2,1)S(1)} %get-tuple-element.265.second_ref.refs_1_), channel_id=1, source_target_pairs={{0,1},{1,0},{2,3},{3,2},{4,5},{5,4},{6,7},{7,6},{8,9},{9,8},{10,11... | collective-permute-start | bytes 1572872 | tf_op jit(solution)/shard_map/ppermute | solution.py:120
  105.5 8.7 %collective-permute-start.44 = (f32[64,128]{1,0:T(8,128)S(1)}, f32[64,128]{1,0:T(8,128)S(1)}, u32[]{:S(2)}, u32[]{:S(2)}) collective-permute-start(f32[64,128]{1,0:T(8,128)S(1)} %get-tuple-element.263.a_ref), channel_id=1, source_target_pairs={{0,2},{1,3},{2,0},{3,1},{4,6},{5,7},{6,4},{7,5},{8,10},{9,11},{10,... | collective-permute-start | bytes 98312 | tf_op jit(solution)/shard_map/ppermute | solution.py:240
  (32 other events, 146.7 us)

commit v3 on v2

--- a/solution.py
+++ b/solution.py
@@ -110,6 +110,7 @@
         self.swap = partner_pairs(devices, 1)
         self.steps = devices // 4
         self.done = 0
+        self.chosen = None
         self.recent = [block]
         self.groups = []
         self.new_recent = self.new_swapped = False
@@ -121,14 +122,19 @@
         self.groups.append(group)
         self.new_swapped = True
 
+    def pass_on_full(self, copies=None):
+        arrived, self.recent = self.recent, self.full
+        self.pass_on(copies)
+        self.recent = arrived
+
     def step(self):
         self.done += 1
         self.new_recent = True
         ahead, behind = self.recent[0], self.recent[-1]
         self.full = self.recent
         if self.done == self.steps:
-            block = ahead
-            if len(self.recent) == 2:
+            block = ahead if self.chosen is None else self.chosen
+            if self.chosen is None and len(self.recent) == 2:
                 block = choose(self.line, self.bits[0], ahead, behind)
             self.recent = [lax.ppermute(block, "row", self.apart)]
         else:
@@ -194,11 +200,14 @@
     theirs_ref[...] = value_ref[pl.ds(pl.multiple_of((1 - side) * half, 8), half), :]
 
 
-def add_two(line, a, b):
-    def kernel(line_ref, a_ref, b_ref, out_ref):
-        out_ref[...] = a_ref[...] + b_ref[...]
-
-    return small_kernel(kernel, f32(*a.shape), (line, a, b), "add_two")
+def add_all(line, values):
+    def kernel(line_ref, *refs):
+        total = refs[0][...]
+        for ref in refs[1:-1]:
+            total = total + ref[...]
+        refs[-1][...] = total
+
+    return small_kernel(kernel, f32(*values[0].shape), (line, *values), "add_all")
 
 
 def add_and_halve(line, bit, a, b):
@@ -250,16 +259,16 @@
                 if self.rounds[0] == "halve":
                     self.mine, self.theirs = add_and_halve(line, chip_bit, self.mine, got)
                 else:
-                    self.mine, self.theirs = add_two(line, self.mine, got), None
+                    self.mine, self.theirs = add_all(line, [self.mine, got]), None
             elif kind == "halve":
-                self.mine = add_two(line, self.mine, self.pass_on(self.theirs, 2))
+                self.mine = add_all(line, [self.mine, self.pass_on(self.theirs, 2)])
                 self.theirs = None
             elif kind == "join":
                 self.mine = join_halves(line, chip_bit, self.mine, self.pass_on(self.mine, 2))
             elif kind == "last":
                 self.mine = join_halves(line, core_bit, self.mine, self.pass_on(self.mine, 1))
             else:
-                self.mine = add_two(line, self.mine, self.pass_on(self.mine, kind))
+                self.mine = add_all(line, [self.mine, self.pass_on(self.mine, kind)])
 
     def held(self):
         return [self.mine] if self.theirs is None else [self.mine, self.theirs]
@@ -333,50 +342,43 @@
     )
 
 
-def turn(line, snapshots, basis):
-    windows, rows, count = snapshots.shape
-
-    def kernel(line_ref, snap_ref, basis_ref, out_ref, snap_copy_ref, basis_copy_ref):
-        for w in range(windows):
-            out_ref[w] = snap_ref[w].T
-        snap_copy_ref[...] = snap_ref[...]
-        basis_copy_ref[...] = basis_ref[...]
-
-    shapes = (
-        jax.ShapeDtypeStruct((windows, count, rows), snapshots.dtype),
-        jax.ShapeDtypeStruct(snapshots.shape, snapshots.dtype),
-        f32(*basis.shape),
-    )
-    return small_kernel(kernel, shapes, (line, snapshots, basis), "turn")
-
-
-def first_sums(line, bits, snapshots, basis, share):
+def first_sums(line, bits, snapshots, basis):
     _, _, count = snapshots.shape
     rank = basis.shape[1]
     half = f32(count // 2, rank)
 
-    def kernel(line_ref, snap_ref, basis_ref, share_ref, mine_ref, theirs_ref, part):
+    def kernel(
+        line_ref, snap_ref, basis_ref, mine_ref, theirs_ref, snap_copy_ref, basis_copy_ref, part
+    ):
         part[...] = dot2(snap_ref[0], basis_ref[...], lead)
         store_halves(line_ref, bits[0], part, mine_ref, theirs_ref)
+        snap_copy_ref[...] = snap_ref[...]
+        basis_copy_ref[...] = basis_ref[...]
 
     return pl.pallas_call(
         kernel,
-        out_shape=(half, half),
-        in_specs=[in_smem, in_vmem, in_vmem, in_vmem],
-        out_specs=(in_vmem, in_vmem),
+        out_shape=(
+            half,
+            half,
+            jax.ShapeDtypeStruct(snapshots.shape, snapshots.dtype),
+            f32(*basis.shape),
+        ),
+        in_specs=[in_smem, in_vmem, in_vmem],
+        out_specs=(in_vmem,) * 4,
         scratch_shapes=[pltpu.VMEM((count, rank), jnp.float32)],
         compiler_params=params,
         name="first_sums",
-    )(line, snapshots, basis, share)
-
-
-def local_trace(line, prior_cov, snapshots):
+    )(line, snapshots, basis)
+
+
+def local_trace(line, prior_cov, snapshots, event):
     windows, rows, count = snapshots.shape
 
     def total(x):
         return jnp.sum(jnp.sum(x, axis=0, keepdims=True), axis=1, keepdims=True)
 
-    def kernel(line_ref, cov_ref, snap_ref, out_ref):
+    def kernel(line_ref, cov_ref, snap_ref, event_ref, out_ref, copy_ref):
+        copy_ref[...] = snap_ref[...]
         row_at = lax.broadcasted_iota(jnp.int32, (128, 128), 0)
         col_at = lax.broadcasted_iota(jnp.int32, (128, 128), 1)
         diagonal = jnp.zeros((128, 128), jnp.float32)
@@ -392,7 +394,8 @@
         at = lax.broadcasted_iota(jnp.int32, out_ref.shape, 0)
         out_ref[...] = jnp.where(at == 0, trace, prior * (1.0 / rows))
 
-    return small_kernel(kernel, f32(8, 128), (line, prior_cov, snapshots), "local_trace")
+    shapes = (f32(8, 128), jax.ShapeDtypeStruct(snapshots.shape, snapshots.dtype))
+    return small_kernel(kernel, shapes, (line, prior_cov, snapshots, event), "local_trace")
 
 
 def add_products(line_ref, base, cov_ref, block_refs, state, mean):
@@ -544,6 +547,12 @@
 panel = 8
 
 
+def reciprocal(x):
+    guess = pl.reciprocal(x, approx=True)
+    guess = guess * (2.0 - x * guess)
+    return guess * (2.0 - x * guess)
+
+
 def inverse_factor(gram):
     rank = gram.shape[0]
     eye = lax.broadcasted_iota(jnp.int32, (rank, rank), 0) == lax.broadcasted_iota(
@@ -576,7 +585,7 @@
             a = lead_columns[j][j : j + 1]
             b = lead_columns[j][j + 1 : j + 2]
             c = lead_columns[j + 1][j + 1 : j + 2]
-            over = 1.0 / (a * c - b * b)
+            over = reciprocal(a * c - b * b)
             a_over, b_over, c_over = a * over, b * over, c * over
             root = lax.rsqrt(a)
             ratio = b * root * root
@@ -607,59 +616,64 @@
     return small_kernel(kernel, f32(*gram.shape), (line, gram), "factor")
 
 
-def finish(line, bits, gram, theirs, first, applied):
-    rank = applied.shape[1]
+def both_factors(line, bits, gram, theirs, first):
+    rank = gram.shape[1]
     half = rank // 2
 
-    def kernel(line_ref, gram_ref, theirs_ref, first_ref, applied_ref, out_ref, buf):
+    def exact(a, b, dims):
+        return lax.dot_general(
+            a, b, dims, precision=lax.Precision.HIGHEST, preferred_element_type=jnp.float32
+        )
+
+    def kernel(line_ref, gram_ref, theirs_ref, first_ref, out_ref, buf):
         side = line_ref[0, bits[0]]
         buf[pl.ds(pl.multiple_of(side * half, 8), half), :] = gram_ref[...]
         buf[pl.ds(pl.multiple_of((1 - side) * half, 8), half), :] = theirs_ref[...]
         first = first_ref[...]
-
-        def exact(a, b, dims):
-            return lax.dot_general(
-                a,
-                b,
-                dims,
-                precision=lax.Precision.HIGHEST,
-                preferred_element_type=jnp.float32,
-            )
-
         second_gram = exact(exact(first, buf[...], inner), first, trail)
-        second = inverse_factor(second_gram)
-        out_ref[...] = dot3(applied_ref[...], exact(second, first, inner), trail)
+        out_ref[...] = exact(inverse_factor(second_gram), first, inner)
 
     return pl.pallas_call(
         kernel,
-        out_shape=f32(*applied.shape),
-        in_specs=[in_smem] + [in_vmem] * 4,
+        out_shape=f32(rank, rank),
+        in_specs=[in_smem] + [in_vmem] * 3,
         out_specs=in_vmem,
         scratch_shapes=[pltpu.VMEM((rank, rank), jnp.float32)],
         compiler_params=params,
-        name="finish",
-    )(line, gram, theirs, first, applied)
-
-
-def covariance_part(line, numbers, prior_cov, snapshots, blocks, filled):
+        name="both_factors",
+    )(line, gram, theirs, first)
+
+
+def finish(line, factors, applied):
+    def kernel(line_ref, factors_ref, applied_ref, out_ref):
+        out_ref[...] = dot3(applied_ref[...], factors_ref[...], trail)
+
+    return small_kernel(kernel, f32(*applied.shape), (line, factors, applied), "finish")
+
+
+def covariance_part(line, numbers, prior_cov, snapshots, blocks, filled, carry=False):
     rows, _ = prior_cov.shape
     windows, _, snap_count = snapshots.shape
     count = len(blocks)
     more = [] if filled is None else [filled]
+    copied = count if carry else 0
     inv_snap = 1.0 / snap_count
 
     def kernel(line_ref, cov_ref, snap_ref, *refs):
         block_refs, refs = refs[:count], refs[count + len(more) :]
-        out_ref, out_bufs, sems = refs[0], refs[1:-1], refs[-1]
+        out_ref, copy_refs, refs = refs[0], refs[1 : 1 + copied], refs[1 + copied :]
+        out_bufs, sems = refs[:-1], refs[-1]
+        for block_ref, copy_ref in zip(block_refs, copy_refs):
+            copy_ref[...] = block_ref[...]
         copies = []
         for at in range(count):
-            width = block_refs[at].shape[2]
+            width = block_refs[at].shape[1]
             first = pl.multiple_of(line_ref[0, numbers[at]], 128)
             columns = pl.ds(first, width)
             total = cov_ref[:, columns] * forget_factor**windows
             for w in range(windows):
                 weight = forget_factor ** (windows - 1 - w) * inv_snap
-                total = total + weight * dot(snap_ref[w], block_refs[at][w], inner)
+                total = total + weight * dot(snap_ref[w], block_refs[at][w], trail)
             out_bufs[at][...] = total
             copy = pltpu.make_async_copy(out_bufs[at], out_ref.at[:, columns], sems.at[at])
             copy.start()
@@ -667,17 +681,19 @@
         for copy in copies:
             copy.wait()
 
-    return pl.pallas_call(
+    result = pl.pallas_call(
         kernel,
-        out_shape=f32(*prior_cov.shape),
+        out_shape=(f32(*prior_cov.shape),)
+        + tuple(jax.ShapeDtypeStruct(b.shape, b.dtype) for b in blocks[:copied]),
         in_specs=[in_smem] + [in_vmem] * (2 + count) + [in_hbm] * len(more),
-        out_specs=in_hbm,
-        scratch_shapes=[pltpu.VMEM((rows, b.shape[2]), jnp.float32) for b in blocks]
+        out_specs=(in_hbm,) + (in_vmem,) * copied,
+        scratch_shapes=[pltpu.VMEM((rows, b.shape[1]), jnp.float32) for b in blocks]
         + [pltpu.SemaphoreType.DMA((count,))],
         input_output_aliases={3 + count: 0} if more else {},
         compiler_params=params,
         name="covariance_part",
     )(line, prior_cov, snapshots, *blocks, *more)
+    return (result[0], list(result[1:])) if carry else result[0]
 
 
 def local(devices, prior_cov, snapshots, prior_basis):
@@ -698,35 +714,42 @@
         chosen = [blocks[n] for n in numbers]
         return covariance_part(line, numbers, prior_cov, snapshots, chosen, filled)
 
-    turned, snapshots, values = turn(line, snapshots, prior_basis)
-    snap_ring = Ring(line, bits, turned, devices)
-    snap_ring.pass_on()
+    def fill_own(filled, blocks, numbers):
+        return covariance_part(line, numbers, prior_cov, snapshots, blocks, filled, True)
+
+    end = 4 * steps
+    snap_ring = Ring(line, bits, snapshots, devices)
     snap_ring.step()
-    next_share = local_trace(line, prior_cov, snapshots)
-    mine, theirs = first_sums(line, bits, snapshots, values, next_share)
+    mine, theirs, snapshots, values = first_sums(line, bits, snapshots, prior_basis)
     share = new_cov = None
     for window in range(windows):
         got = lax.ppermute(theirs, "row", swap)
         if window == 1:
-            (values, new_cov) = gate_all([snap_ring], [values, new_cov])
+            (values,) = gate_all([snap_ring], [values])
         ring = Ring(line, bits, pack(line, values, mine, got, share), devices)
         sum_rows = mine.shape[0]
         state = None
         for phase in range(1, steps + 1):
+            if phase == steps:
+                chosen = choose(line, bits[0], *ring.recent)
+                ring.chosen, *state = gate([chosen] + list(state))
+                ready = state[0]
             sent = ring.recent
             ring.step()
             arrived, ring.recent = ring.recent, sent
-            extra, waiting = [], [ring]
+            ring.pass_on()
+            extra, waiting, filled = [], [ring], []
             if phase == 1:
-                ring.pass_on()
+                waiting.append(snap_ring)
                 if window == 0:
-                    waiting.append(snap_ring)
+                    next_share, snap_copy = local_trace(line, prior_cov, snapshots, sent[0])
+                    arrived = gate(arrived, [next_share])
+                    extra = [snap_copy]
                 else:
                     snap_ring.recent = gate(snap_ring.recent, [sent[0]])
                     snap_ring.pass_on()
-                    waiting.append(snap_ring)
-                    new_cov = fill(new_cov, [6, 8])
-                    extra.append(new_cov)
+                    arrived = gate(arrived)
+                    filled = [6, 8]
             else:
                 state, _ = product_part(
                     line,
@@ -738,23 +761,45 @@
                     share,
                     [],
                 )
-                ring.pass_on()
                 arrived = gate(arrived, [state[0]])
                 extra += state
-                if window == 0 and phase == steps - 1:
-                    snap_ring.new_recent = True
+                if window == 0 and phase == 2:
+                    snap_ring.full = [snap_copy]
+                    snap_ring.pass_on_full()
+                    snap_ring.groups[0][0] = snapshots
                     waiting.append(snap_ring)
-                if phase == steps:
-                    if window == 0:
-                        snap_ring.pass_on()
-                    snap_ring.new_recent = True
-                    waiting.append(snap_ring)
+                if window == 0 and phase == 3:
+                    filled = [0, 1]
+                if window == 1 and phase == 2:
+                    filled = [7, 9]
+                if window == 1 and phase == 3:
+                    filled = [3, 5]
+            if filled:
+                new_cov = fill(new_cov, filled)
+                extra.append(new_cov)
             ring.recent = arrived
+            if phase == steps and window == 1:
+                snap_ring.new_recent = True
+                waiting.append(snap_ring)
+            if phase == steps and window == 0:
+                snap_ring.recent = gate(snap_ring.recent, [ready])
+                snap_ring.step()
+                if window == 0:
+                    new_cov, copies = fill_own(new_cov, snap_ring.full, [2, 4])
+                    extra += copies + [new_cov]
+                    filled = [2, 4]
             extra = gate_all(waiting, extra)
-            if window == 1 and phase == 1:
+            if window == 0 and phase == 1:
+                snap_copy = extra.pop()
+            if filled:
                 new_cov = extra.pop()
+            if window == 0 and phase == steps:
+                extra, copies = extra[:-2], extra[-2:]
             state = extra or None
-        snap_ring.step()
+        if window == 0:
+            snap_ring.pass_on_full(copies)
+        else:
+            snap_ring.step()
         state, _ = product_part(
             line,
             starts[steps - 1],
@@ -781,7 +826,6 @@
             (values,) = result
             share = next_share
             mine, theirs = window_sums(line, bits, values, snapshots)
-            new_cov = fill(None, range(6))
     applied, mine, theirs, first_gram = result
     total = Total(line, bits, mine, theirs, devices, False)
     total.rounds.pop()
@@ -793,13 +837,11 @@
         snap_ring.step()
     (first, new_cov) = gate_all([total, snap_ring], [first, new_cov])
 
-    end = 4 * steps
     snap_ring.step()
-    arrived, snap_ring.recent = snap_ring.recent, snap_ring.full
-    snap_ring.pass_on()
-    snap_ring.recent = arrived
+    snap_ring.pass_on_full()
     total.round()
-    new_cov = fill(new_cov, [7, 9] + list(range(10, end - 6)))
+    if end > 16:
+        new_cov = fill(new_cov, range(10, end - 6))
     new_cov = fill(new_cov, [end - 6, end - 4])
     (first, new_cov) = gate_all([total, snap_ring], [first, new_cov])
     snap_ring.pass_on()
@@ -811,7 +853,8 @@
     new_cov = fill(new_cov, [end - 2, end - 1])
     (first, new_cov) = gate_all([total], [first, new_cov])
     theirs = lax.ppermute(total.mine, "row", swap)
-    new_basis = finish(line, bits, total.mine, theirs, first, applied)
+    factors = both_factors(line, bits, total.mine, theirs, first)
+    new_basis = finish(line, factors, applied)
     return (new_cov, new_basis)
 
 

time: 133 us -> 128 us (0.962)
  waiting for transfers between devices: 31.8 us -> 23.8 us
  Pallas kernels: 59.1 us -> 61.3 us
    ppermute x9, waiting for transfers between devices: 13 us -> 5.88 us  [step(): lax.ppermute(behind, 'row', self.back)]
    ppermute x3, waiting for transfers between devices: 3.37 us -> 1.16 us  [step(): self.recent = [lax.ppermute(block, 'row', self.apart)]]
    ppermute x9, starting transfers between devices: 11.5 us -> 9.45 us  [step(): lax.ppermute(ahead, 'row', self.forth)]
    ppermute x3, starting transfers between devices: 3.62 us -> 5.19 us  [step(): self.recent = [lax.ppermute(block, 'row', self.apart)]]
    pallas_call x8 -> x10, Pallas kernels: 26.2 us -> 27.7 us  [the longest x8 21.4 us: covariance_part(): pl.pallas_call(kernel, out_shape=(f32(*prior_cov.shape),) + tuple((jax.Sh...]
    ppermute x4, waiting for transfers between devices: 5.76 us -> 7.22 us  [pass_on(): return lax.ppermute(value, 'row', partner_pairs(self.devices, mask))]
    ppermute x9, starting transfers between devices: 8.85 us -> 10.2 us  [step(): lax.ppermute(behind, 'row', self.back)]
  transfers between devices with their start and end apart: 52 -> 52, of which waited for: 21 -> 17; matrix products, arithmetic and copies ran while one was open for 0% -> 1% of each run, Pallas kernels for 37% -> 40%
where the time goes in v3:
time: 128 us; the launch traced here: 127 us
  Pallas kernels  61.3 us (48%)
  starting transfers between devices  32.6 us (25%)
  waiting for transfers between devices  23.8 us (19%)
  local copies, waits for them, and re-layouts  8.45 us (7%)
    pallas_call x20, Pallas kernels, small_kernel(): pl.pallas_call(kernel, out_shape=out_shape, in_specs=[in_smem] + [in_vmem...  28.6 us
    pallas_call x8, Pallas kernels, covariance_part(): pl.pallas_call(kernel, out_shape=(f32(*prior_cov.shape),) + tuple((jax.Sh...  21.4 us
    ppermute x9, starting transfers between devices, step(): lax.ppermute(behind, 'row', self.back)  10.2 us
    ppermute x9, starting transfers between devices, step(): lax.ppermute(ahead, 'row', self.forth)  9.45 us
    unnamed x8, local copies, waits for them, and re-layouts  7.76 us
    ppermute x4, waiting for transfers between devices, pass_on(): return lax.ppermute(value, 'row', partner_pairs(self.devices, mask))  7.22 us
    ppermute x9, waiting for transfers between devices, step(): lax.ppermute(ahead, 'row', self.forth)  6.68 us
    ppermute x9, waiting for transfers between devices, step(): lax.ppermute(behind, 'row', self.back)  5.88 us
  transfers between devices with their start and end apart: 52, of which 17 were waited for; matrix products, arithmetic and copies ran while one was open for 1% of the time, Pallas kernels for 40%

profile of v3, /device:TPU:0, one launch (start us, length us, event | category | flops | bytes accessed | tf_op | source)
XLA Modules:
  0.0 127.4 jit_solution(8960983510776564391)
XLA Ops:
  0.6 3.0 %collective-permute-start.5 = (bf16[2,512,256]{2,1,0:T(8,128)(2,1)}, bf16[2,512,256]{2,1,0:T(8,128)(2,1)S(1)}, u32[]{:S(2)}, u32[]{:S(2)}) collective-permute-start(bf16[2,512,256]{2,1,0:T(8,128)(2,1)} %snap_ref.1), channel_id=1, source_target_pairs={{0,2},{1,3},{4,0},{5,1},{8,4},{9,5},{12,8},{13,9},{14,12},{15,13},... | collective-permute-start | bytes 1572872 | tf_op jit(solution)/shard_map/ppermute | solution.py:143
  9.4 2.0 %collective-permute-start.2 = (bf16[656,128]{1,0:T(8,128)(2,1)S(1)}, bf16[656,128]{1,0:T(8,128)(2,1)S(1)}, u32[]{:S(2)}, u32[]{:S(2)}) collective-permute-start(bf16[656,128]{1,0:T(8,128)(2,1)S(1)} %pack.2.event_ref.refs_0_), channel_id=1, source_target_pairs={{0,2},{1,3},{4,0},{5,1},{8,4},{9,5},{12,8},{13,9},{14,12},{15,13},... | collective-permute-start | bytes 503816 | tf_op jit(solution)/shard_map/ppermute | solution.py:143
  11.5 5.8 %copy-done = f32[512,8192]{1,0:T(8,128)S(1)} copy-done((f32[512,8192]{1,0:T(8,128)S(1)}, f32[512,8192]{1,0:T(8,128)}, u32[]{:S(2)}) %copy-start) | copy-done | bytes 16777240
  24.9 2.8 %collective-permute-done.6.refs_0_ = bf16[656,128]{1,0:T(8,128)(2,1)S(1)} collective-permute-done((bf16[656,128]{1,0:T(8,128)(2,1)S(1)}, bf16[656,128]{1,0:T(8,128)(2,1)S(1)}, u32[]{:S(2)}, u32[]{:S(2)}) %collective-permute-start.6) | collective-permute-done | bytes 167968 | tf_op jit(solution)/shard_map/ppermute | solution.py:142
  30.4 2.7 %covariance_part.8.refs_7_ = f32[512,8192]{1,0:T(8,128)} custom-call(s32[1,18]{1,0:T(1,128)S(1)} %constant_dynamic-slice_fusion.line_ref, f32[512,8192]{1,0:T(8,128)S(1)} %copy-done.1, bf16[2,512,256]{2,1,0:T(8,128)(2,1)S(1)} %get-tuple-element.168.snap_ref.refs_0_.refs_5_.refs_7_, ...), custom_call_target="tpu_custom_call" | custom-call | tf_op jit(solution)/shard_map/covariance_part/pallas_call | solution.py:684
  33.0 1.9 %product_part.9 = (f32[512,128]{1,0:T(8,128)S(1)}, f32[128,128]{1,0:T(8,128)S(1)}, f32[128,128]{1,0:T(8,128)S(1)}) custom-call(s32[1,18]{1,0:T(1,128)S(1)} %constant_dynamic-slice_fusion.line_ref, f32[512,8192]{1,0:T(8,128)S(1)} %copy-done.1, bf16[656,128]{1,0:T(8,128)(2,1)S(1)} %get-tuple-element.175.refs_0_, ...), custom_call_target="tpu_custom_call" | custom-call | tf_op jit(solution)/shard_map/product_part/pallas_call | solution.py:168
  39.9 2.8 %covariance_part.9 = (f32[512,8192]{1,0:T(8,128)}, bf16[2,512,256]{2,1,0:T(8,128)(2,1)S(1)}, bf16[2,512,256]{2,1,0:T(8,128)(2,1)S(1)}) custom-call(s32[1,18]{1,0:T(1,128)S(1)} %constant_dynamic-slice_fusion.line_ref, f32[512,8192]{1,0:T(8,128)S(1)} %copy-done.1, ...), custom_call_target="tpu_custom_call", output_to_operand_aliasing={{0}: (5, {})} | custom-call | tf_op jit(solution)/shard_map/covariance_part/pallas_call | solution.py:684
  42.7 1.9 %product_part.10 = (f32[512,128]{1,0:T(8,128)S(1)}, f32[128,128]{1,0:T(8,128)S(1)}, f32[128,128]{1,0:T(8,128)S(1)}) custom-call(s32[1,18]{1,0:T(1,128)S(1)} %constant_dynamic-slice_fusion.line_ref, f32[512,8192]{1,0:T(8,128)S(1)} %copy-done.1, bf16[656,128]{1,0:T(8,128)(2,1)S(1)} %get-tuple-element.184.refs_0_, ...), custom_call_target="tpu_custom_call" | custom-call | tf_op jit(solution)/shard_map/product_part/pallas_call | solution.py:168
  45.3 1.9 %product_part.11 = (f32[512,128]{1,0:T(8,128)S(1)}, f32[128,128]{1,0:T(8,128)S(1)}, f32[128,128]{1,0:T(8,128)S(1)}) custom-call(s32[1,18]{1,0:T(1,128)S(1)} %constant_dynamic-slice_fusion.line_ref, f32[512,8192]{1,0:T(8,128)S(1)} %copy-done.1, bf16[656,128]{1,0:T(8,128)(2,1)S(1)} %get-tuple-element.197.first_ref.refs_0_, ...), custom_call_target="tpu_custom_call" | custom-call | tf_op jit(solution)/shard_map/product_part/pallas_call | solution.py:168
  56.4 2.7 %covariance_part.10.refs_5_ = f32[512,8192]{1,0:T(8,128)} custom-call(s32[1,18]{1,0:T(1,128)S(1)} %constant_dynamic-slice_fusion.line_ref, f32[512,8192]{1,0:T(8,128)S(1)} %copy-done.1, bf16[2,512,256]{2,1,0:T(8,128)(2,1)S(1)} %get-tuple-element.168.snap_ref.refs_0_.refs_5_.refs_7_, ...), custom_call_target="tpu_custom_call", output_to_operand_aliasing={{}: (5, {})} | custom-call | tf_op jit(solution)/shard_map/covariance_part/pallas_call | solution.py:684
  59.0 2.3 %collective-permute-done.25.refs_1_ = bf16[784,128]{1,0:T(8,128)(2,1)S(1)} collective-permute-done((bf16[784,128]{1,0:T(8,128)(2,1)S(1)}, bf16[784,128]{1,0:T(8,128)(2,1)S(1)}, u32[]{:S(2)}, u32[]{:S(2)}) %collective-permute-start.25) | collective-permute-done | bytes 200736 | tf_op jit(solution)/shard_map/ppermute | solution.py:143
  66.2 2.7 %covariance_part.11.refs_9_ = f32[512,8192]{1,0:T(8,128)} custom-call(s32[1,18]{1,0:T(1,128)S(1)} %constant_dynamic-slice_fusion.line_ref, f32[512,8192]{1,0:T(8,128)S(1)} %copy-done.1, bf16[2,512,256]{2,1,0:T(8,128)(2,1)S(1)} %get-tuple-element.168.snap_ref.refs_0_.refs_5_.refs_7_, ...), custom_call_target="tpu_custom_call", output_to_operand_aliasing={{}: (5, {})} | custom-call | tf_op jit(solution)/shard_map/covariance_part/pallas_call | solution.py:684
  71.6 2.7 %covariance_part.12.refs_9_ = f32[512,8192]{1,0:T(8,128)} custom-call(s32[1,18]{1,0:T(1,128)S(1)} %constant_dynamic-slice_fusion.line_ref, f32[512,8192]{1,0:T(8,128)S(1)} %copy-done.1, bf16[2,512,256]{2,1,0:T(8,128)(2,1)S(1)} %get-tuple-element.168.snap_ref.refs_0_.refs_5_.refs_7_, ...), custom_call_target="tpu_custom_call", output_to_operand_aliasing={{}: (5, {})} | custom-call | tf_op jit(solution)/shard_map/covariance_part/pallas_call | solution.py:684
  74.2 2.5 %product_part.13 = (f32[512,128]{1,0:T(8,128)S(1)}, f32[256,128]{1,0:T(8,128)S(1)}, f32[256,128]{1,0:T(8,128)S(1)}, f32[128,128]{1,0:T(8,128)S(1)}, f32[1,128]{1,0:T(1,128)S(1)}) custom-call(s32[1,18]{1,0:T(1,128)S(1)} %constant_dynamic-slice_fusion.line_ref, f32[512,8192]{1,0:T(8,128)S(1)} %copy-done.1, bf16[784,128]{1,0:T(8,128)(2,1)S(1)} %get-tuple-element.238.refs_0_, ...), custom_call_target="tpu_custom_call" | custom-call | tf_op jit(solution)/shard_map/product_part/pallas_call | solution.py:168
  79.5 2.5 %product_part.14 = (f32[512,128]{1,0:T(8,128)S(1)}, f32[256,128]{1,0:T(8,128)S(1)}, f32[256,128]{1,0:T(8,128)S(1)}, f32[128,128]{1,0:T(8,128)S(1)}, f32[1,128]{1,0:T(1,128)S(1)}) custom-call(s32[1,18]{1,0:T(1,128)S(1)} %constant_dynamic-slice_fusion.line_ref, f32[512,8192]{1,0:T(8,128)S(1)} %copy-done.1, bf16[784,128]{1,0:T(8,128)(2,1)S(1)} %get-tuple-element.251.refs_0_, ...), custom_call_target="tpu_custom_call" | custom-call | tf_op jit(solution)/shard_map/product_part/pallas_call | solution.py:168
  85.2 2.5 %product_part.15 = (f32[512,128]{1,0:T(8,128)S(1)}, f32[256,128]{1,0:T(8,128)S(1)}, f32[256,128]{1,0:T(8,128)S(1)}, f32[128,128]{1,0:T(8,128)S(1)}, f32[1,128]{1,0:T(1,128)S(1)}) custom-call(s32[1,18]{1,0:T(1,128)S(1)} %constant_dynamic-slice_fusion.line_ref, f32[512,8192]{1,0:T(8,128)S(1)} %copy-done.1, ...), custom_call_target="tpu_custom_call" | custom-call | tf_op jit(solution)/shard_map/product_part/pallas_call | solution.py:168
  87.7 2.3 %product_end.3 = (f32[512,128]{1,0:T(8,128)S(1)}, f32[64,128]{1,0:T(8,128)S(1)}, f32[64,128]{1,0:T(8,128)S(1)}, f32[128,128]{1,0:T(8,128)S(1)}) custom-call(s32[1,18]{1,0:T(1,128)S(1)} %constant_dynamic-slice_fusion.line_ref, f32[512,8192]{1,0:T(8,128)S(1)} %copy-done.1, bf16[784,128]{1,0:T(8,128)(2,1)S(1)} %get-tuple-element.290.refs_0_, ...), custom_call_target="tpu_custom_call" | custom-call | tf_op jit(solution)/shard_map/product_end/pallas_call | solution.py:510
  90.6 4.9 %factor.1.refs_3_ = f32[128,128]{1,0:T(8,128)S(1)} custom-call(s32[1,18]{1,0:T(1,128)S(1)} %constant_dynamic-slice_fusion.line_ref, f32[128,128]{1,0:T(8,128)S(1)} %get-tuple-element.307.gram_ref), custom_call_target="tpu_custom_call" | custom-call | tf_op jit(solution)/shard_map/factor/pallas_call | solution.py:168
  98.0 1.8 %collective-permute-start.45 = (bf16[2,512,256]{2,1,0:T(8,128)(2,1)S(1)}, bf16[2,512,256]{2,1,0:T(8,128)(2,1)S(1)}, u32[]{:S(2)}, u32[]{:S(2)}) collective-permute-start(bf16[2,512,256]{2,1,0:T(8,128)(2,1)S(1)} %choose.5), channel_id=1, source_target_pairs={{0,4},{4,8},{8,12},{12,14},{14,10},{10,6},{6,2},{2,0},{1,3},{5,1},... | collective-permute-start | bytes 1572872 | tf_op jit(solution)/shard_map/ppermute | solution.py:139
  100.8 2.7 %covariance_part.13.refs_5_ = f32[512,8192]{1,0:T(8,128)} custom-call(s32[1,18]{1,0:T(1,128)S(1)} %constant_dynamic-slice_fusion.line_ref, f32[512,8192]{1,0:T(8,128)S(1)} %copy-done.1, bf16[2,512,256]{2,1,0:T(8,128)(2,1)S(1)} %get-tuple-element.168.snap_ref.refs_0_.refs_5_.refs_7_, ...), custom_call_target="tpu_custom_call", output_to_operand_aliasing={{}: (5, {})} | custom-call | tf_op jit(solution)/shard_map/covariance_part/pallas_call | solution.py:684
  103.5 4.7 %collective-permute-done.44.refs_1_ = f32[64,128]{1,0:T(8,128)S(1)} collective-permute-done((f32[64,128]{1,0:T(8,128)S(1)}, f32[64,128]{1,0:T(8,128)S(1)}, u32[]{:S(2)}, u32[]{:S(2)}) %collective-permute-start.44) | collective-permute-done | bytes 32800 | tf_op jit(solution)/shard_map/ppermute | solution.py:249
  109.1 2.7 %covariance_part.14.refs_3_ = f32[512,8192]{1,0:T(8,128)} custom-call(s32[1,18]{1,0:T(1,128)S(1)} %constant_dynamic-slice_fusion.line_ref, f32[512,8192]{1,0:T(8,128)S(1)} %copy-done.1, bf16[2,512,256]{2,1,0:T(8,128)(2,1)S(1)} %get-tuple-element.168.snap_ref.refs_0_.refs_5_.refs_7_, ...), custom_call_target="tpu_custom_call", output_to_operand_aliasing={{}: (5, {})} | custom-call | tf_op jit(solution)/shard_map/covariance_part/pallas_call | solution.py:684
  114.4 2.7 %covariance_part.15.refs_2_ = f32[512,8192]{1,0:T(8,128)} custom-call(s32[1,18]{1,0:T(1,128)S(1)} %constant_dynamic-slice_fusion.line_ref, f32[512,8192]{1,0:T(8,128)S(1)} %copy-done.1, bf16[2,512,256]{2,1,0:T(8,128)(2,1)S(1)} %get-tuple-element.168.snap_ref.refs_0_.refs_5_.refs_7_, ...), custom_call_target="tpu_custom_call", output_to_operand_aliasing={{}: (5, {})} | custom-call | tf_op jit(solution)/shard_map/covariance_part/pallas_call | solution.py:684
  120.5 5.4 %both_factors.1.factors_ref = f32[128,128]{1,0:T(8,128)S(1)} custom-call(s32[1,18]{1,0:T(1,128)S(1)} %constant_dynamic-slice_fusion.line_ref, f32[64,128]{1,0:T(8,128)S(1)} %get-tuple-element.325.gram_ref, f32[64,128]{1,0:T(8,128)S(1)} %collective-permute-done.51.theirs_ref, f32[128,128]{1,0:T(8,128)S(1)} %get-tuple-element.326.first_ref), custom_call_target="tpu_custom_call" | custom-call | tf_op jit(solution)/shard_map/both_factors/pallas_call | solution.py:636
  (147 shorter events, 56.7 us)
Async XLA Ops:
  0.6 20.2 %collective-permute-start.5 = (bf16[2,512,256]{2,1,0:T(8,128)(2,1)}, bf16[2,512,256]{2,1,0:T(8,128)(2,1)S(1)}, u32[]{:S(2)}, u32[]{:S(2)}) collective-permute-start(bf16[2,512,256]{2,1,0:T(8,128)(2,1)} %snap_ref.1), channel_id=1, source_target_pairs={{0,2},{1,3},{4,0},{5,1},{8,4},{9,5},{12,8},{13,9},{14,12},{15,13},... | collective-permute-start | bytes 1572872 | tf_op jit(solution)/shard_map/ppermute | solution.py:143
  3.6 17.2 %collective-permute-start.4 = (bf16[2,512,256]{2,1,0:T(8,128)(2,1)}, bf16[2,512,256]{2,1,0:T(8,128)(2,1)S(1)}, u32[]{:S(2)}, u32[]{:S(2)}) collective-permute-start(bf16[2,512,256]{2,1,0:T(8,128)(2,1)} %snap_ref.1), channel_id=1, source_target_pairs={{0,4},{1,5},{4,8},{5,9},{8,12},{9,13},{12,14},{13,15},{14,10},{15,... | collective-permute-start | bytes 1572872 | tf_op jit(solution)/shard_map/ppermute | solution.py:142
  9.4 10.1 %collective-permute-start.2 = (bf16[656,128]{1,0:T(8,128)(2,1)S(1)}, bf16[656,128]{1,0:T(8,128)(2,1)S(1)}, u32[]{:S(2)}, u32[]{:S(2)}) collective-permute-start(bf16[656,128]{1,0:T(8,128)(2,1)S(1)} %pack.2.event_ref.refs_0_), channel_id=1, source_target_pairs={{0,2},{1,3},{4,0},{5,1},{8,4},{9,5},{12,8},{13,9},{14,12},{15,13},... | collective-permute-start | bytes 503816 | tf_op jit(solution)/shard_map/ppermute | solution.py:143
  11.3 9.5 %collective-permute-start.1 = (bf16[656,128]{1,0:T(8,128)(2,1)S(1)}, bf16[656,128]{1,0:T(8,128)(2,1)S(1)}, u32[]{:S(2)}, u32[]{:S(2)}) collective-permute-start(bf16[656,128]{1,0:T(8,128)(2,1)S(1)} %pack.2.event_ref.refs_0_), channel_id=1, source_target_pairs={{0,4},{1,5},{4,8},{5,9},{8,12},{9,13},{12,14},{13,15},{14,10},{15,... | collective-permute-start | bytes 503816 | tf_op jit(solution)/shard_map/ppermute | solution.py:142
  11.4 9.4 %collective-permute-start.3 = (bf16[656,128]{1,0:T(8,128)(2,1)S(1)}, bf16[656,128]{1,0:T(8,128)(2,1)S(1)}, u32[]{:S(2)}, u32[]{:S(2)}) collective-permute-start(bf16[656,128]{1,0:T(8,128)(2,1)S(1)} %pack.2.event_ref.refs_0_), channel_id=1, source_target_pairs={{0,1},{1,0},{2,3},{3,2},{4,5},{5,4},{6,7},{7,6},{8,9},{9,8},{10,11... | collective-permute-start | bytes 503816 | tf_op jit(solution)/shard_map/ppermute | solution.py:121
  27.8 7.2 %collective-permute-start.11 = (bf16[656,128]{1,0:T(8,128)(2,1)S(1)}, bf16[656,128]{1,0:T(8,128)(2,1)S(1)}, u32[]{:S(2)}, u32[]{:S(2)}) collective-permute-start(bf16[656,128]{1,0:T(8,128)(2,1)S(1)} %get-tuple-element.184.refs_0_), channel_id=1, source_target_pairs={{0,4},{1,5},{4,8},{5,9},{8,12},{9,13},{12,14},{13,15},{14,10},{15,... | collective-permute-start | bytes 503816 | tf_op jit(solution)/shard_map/ppermute | solution.py:142
  35.6 9.0 %collective-permute-start.17 = (bf16[656,128]{1,0:T(8,128)(2,1)S(1)}, bf16[656,128]{1,0:T(8,128)(2,1)S(1)}, u32[]{:S(2)}, u32[]{:S(2)}) collective-permute-start(bf16[656,128]{1,0:T(8,128)(2,1)S(1)} %get-tuple-element.205), channel_id=1, source_target_pairs={{0,4},{4,8},{8,12},{12,14},{14,10},{10,6},{6,2},{2,0},{1,3},{5,1},... | collective-permute-start | bytes 503816 | tf_op jit(solution)/shard_map/ppermute | solution.py:139
  37.4 7.3 %collective-permute-start.18 = (bf16[656,128]{1,0:T(8,128)(2,1)S(1)}, bf16[656,128]{1,0:T(8,128)(2,1)S(1)}, u32[]{:S(2)}, u32[]{:S(2)}) collective-permute-start(bf16[656,128]{1,0:T(8,128)(2,1)S(1)} %get-tuple-element.197.first_ref.refs_0_), channel_id=1, source_target_pairs={{0,1},{1,0},{2,3},{3,2},{4,5},{5,4},{6,7},{7,6},{8,9},{9,8},{10,11... | collective-permute-start | bytes 503816 | tf_op jit(solution)/shard_map/ppermute | solution.py:121
  37.4 7.3 %collective-permute-start.19 = (bf16[656,128]{1,0:T(8,128)(2,1)S(1)}, bf16[656,128]{1,0:T(8,128)(2,1)S(1)}, u32[]{:S(2)}, u32[]{:S(2)}) collective-permute-start(bf16[656,128]{1,0:T(8,128)(2,1)S(1)} %get-tuple-element.198.second_ref.refs_2_), channel_id=1, source_target_pairs={{0,1},{1,0},{2,3},{3,2},{4,5},{5,4},{6,7},{7,6},{8,9},{9,8},{10,11... | collective-permute-start | bytes 503816 | tf_op jit(solution)/shard_map/ppermute | solution.py:121
  37.9 14.4 %collective-permute-start.15 = (bf16[2,512,256]{2,1,0:T(8,128)(2,1)S(1)}, bf16[2,512,256]{2,1,0:T(8,128)(2,1)S(1)}, u32[]{:S(2)}, u32[]{:S(2)}) collective-permute-start(bf16[2,512,256]{2,1,0:T(8,128)(2,1)S(1)} %get-tuple-element.203.refs_0_), channel_id=1, source_target_pairs={{0,4},{1,5},{4,8},{5,9},{8,12},{9,13},{12,14},{13,15},{14,10},{15,... | collective-permute-start | bytes 1572872 | tf_op jit(solution)/shard_map/ppermute | solution.py:142
  39.5 13.6 %collective-permute-start.16 = (bf16[2,512,256]{2,1,0:T(8,128)(2,1)S(1)}, bf16[2,512,256]{2,1,0:T(8,128)(2,1)S(1)}, u32[]{:S(2)}, u32[]{:S(2)}) collective-permute-start(bf16[2,512,256]{2,1,0:T(8,128)(2,1)S(1)} %get-tuple-element.204.refs_1_), channel_id=1, source_target_pairs={{0,2},{1,3},{4,0},{5,1},{8,4},{9,5},{12,8},{13,9},{14,12},{15,13},... | collective-permute-start | bytes 1572872 | tf_op jit(solution)/shard_map/ppermute | solution.py:143
  44.7 8.3 %collective-permute-start.20 = (bf16[2,512,256]{2,1,0:T(8,128)(2,1)S(1)}, bf16[2,512,256]{2,1,0:T(8,128)(2,1)S(1)}, u32[]{:S(2)}, u32[]{:S(2)}) collective-permute-start(bf16[2,512,256]{2,1,0:T(8,128)(2,1)S(1)} %get-tuple-element.217), channel_id=1, source_target_pairs={{0,1},{1,0},{2,3},{3,2},{4,5},{5,4},{6,7},{7,6},{8,9},{9,8},{10,11... | collective-permute-start | bytes 1572872 | tf_op jit(solution)/shard_map/ppermute | solution.py:121
  44.8 8.3 %collective-permute-start.21 = (bf16[2,512,256]{2,1,0:T(8,128)(2,1)S(1)}, bf16[2,512,256]{2,1,0:T(8,128)(2,1)S(1)}, u32[]{:S(2)}, u32[]{:S(2)}) collective-permute-start(bf16[2,512,256]{2,1,0:T(8,128)(2,1)S(1)} %get-tuple-element.218), channel_id=1, source_target_pairs={{0,1},{1,0},{2,3},{3,2},{4,5},{5,4},{6,7},{7,6},{8,9},{9,8},{10,11... | collective-permute-start | bytes 1572872 | tf_op jit(solution)/shard_map/ppermute | solution.py:121
  53.8 8.2 %collective-permute-start.27 = (bf16[2,512,256]{2,1,0:T(8,128)(2,1)S(1)}, bf16[2,512,256]{2,1,0:T(8,128)(2,1)S(1)}, u32[]{:S(2)}, u32[]{:S(2)}) collective-permute-start(bf16[2,512,256]{2,1,0:T(8,128)(2,1)S(1)} %get-tuple-element.235.refs_0_.refs_3_), channel_id=1, source_target_pairs={{0,1},{1,0},{2,3},{3,2},{4,5},{5,4},{6,7},{7,6},{8,9},{9,8},{10,11... | collective-permute-start | bytes 1572872 | tf_op jit(solution)/shard_map/ppermute | solution.py:121
  53.8 8.1 %collective-permute-start.28 = (bf16[2,512,256]{2,1,0:T(8,128)(2,1)S(1)}, bf16[2,512,256]{2,1,0:T(8,128)(2,1)S(1)}, u32[]{:S(2)}, u32[]{:S(2)}) collective-permute-start(bf16[2,512,256]{2,1,0:T(8,128)(2,1)S(1)} %get-tuple-element.236.refs_1_.refs_4_), channel_id=1, source_target_pairs={{0,1},{1,0},{2,3},{3,2},{4,5},{5,4},{6,7},{7,6},{8,9},{9,8},{10,11... | collective-permute-start | bytes 1572872 | tf_op jit(solution)/shard_map/ppermute | solution.py:121
  54.3 7.0 %collective-permute-start.25 = (bf16[784,128]{1,0:T(8,128)(2,1)S(1)}, bf16[784,128]{1,0:T(8,128)(2,1)S(1)}, u32[]{:S(2)}, u32[]{:S(2)}) collective-permute-start(bf16[784,128]{1,0:T(8,128)(2,1)S(1)} %pack.3.refs_2_.refs_0_), channel_id=1, source_target_pairs={{0,2},{1,3},{4,0},{5,1},{8,4},{9,5},{12,8},{13,9},{14,12},{15,13},... | collective-permute-start | bytes 602120 | tf_op jit(solution)/shard_map/ppermute | solution.py:143
  62.0 6.9 %collective-permute-start.29 = (bf16[784,128]{1,0:T(8,128)(2,1)S(1)}, bf16[784,128]{1,0:T(8,128)(2,1)S(1)}, u32[]{:S(2)}, u32[]{:S(2)}) collective-permute-start(bf16[784,128]{1,0:T(8,128)(2,1)S(1)} %get-tuple-element.238.refs_0_), channel_id=1, source_target_pairs={{0,4},{1,5},{4,8},{5,9},{8,12},{9,13},{12,14},{13,15},{14,10},{15,... | collective-permute-start | bytes 602120 | tf_op jit(solution)/shard_map/ppermute | solution.py:142
  69.0 7.7 %collective-permute-start.33 = (bf16[784,128]{1,0:T(8,128)(2,1)S(1)}, bf16[784,128]{1,0:T(8,128)(2,1)S(1)}, u32[]{:S(2)}, u32[]{:S(2)}) collective-permute-start(bf16[784,128]{1,0:T(8,128)(2,1)S(1)} %get-tuple-element.251.refs_0_), channel_id=1, source_target_pairs={{0,4},{1,5},{4,8},{5,9},{8,12},{9,13},{12,14},{13,15},{14,10},{15,... | collective-permute-start | bytes 602120 | tf_op jit(solution)/shard_map/ppermute | solution.py:142
  83.1 13.0 %collective-permute-start.42 = (bf16[2,512,256]{2,1,0:T(8,128)(2,1)S(1)}, bf16[2,512,256]{2,1,0:T(8,128)(2,1)S(1)}, u32[]{:S(2)}, u32[]{:S(2)}) collective-permute-start(bf16[2,512,256]{2,1,0:T(8,128)(2,1)S(1)} %get-tuple-element.305), channel_id=1, source_target_pairs={{0,4},{1,5},{4,8},{5,9},{8,12},{9,13},{12,14},{13,15},{14,10},{15,... | collective-permute-start | bytes 1572872 | tf_op jit(solution)/shard_map/ppermute | solution.py:142
  84.8 12.6 %collective-permute-start.43 = (bf16[2,512,256]{2,1,0:T(8,128)(2,1)S(1)}, bf16[2,512,256]{2,1,0:T(8,128)(2,1)S(1)}, u32[]{:S(2)}, u32[]{:S(2)}) collective-permute-start(bf16[2,512,256]{2,1,0:T(8,128)(2,1)S(1)} %get-tuple-element.306), channel_id=1, source_target_pairs={{0,2},{1,3},{4,0},{5,1},{8,4},{9,5},{12,8},{13,9},{14,12},{15,13},... | collective-permute-start | bytes 1572872 | tf_op jit(solution)/shard_map/ppermute | solution.py:143
  98.0 10.8 %collective-permute-start.45 = (bf16[2,512,256]{2,1,0:T(8,128)(2,1)S(1)}, bf16[2,512,256]{2,1,0:T(8,128)(2,1)S(1)}, u32[]{:S(2)}, u32[]{:S(2)}) collective-permute-start(bf16[2,512,256]{2,1,0:T(8,128)(2,1)S(1)} %choose.5), channel_id=1, source_target_pairs={{0,4},{4,8},{8,12},{12,14},{14,10},{10,6},{6,2},{2,0},{1,3},{5,1},... | collective-permute-start | bytes 1572872 | tf_op jit(solution)/shard_map/ppermute | solution.py:139
  99.8 8.9 %collective-permute-start.46 = (bf16[2,512,256]{2,1,0:T(8,128)(2,1)S(1)}, bf16[2,512,256]{2,1,0:T(8,128)(2,1)S(1)}, u32[]{:S(2)}, u32[]{:S(2)}) collective-permute-start(bf16[2,512,256]{2,1,0:T(8,128)(2,1)S(1)} %get-tuple-element.310.first_ref.refs_0_), channel_id=1, source_target_pairs={{0,1},{1,0},{2,3},{3,2},{4,5},{5,4},{6,7},{7,6},{8,9},{9,8},{10,11... | collective-permute-start | bytes 1572872 | tf_op jit(solution)/shard_map/ppermute | solution.py:121
  99.8 8.9 %collective-permute-start.47 = (bf16[2,512,256]{2,1,0:T(8,128)(2,1)S(1)}, bf16[2,512,256]{2,1,0:T(8,128)(2,1)S(1)}, u32[]{:S(2)}, u32[]{:S(2)}) collective-permute-start(bf16[2,512,256]{2,1,0:T(8,128)(2,1)S(1)} %get-tuple-element.311.second_ref.refs_1_), channel_id=1, source_target_pairs={{0,1},{1,0},{2,3},{3,2},{4,5},{5,4},{6,7},{7,6},{8,9},{9,8},{10,11... | collective-permute-start | bytes 1572872 | tf_op jit(solution)/shard_map/ppermute | solution.py:121
  100.3 7.8 %collective-permute-start.44 = (f32[64,128]{1,0:T(8,128)S(1)}, f32[64,128]{1,0:T(8,128)S(1)}, u32[]{:S(2)}, u32[]{:S(2)}) collective-permute-start(f32[64,128]{1,0:T(8,128)S(1)} %get-tuple-element.309.refs_0_), channel_id=1, source_target_pairs={{0,2},{1,3},{2,0},{3,1},{4,6},{5,7},{6,4},{7,5},{8,10},{9,11},{10,... | collective-permute-start | bytes 98312 | tf_op jit(solution)/shard_map/ppermute | solution.py:249
  (32 other events, 148.3 us)

commit v4 on v3

--- a/solution.py
+++ b/solution.py
@@ -68,12 +68,13 @@
     return list(range(0, chips, 2)) + list(range(chips - 1, 0, -2))
 
 
-def ring_pairs(devices, way):
+def ring_pairs(devices, stream):
     order = ring_order(devices)
     chips = len(order)
     pairs = []
     for at in range(chips):
         for core in range(2):
+            way = 1 if core == stream else -1
             pairs.append((2 * order[at] + core, 2 * order[(at + way) % chips] + core))
     return pairs
 
@@ -90,9 +91,11 @@
         at, core = order.index(me // 2), me % 2
         line = [me * rows, (me ^ 1) * rows]
         for step in range(1, chips // 2):
-            for there in (at - step, at + step):
-                chip = order[there % chips]
-                line += [(2 * chip + core) * rows, (2 * chip + 1 - core) * rows]
+            for stream in range(2):
+                way = 1 if core == stream else -1
+                mine = order[(at - way * step) % chips]
+                theirs = order[(at + way * step) % chips]
+                line += [(2 * mine + core) * rows, (2 * theirs + 1 - core) * rows]
         chip = order[(at + chips // 2) % chips]
         line += [(2 * chip + core) * rows, (2 * chip + 1 - core) * rows]
         line += [core, (me // 2) % 2]
@@ -101,16 +104,11 @@
 
 
 class Ring:
-    def __init__(self, line, bits, block, devices):
-        self.line, self.bits = line, bits
-        self.forth, self.back = ring_pairs(devices, 1), ring_pairs(devices, -1)
-        self.apart = [p for p in self.forth if p[0] % 2 == 0] + [
-            p for p in self.back if p[0] % 2 == 1
-        ]
+    def __init__(self, block, devices):
+        self.streams = [ring_pairs(devices, stream) for stream in range(2)]
         self.swap = partner_pairs(devices, 1)
         self.steps = devices // 4
         self.done = 0
-        self.chosen = None
         self.recent = [block]
         self.groups = []
         self.new_recent = self.new_swapped = False
@@ -130,18 +128,11 @@
     def step(self):
         self.done += 1
         self.new_recent = True
-        ahead, behind = self.recent[0], self.recent[-1]
         self.full = self.recent
-        if self.done == self.steps:
-            block = ahead if self.chosen is None else self.chosen
-            if self.chosen is None and len(self.recent) == 2:
-                block = choose(self.line, self.bits[0], ahead, behind)
-            self.recent = [lax.ppermute(block, "row", self.apart)]
-        else:
-            self.recent = [
-                lax.ppermute(ahead, "row", self.forth),
-                lax.ppermute(behind, "row", self.back),
-            ]
+        sent = self.recent if len(self.recent) == 2 else self.recent * 2
+        last = self.done == self.steps
+        streams = self.streams[:1] if last else self.streams
+        self.recent = [lax.ppermute(b, "row", pairs) for b, pairs in zip(sent, streams)]
 
     def held(self):
         return (self.recent if self.new_recent else []) + (
@@ -177,20 +168,6 @@
 
 def f32(*shape):
     return jax.ShapeDtypeStruct(shape, jnp.float32)
-
-
-def choose(line, bit, first, second):
-    def kernel(line_ref, first_ref, second_ref, out_ref):
-        @pl.when(line_ref[0, bit] == 0)
-        def _():
-            out_ref[...] = first_ref[...]
-
-        @pl.when(line_ref[0, bit] == 1)
-        def _():
-            out_ref[...] = second_ref[...]
-
-    shape = jax.ShapeDtypeStruct(first.shape, first.dtype)
-    return small_kernel(kernel, shape, (line, first, second), "choose")
 
 
 def store_halves(line_ref, bit, value_ref, mine_ref, theirs_ref):
@@ -718,7 +695,7 @@
         return covariance_part(line, numbers, prior_cov, snapshots, blocks, filled, True)
 
     end = 4 * steps
-    snap_ring = Ring(line, bits, snapshots, devices)
+    snap_ring = Ring(snapshots, devices)
     snap_ring.step()
     mine, theirs, snapshots, values = first_sums(line, bits, snapshots, prior_basis)
     share = new_cov = None
@@ -726,13 +703,11 @@
         got = lax.ppermute(theirs, "row", swap)
         if window == 1:
             (values,) = gate_all([snap_ring], [values])
-        ring = Ring(line, bits, pack(line, values, mine, got, share), devices)
+        ring = Ring(pack(line, values, mine, got, share), devices)
         sum_rows = mine.shape[0]
         state = None
         for phase in range(1, steps + 1):
             if phase == steps:
-                chosen = choose(line, bits[0], *ring.recent)
-                ring.chosen, *state = gate([chosen] + list(state))
                 ready = state[0]
             sent = ring.recent
             ring.step()
@@ -749,7 +724,7 @@
                     snap_ring.recent = gate(snap_ring.recent, [sent[0]])
                     snap_ring.pass_on()
                     arrived = gate(arrived)
-                    filled = [6, 8]
+                    filled = [3, 5, 6, 8]
             else:
                 state, _ = product_part(
                     line,
@@ -772,8 +747,6 @@
                     filled = [0, 1]
                 if window == 1 and phase == 2:
                     filled = [7, 9]
-                if window == 1 and phase == 3:
-                    filled = [3, 5]
             if filled:
                 new_cov = fill(new_cov, filled)
                 extra.append(new_cov)

time: 128 us -> 125 us (0.977)
  Pallas kernels: 61.3 us -> 58.5 us
    pallas_call x20 -> x17, Pallas kernels: 28.6 us -> 26.9 us  [small_kernel(): pl.pallas_call(kernel, out_shape=out_shape, in_specs=[in_smem] + [in_vmem...]
    pallas_call x8 -> x7, Pallas kernels: 21.4 us -> 20.3 us  [covariance_part(): pl.pallas_call(kernel, out_shape=(f32(*prior_cov.shape),) + tuple((jax.Sh...]
  transfers between devices with their start and end apart: 52 -> 52, of which waited for: 17 -> 15; matrix products, arithmetic and copies ran while one was open for 1% -> 1% of each run, Pallas kernels for 40% -> 40%
where the time goes in v4:
time: 125 us; the launch traced here: 124 us
  Pallas kernels  58.5 us (47%)
  starting transfers between devices  32.1 us (26%)
  waiting for transfers between devices  24.1 us (19%)
  local copies, waits for them, and re-layouts  8.58 us (7%)
    pallas_call x17, Pallas kernels, small_kernel(): pl.pallas_call(kernel, out_shape=out_shape, in_specs=[in_smem] + [in_vmem...  26.9 us
    ppermute x21, starting transfers between devices, step(): lax.ppermute(b, 'row', pairs)  23.6 us
    pallas_call x7, Pallas kernels, covariance_part(): pl.pallas_call(kernel, out_shape=(f32(*prior_cov.shape),) + tuple((jax.Sh...  20.3 us
    ppermute x21, waiting for transfers between devices, step(): lax.ppermute(b, 'row', pairs)  13.4 us
    unnamed x8, local copies, waits for them, and re-layouts  7.88 us
    ppermute x4, waiting for transfers between devices, pass_on(): return lax.ppermute(value, 'row', partner_pairs(self.devices, mask))  7.8 us
    pallas_call x1, Pallas kernels, both_factors(): pl.pallas_call(kernel, out_shape=f32(rank, rank), in_specs=[in_smem] + [i...  5.4 us
    ppermute x24, starting transfers between devices, pass_on(): group += [block, lax.ppermute(copy, 'row', self.swap)]  5.28 us
  transfers between devices with their start and end apart: 52, of which 15 were waited for; matrix products, arithmetic and copies ran while one was open for 1% of the time, Pallas kernels for 40%

profile of v4, /device:TPU:0, one launch (start us, length us, event | category | flops | bytes accessed | tf_op | source)
XLA Modules:
  0.0 124.5 jit_solution(17275632324262617397)
XLA Ops:
  0.6 3.0 %collective-permute-start.5 = (bf16[2,512,256]{2,1,0:T(8,128)(2,1)}, bf16[2,512,256]{2,1,0:T(8,128)(2,1)S(1)}, u32[]{:S(2)}, u32[]{:S(2)}) collective-permute-start(bf16[2,512,256]{2,1,0:T(8,128)(2,1)} %snap_ref.1), channel_id=1, source_target_pairs={{0,2},{1,5},{4,0},{5,9},{8,4},{9,13},{12,8},{13,15},{14,12},{15,11... | collective-permute-start | bytes 1572872 | tf_op jit(solution)/shard_map/ppermute | solution.py:135
  9.4 2.0 %collective-permute-start.2 = (bf16[656,128]{1,0:T(8,128)(2,1)S(1)}, bf16[656,128]{1,0:T(8,128)(2,1)S(1)}, u32[]{:S(2)}, u32[]{:S(2)}) collective-permute-start(bf16[656,128]{1,0:T(8,128)(2,1)S(1)} %pack.2.event_ref.refs_0_), channel_id=1, source_target_pairs={{0,2},{1,5},{4,0},{5,9},{8,4},{9,13},{12,8},{13,15},{14,12},{15,11... | collective-permute-start | bytes 503816 | tf_op jit(solution)/shard_map/ppermute | solution.py:135
  11.5 5.8 %copy-done = f32[512,8192]{1,0:T(8,128)S(1)} copy-done((f32[512,8192]{1,0:T(8,128)S(1)}, f32[512,8192]{1,0:T(8,128)}, u32[]{:S(2)}) %copy-start) | copy-done | bytes 16777240
  20.2 2.1 %collective-permute-start.6 = (bf16[656,128]{1,0:T(8,128)(2,1)S(1)}, bf16[656,128]{1,0:T(8,128)(2,1)S(1)}, u32[]{:S(2)}, u32[]{:S(2)}) collective-permute-start(bf16[656,128]{1,0:T(8,128)(2,1)S(1)} %get-tuple-element.164.refs_0_), channel_id=1, source_target_pairs={{0,4},{1,3},{4,8},{5,1},{8,12},{9,5},{12,14},{13,9},{14,10},{15,13... | collective-permute-start | bytes 503816 | tf_op jit(solution)/shard_map/ppermute | solution.py:135
  24.3 2.8 %collective-permute-done.6.refs_0_ = bf16[656,128]{1,0:T(8,128)(2,1)S(1)} collective-permute-done((bf16[656,128]{1,0:T(8,128)(2,1)S(1)}, bf16[656,128]{1,0:T(8,128)(2,1)S(1)}, u32[]{:S(2)}, u32[]{:S(2)}) %collective-permute-start.6) | collective-permute-done | bytes 167968 | tf_op jit(solution)/shard_map/ppermute | solution.py:135
  30.4 2.7 %covariance_part.7.refs_7_ = f32[512,8192]{1,0:T(8,128)} custom-call(s32[1,18]{1,0:T(1,128)S(1)} %constant_dynamic-slice_fusion.line_ref, f32[512,8192]{1,0:T(8,128)S(1)} %copy-done.1, bf16[2,512,256]{2,1,0:T(8,128)(2,1)S(1)} %get-tuple-element.157.snap_ref.refs_0_.refs_5_.refs_7_, ...), custom_call_target="tpu_custom_call" | custom-call | tf_op jit(solution)/shard_map/covariance_part/pallas_call | solution.py:661
  33.0 1.9 %product_part.9 = (f32[512,128]{1,0:T(8,128)S(1)}, f32[128,128]{1,0:T(8,128)S(1)}, f32[128,128]{1,0:T(8,128)S(1)}) custom-call(s32[1,18]{1,0:T(1,128)S(1)} %constant_dynamic-slice_fusion.line_ref, f32[512,8192]{1,0:T(8,128)S(1)} %copy-done.1, bf16[656,128]{1,0:T(8,128)(2,1)S(1)} %get-tuple-element.164.refs_0_, ...), custom_call_target="tpu_custom_call" | custom-call | tf_op jit(solution)/shard_map/product_part/pallas_call | solution.py:159
  39.2 2.8 %covariance_part.8 = (f32[512,8192]{1,0:T(8,128)}, bf16[2,512,256]{2,1,0:T(8,128)(2,1)S(1)}, bf16[2,512,256]{2,1,0:T(8,128)(2,1)S(1)}) custom-call(s32[1,18]{1,0:T(1,128)S(1)} %constant_dynamic-slice_fusion.line_ref, f32[512,8192]{1,0:T(8,128)S(1)} %copy-done.1, ...), custom_call_target="tpu_custom_call", output_to_operand_aliasing={{0}: (5, {})} | custom-call | tf_op jit(solution)/shard_map/covariance_part/pallas_call | solution.py:661
  42.0 1.9 %product_part.10 = (f32[512,128]{1,0:T(8,128)S(1)}, f32[128,128]{1,0:T(8,128)S(1)}, f32[128,128]{1,0:T(8,128)S(1)}) custom-call(s32[1,18]{1,0:T(1,128)S(1)} %constant_dynamic-slice_fusion.line_ref, f32[512,8192]{1,0:T(8,128)S(1)} %copy-done.1, bf16[656,128]{1,0:T(8,128)(2,1)S(1)} %get-tuple-element.173.refs_0_, ...), custom_call_target="tpu_custom_call" | custom-call | tf_op jit(solution)/shard_map/product_part/pallas_call | solution.py:159
  44.6 1.9 %product_part.11 = (f32[512,128]{1,0:T(8,128)S(1)}, f32[128,128]{1,0:T(8,128)S(1)}, f32[128,128]{1,0:T(8,128)S(1)}) custom-call(s32[1,18]{1,0:T(1,128)S(1)} %constant_dynamic-slice_fusion.line_ref, f32[512,8192]{1,0:T(8,128)S(1)} %copy-done.1, bf16[656,128]{1,0:T(8,128)(2,1)S(1)} %get-tuple-element.189.refs_0_, ...), custom_call_target="tpu_custom_call" | custom-call | tf_op jit(solution)/shard_map/product_part/pallas_call | solution.py:159
  49.8 1.9 %collective-permute-done.15.refs_0_ = bf16[2,512,256]{2,1,0:T(8,128)(2,1)S(1)} collective-permute-done((bf16[2,512,256]{2,1,0:T(8,128)(2,1)S(1)}, bf16[2,512,256]{2,1,0:T(8,128)(2,1)S(1)}, u32[]{:S(2)}, u32[]{:S(2)}) %collective-permute-start.15) | collective-permute-done | bytes 524320 | tf_op jit(solution)/shard_map/ppermute | solution.py:135
  55.1 4.2 %covariance_part.9.refs_5_ = f32[512,8192]{1,0:T(8,128)} custom-call(s32[1,18]{1,0:T(1,128)S(1)} %constant_dynamic-slice_fusion.line_ref, f32[512,8192]{1,0:T(8,128)S(1)} %copy-done.1, bf16[2,512,256]{2,1,0:T(8,128)(2,1)S(1)} %get-tuple-element.157.snap_ref.refs_0_.refs_5_.refs_7_, ...), custom_call_target="tpu_custom_call", output_to_operand_aliasing={{}: (7, {})} | custom-call | tf_op jit(solution)/shard_map/covariance_part/pallas_call | solution.py:661
  64.9 2.7 %covariance_part.10.refs_9_ = f32[512,8192]{1,0:T(8,128)} custom-call(s32[1,18]{1,0:T(1,128)S(1)} %constant_dynamic-slice_fusion.line_ref, f32[512,8192]{1,0:T(8,128)S(1)} %copy-done.1, bf16[2,512,256]{2,1,0:T(8,128)(2,1)S(1)} %get-tuple-element.157.snap_ref.refs_0_.refs_5_.refs_7_, ...), custom_call_target="tpu_custom_call", output_to_operand_aliasing={{}: (5, {})} | custom-call | tf_op jit(solution)/shard_map/covariance_part/pallas_call | solution.py:661
  70.9 2.5 %product_part.13 = (f32[512,128]{1,0:T(8,128)S(1)}, f32[256,128]{1,0:T(8,128)S(1)}, f32[256,128]{1,0:T(8,128)S(1)}, f32[128,128]{1,0:T(8,128)S(1)}, f32[1,128]{1,0:T(1,128)S(1)}) custom-call(s32[1,18]{1,0:T(1,128)S(1)} %constant_dynamic-slice_fusion.line_ref, f32[512,8192]{1,0:T(8,128)S(1)} %copy-done.1, bf16[784,128]{1,0:T(8,128)(2,1)S(1)} %get-tuple-element.225.refs_0_, ...), custom_call_target="tpu_custom_call" | custom-call | tf_op jit(solution)/shard_map/product_part/pallas_call | solution.py:159
  73.4 2.3 %collective-permute-done.33.refs_0_ = bf16[784,128]{1,0:T(8,128)(2,1)S(1)} collective-permute-done((bf16[784,128]{1,0:T(8,128)(2,1)S(1)}, bf16[784,128]{1,0:T(8,128)(2,1)S(1)}, u32[]{:S(2)}, u32[]{:S(2)}) %collective-permute-start.33) | collective-permute-done | bytes 200736 | tf_op jit(solution)/shard_map/ppermute | solution.py:135
  77.4 2.5 %product_part.14 = (f32[512,128]{1,0:T(8,128)S(1)}, f32[256,128]{1,0:T(8,128)S(1)}, f32[256,128]{1,0:T(8,128)S(1)}, f32[128,128]{1,0:T(8,128)S(1)}, f32[1,128]{1,0:T(1,128)S(1)}) custom-call(s32[1,18]{1,0:T(1,128)S(1)} %constant_dynamic-slice_fusion.line_ref, f32[512,8192]{1,0:T(8,128)S(1)} %copy-done.1, bf16[784,128]{1,0:T(8,128)(2,1)S(1)} %get-tuple-element.238.refs_0_, ...), custom_call_target="tpu_custom_call" | custom-call | tf_op jit(solution)/shard_map/product_part/pallas_call | solution.py:159
  83.5 2.5 %product_part.15 = (f32[512,128]{1,0:T(8,128)S(1)}, f32[256,128]{1,0:T(8,128)S(1)}, f32[256,128]{1,0:T(8,128)S(1)}, f32[128,128]{1,0:T(8,128)S(1)}, f32[1,128]{1,0:T(1,128)S(1)}) custom-call(s32[1,18]{1,0:T(1,128)S(1)} %constant_dynamic-slice_fusion.line_ref, f32[512,8192]{1,0:T(8,128)S(1)} %copy-done.1, bf16[784,128]{1,0:T(8,128)(2,1)S(1)} %get-tuple-element.254.refs_0_, ...), custom_call_target="tpu_custom_call" | custom-call | tf_op jit(solution)/shard_map/product_part/pallas_call | solution.py:159
  86.0 2.3 %product_end.3 = (f32[512,128]{1,0:T(8,128)S(1)}, f32[64,128]{1,0:T(8,128)S(1)}, f32[64,128]{1,0:T(8,128)S(1)}, f32[128,128]{1,0:T(8,128)S(1)}) custom-call(s32[1,18]{1,0:T(1,128)S(1)} %constant_dynamic-slice_fusion.line_ref, f32[512,8192]{1,0:T(8,128)S(1)} %copy-done.1, bf16[784,128]{1,0:T(8,128)(2,1)S(1)} %get-tuple-element.268.refs_0_, ...), custom_call_target="tpu_custom_call" | custom-call | tf_op jit(solution)/shard_map/product_end/pallas_call | solution.py:487
  88.9 4.9 %factor.1.refs_3_ = f32[128,128]{1,0:T(8,128)S(1)} custom-call(s32[1,18]{1,0:T(1,128)S(1)} %constant_dynamic-slice_fusion.line_ref, f32[128,128]{1,0:T(8,128)S(1)} %get-tuple-element.285.gram_ref), custom_call_target="tpu_custom_call" | custom-call | tf_op jit(solution)/shard_map/factor/pallas_call | solution.py:159
  97.4 2.7 %covariance_part.11.refs_5_ = f32[512,8192]{1,0:T(8,128)} custom-call(s32[1,18]{1,0:T(1,128)S(1)} %constant_dynamic-slice_fusion.line_ref, f32[512,8192]{1,0:T(8,128)S(1)} %copy-done.1, bf16[2,512,256]{2,1,0:T(8,128)(2,1)S(1)} %get-tuple-element.157.snap_ref.refs_0_.refs_5_.refs_7_, ...), custom_call_target="tpu_custom_call", output_to_operand_aliasing={{}: (5, {})} | custom-call | tf_op jit(solution)/shard_map/covariance_part/pallas_call | solution.py:661
  100.1 5.2 %collective-permute-done.44.refs_1_ = f32[64,128]{1,0:T(8,128)S(1)} collective-permute-done((f32[64,128]{1,0:T(8,128)S(1)}, f32[64,128]{1,0:T(8,128)S(1)}, u32[]{:S(2)}, u32[]{:S(2)}) %collective-permute-start.44) | collective-permute-done | bytes 32800 | tf_op jit(solution)/shard_map/ppermute | solution.py:226
  106.0 2.7 %covariance_part.12.refs_3_ = f32[512,8192]{1,0:T(8,128)} custom-call(s32[1,18]{1,0:T(1,128)S(1)} %constant_dynamic-slice_fusion.line_ref, f32[512,8192]{1,0:T(8,128)S(1)} %copy-done.1, bf16[2,512,256]{2,1,0:T(8,128)(2,1)S(1)} %get-tuple-element.157.snap_ref.refs_0_.refs_5_.refs_7_, ...), custom_call_target="tpu_custom_call", output_to_operand_aliasing={{}: (5, {})} | custom-call | tf_op jit(solution)/shard_map/covariance_part/pallas_call | solution.py:661
  111.7 2.7 %covariance_part.13.refs_2_ = f32[512,8192]{1,0:T(8,128)} custom-call(s32[1,18]{1,0:T(1,128)S(1)} %constant_dynamic-slice_fusion.line_ref, f32[512,8192]{1,0:T(8,128)S(1)} %copy-done.1, bf16[2,512,256]{2,1,0:T(8,128)(2,1)S(1)} %get-tuple-element.157.snap_ref.refs_0_.refs_5_.refs_7_, ...), custom_call_target="tpu_custom_call", output_to_operand_aliasing={{}: (5, {})} | custom-call | tf_op jit(solution)/shard_map/covariance_part/pallas_call | solution.py:661
  117.6 5.4 %both_factors.1.factors_ref = f32[128,128]{1,0:T(8,128)S(1)} custom-call(s32[1,18]{1,0:T(1,128)S(1)} %constant_dynamic-slice_fusion.line_ref, f32[64,128]{1,0:T(8,128)S(1)} %get-tuple-element.303.gram_ref, f32[64,128]{1,0:T(8,128)S(1)} %collective-permute-done.51.theirs_ref, f32[128,128]{1,0:T(8,128)S(1)} %get-tuple-element.304.first_ref), custom_call_target="tpu_custom_call" | custom-call | tf_op jit(solution)/shard_map/both_factors/pallas_call | solution.py:613
  (141 shorter events, 52.2 us)
Async XLA Ops:
  0.6 19.1 %collective-permute-start.5 = (bf16[2,512,256]{2,1,0:T(8,128)(2,1)}, bf16[2,512,256]{2,1,0:T(8,128)(2,1)S(1)}, u32[]{:S(2)}, u32[]{:S(2)}) collective-permute-start(bf16[2,512,256]{2,1,0:T(8,128)(2,1)} %snap_ref.1), channel_id=1, source_target_pairs={{0,2},{1,5},{4,0},{5,9},{8,4},{9,13},{12,8},{13,15},{14,12},{15,11... | collective-permute-start | bytes 1572872 | tf_op jit(solution)/shard_map/ppermute | solution.py:135
  3.6 16.1 %collective-permute-start.4 = (bf16[2,512,256]{2,1,0:T(8,128)(2,1)}, bf16[2,512,256]{2,1,0:T(8,128)(2,1)S(1)}, u32[]{:S(2)}, u32[]{:S(2)}) collective-permute-start(bf16[2,512,256]{2,1,0:T(8,128)(2,1)} %snap_ref.1), channel_id=1, source_target_pairs={{0,4},{1,3},{4,8},{5,1},{8,12},{9,5},{12,14},{13,9},{14,10},{15,13... | collective-permute-start | bytes 1572872 | tf_op jit(solution)/shard_map/ppermute | solution.py:135
  9.4 10.4 %collective-permute-start.2 = (bf16[656,128]{1,0:T(8,128)(2,1)S(1)}, bf16[656,128]{1,0:T(8,128)(2,1)S(1)}, u32[]{:S(2)}, u32[]{:S(2)}) collective-permute-start(bf16[656,128]{1,0:T(8,128)(2,1)S(1)} %pack.2.event_ref.refs_0_), channel_id=1, source_target_pairs={{0,2},{1,5},{4,0},{5,9},{8,4},{9,13},{12,8},{13,15},{14,12},{15,11... | collective-permute-start | bytes 503816 | tf_op jit(solution)/shard_map/ppermute | solution.py:135
  11.3 8.4 %collective-permute-start.1 = (bf16[656,128]{1,0:T(8,128)(2,1)S(1)}, bf16[656,128]{1,0:T(8,128)(2,1)S(1)}, u32[]{:S(2)}, u32[]{:S(2)}) collective-permute-start(bf16[656,128]{1,0:T(8,128)(2,1)S(1)} %pack.2.event_ref.refs_0_), channel_id=1, source_target_pairs={{0,4},{1,3},{4,8},{5,1},{8,12},{9,5},{12,14},{13,9},{14,10},{15,13... | collective-permute-start | bytes 503816 | tf_op jit(solution)/shard_map/ppermute | solution.py:135
  11.4 8.3 %collective-permute-start.3 = (bf16[656,128]{1,0:T(8,128)(2,1)S(1)}, bf16[656,128]{1,0:T(8,128)(2,1)S(1)}, u32[]{:S(2)}, u32[]{:S(2)}) collective-permute-start(bf16[656,128]{1,0:T(8,128)(2,1)S(1)} %pack.2.event_ref.refs_0_), channel_id=1, source_target_pairs={{0,1},{1,0},{2,3},{3,2},{4,5},{5,4},{6,7},{7,6},{8,9},{9,8},{10,11... | collective-permute-start | bytes 503816 | tf_op jit(solution)/shard_map/ppermute | solution.py:119
  19.8 7.9 %collective-permute-start.10 = (bf16[2,512,256]{2,1,0:T(8,128)(2,1)S(1)}, bf16[2,512,256]{2,1,0:T(8,128)(2,1)S(1)}, u32[]{:S(2)}, u32[]{:S(2)}) collective-permute-start(bf16[2,512,256]{2,1,0:T(8,128)(2,1)S(1)} %get-tuple-element.170), channel_id=1, source_target_pairs={{0,1},{1,0},{2,3},{3,2},{4,5},{5,4},{6,7},{7,6},{8,9},{9,8},{10,11... | collective-permute-start | bytes 1572872 | tf_op jit(solution)/shard_map/ppermute | solution.py:119
  35.0 8.9 %collective-permute-start.17 = (bf16[656,128]{1,0:T(8,128)(2,1)S(1)}, bf16[656,128]{1,0:T(8,128)(2,1)S(1)}, u32[]{:S(2)}, u32[]{:S(2)}) collective-permute-start(bf16[656,128]{1,0:T(8,128)(2,1)S(1)} %get-tuple-element.189.refs_0_), channel_id=1, source_target_pairs={{0,4},{1,3},{4,8},{5,1},{8,12},{9,5},{12,14},{13,9},{14,10},{15,13... | collective-permute-start | bytes 503816 | tf_op jit(solution)/shard_map/ppermute | solution.py:135
  36.6 7.3 %collective-permute-start.19 = (bf16[656,128]{1,0:T(8,128)(2,1)S(1)}, bf16[656,128]{1,0:T(8,128)(2,1)S(1)}, u32[]{:S(2)}, u32[]{:S(2)}) collective-permute-start(bf16[656,128]{1,0:T(8,128)(2,1)S(1)} %get-tuple-element.195.refs_2_), channel_id=1, source_target_pairs={{0,1},{1,0},{2,3},{3,2},{4,5},{5,4},{6,7},{7,6},{8,9},{9,8},{10,11... | collective-permute-start | bytes 503816 | tf_op jit(solution)/shard_map/ppermute | solution.py:119
  36.6 7.3 %collective-permute-start.18 = (bf16[656,128]{1,0:T(8,128)(2,1)S(1)}, bf16[656,128]{1,0:T(8,128)(2,1)S(1)}, u32[]{:S(2)}, u32[]{:S(2)}) collective-permute-start(bf16[656,128]{1,0:T(8,128)(2,1)S(1)} %get-tuple-element.189.refs_0_), channel_id=1, source_target_pairs={{0,1},{1,0},{2,3},{3,2},{4,5},{5,4},{6,7},{7,6},{8,9},{9,8},{10,11... | collective-permute-start | bytes 503816 | tf_op jit(solution)/shard_map/ppermute | solution.py:119
  37.2 14.5 %collective-permute-start.15 = (bf16[2,512,256]{2,1,0:T(8,128)(2,1)S(1)}, bf16[2,512,256]{2,1,0:T(8,128)(2,1)S(1)}, u32[]{:S(2)}, u32[]{:S(2)}) collective-permute-start(bf16[2,512,256]{2,1,0:T(8,128)(2,1)S(1)} %get-tuple-element.187.refs_0_), channel_id=1, source_target_pairs={{0,4},{1,3},{4,8},{5,1},{8,12},{9,5},{12,14},{13,9},{14,10},{15,13... | collective-permute-start | bytes 1572872 | tf_op jit(solution)/shard_map/ppermute | solution.py:135
  38.8 12.9 %collective-permute-start.16 = (bf16[2,512,256]{2,1,0:T(8,128)(2,1)S(1)}, bf16[2,512,256]{2,1,0:T(8,128)(2,1)S(1)}, u32[]{:S(2)}, u32[]{:S(2)}) collective-permute-start(bf16[2,512,256]{2,1,0:T(8,128)(2,1)S(1)} %get-tuple-element.188.refs_1_), channel_id=1, source_target_pairs={{0,2},{1,5},{4,0},{5,9},{8,4},{9,13},{12,8},{13,15},{14,12},{15,11... | collective-permute-start | bytes 1572872 | tf_op jit(solution)/shard_map/ppermute | solution.py:135
  44.0 7.7 %collective-permute-start.20 = (bf16[2,512,256]{2,1,0:T(8,128)(2,1)S(1)}, bf16[2,512,256]{2,1,0:T(8,128)(2,1)S(1)}, u32[]{:S(2)}, u32[]{:S(2)}) collective-permute-start(bf16[2,512,256]{2,1,0:T(8,128)(2,1)S(1)} %get-tuple-element.202), channel_id=1, source_target_pairs={{0,1},{1,0},{2,3},{3,2},{4,5},{5,4},{6,7},{7,6},{8,9},{9,8},{10,11... | collective-permute-start | bytes 1572872 | tf_op jit(solution)/shard_map/ppermute | solution.py:119
  44.0 7.6 %collective-permute-start.21 = (bf16[2,512,256]{2,1,0:T(8,128)(2,1)S(1)}, bf16[2,512,256]{2,1,0:T(8,128)(2,1)S(1)}, u32[]{:S(2)}, u32[]{:S(2)}) collective-permute-start(bf16[2,512,256]{2,1,0:T(8,128)(2,1)S(1)} %get-tuple-element.203), channel_id=1, source_target_pairs={{0,1},{1,0},{2,3},{3,2},{4,5},{5,4},{6,7},{7,6},{8,9},{9,8},{10,11... | collective-permute-start | bytes 1572872 | tf_op jit(solution)/shard_map/ppermute | solution.py:119
  52.5 8.1 %collective-permute-start.27 = (bf16[2,512,256]{2,1,0:T(8,128)(2,1)S(1)}, bf16[2,512,256]{2,1,0:T(8,128)(2,1)S(1)}, u32[]{:S(2)}, u32[]{:S(2)}) collective-permute-start(bf16[2,512,256]{2,1,0:T(8,128)(2,1)S(1)} %get-tuple-element.220.refs_2_.refs_3_), channel_id=1, source_target_pairs={{0,1},{1,0},{2,3},{3,2},{4,5},{5,4},{6,7},{7,6},{8,9},{9,8},{10,11... | collective-permute-start | bytes 1572872 | tf_op jit(solution)/shard_map/ppermute | solution.py:119
  52.5 8.1 %collective-permute-start.28 = (bf16[2,512,256]{2,1,0:T(8,128)(2,1)S(1)}, bf16[2,512,256]{2,1,0:T(8,128)(2,1)S(1)}, u32[]{:S(2)}, u32[]{:S(2)}) collective-permute-start(bf16[2,512,256]{2,1,0:T(8,128)(2,1)S(1)} %get-tuple-element.221.refs_3_.refs_4_), channel_id=1, source_target_pairs={{0,1},{1,0},{2,3},{3,2},{4,5},{5,4},{6,7},{7,6},{8,9},{9,8},{10,11... | collective-permute-start | bytes 1572872 | tf_op jit(solution)/shard_map/ppermute | solution.py:119
  53.0 7.6 %collective-permute-start.25 = (bf16[784,128]{1,0:T(8,128)(2,1)S(1)}, bf16[784,128]{1,0:T(8,128)(2,1)S(1)}, u32[]{:S(2)}, u32[]{:S(2)}) collective-permute-start(bf16[784,128]{1,0:T(8,128)(2,1)S(1)} %pack.3.refs_2_.refs_0_), channel_id=1, source_target_pairs={{0,2},{1,5},{4,0},{5,9},{8,4},{9,13},{12,8},{13,15},{14,12},{15,11... | collective-permute-start | bytes 602120 | tf_op jit(solution)/shard_map/ppermute | solution.py:135
  60.6 7.6 %collective-permute-start.29 = (bf16[784,128]{1,0:T(8,128)(2,1)S(1)}, bf16[784,128]{1,0:T(8,128)(2,1)S(1)}, u32[]{:S(2)}, u32[]{:S(2)}) collective-permute-start(bf16[784,128]{1,0:T(8,128)(2,1)S(1)} %get-tuple-element.225.refs_0_), channel_id=1, source_target_pairs={{0,4},{1,3},{4,8},{5,1},{8,12},{9,5},{12,14},{13,9},{14,10},{15,13... | collective-permute-start | bytes 602120 | tf_op jit(solution)/shard_map/ppermute | solution.py:135
  68.3 7.3 %collective-permute-start.33 = (bf16[784,128]{1,0:T(8,128)(2,1)S(1)}, bf16[784,128]{1,0:T(8,128)(2,1)S(1)}, u32[]{:S(2)}, u32[]{:S(2)}) collective-permute-start(bf16[784,128]{1,0:T(8,128)(2,1)S(1)} %get-tuple-element.238.refs_0_), channel_id=1, source_target_pairs={{0,4},{1,3},{4,8},{5,1},{8,12},{9,5},{12,14},{13,9},{14,10},{15,13... | collective-permute-start | bytes 602120 | tf_op jit(solution)/shard_map/ppermute | solution.py:135
  81.4 13.4 %collective-permute-start.42 = (bf16[2,512,256]{2,1,0:T(8,128)(2,1)S(1)}, bf16[2,512,256]{2,1,0:T(8,128)(2,1)S(1)}, u32[]{:S(2)}, u32[]{:S(2)}) collective-permute-start(bf16[2,512,256]{2,1,0:T(8,128)(2,1)S(1)} %get-tuple-element.283), channel_id=1, source_target_pairs={{0,4},{1,3},{4,8},{5,1},{8,12},{9,5},{12,14},{13,9},{14,10},{15,13... | collective-permute-start | bytes 1572872 | tf_op jit(solution)/shard_map/ppermute | solution.py:135
  82.7 12.1 %collective-permute-start.43 = (bf16[2,512,256]{2,1,0:T(8,128)(2,1)S(1)}, bf16[2,512,256]{2,1,0:T(8,128)(2,1)S(1)}, u32[]{:S(2)}, u32[]{:S(2)}) collective-permute-start(bf16[2,512,256]{2,1,0:T(8,128)(2,1)S(1)} %get-tuple-element.284), channel_id=1, source_target_pairs={{0,2},{1,5},{4,0},{5,9},{8,4},{9,13},{12,8},{13,15},{14,12},{15,11... | collective-permute-start | bytes 1572872 | tf_op jit(solution)/shard_map/ppermute | solution.py:135
  94.9 11.0 %collective-permute-start.47 = (bf16[2,512,256]{2,1,0:T(8,128)(2,1)S(1)}, bf16[2,512,256]{2,1,0:T(8,128)(2,1)S(1)}, u32[]{:S(2)}, u32[]{:S(2)}) collective-permute-start(bf16[2,512,256]{2,1,0:T(8,128)(2,1)S(1)} %get-tuple-element.289.refs_1_), channel_id=1, source_target_pairs={{0,1},{1,0},{2,3},{3,2},{4,5},{5,4},{6,7},{7,6},{8,9},{9,8},{10,11... | collective-permute-start | bytes 1572872 | tf_op jit(solution)/shard_map/ppermute | solution.py:119
  94.9 11.0 %collective-permute-start.46 = (bf16[2,512,256]{2,1,0:T(8,128)(2,1)S(1)}, bf16[2,512,256]{2,1,0:T(8,128)(2,1)S(1)}, u32[]{:S(2)}, u32[]{:S(2)}) collective-permute-start(bf16[2,512,256]{2,1,0:T(8,128)(2,1)S(1)} %get-tuple-element.288.refs_0_), channel_id=1, source_target_pairs={{0,1},{1,0},{2,3},{3,2},{4,5},{5,4},{6,7},{7,6},{8,9},{9,8},{10,11... | collective-permute-start | bytes 1572872 | tf_op jit(solution)/shard_map/ppermute | solution.py:119
  95.4 10.5 %collective-permute-start.45 = (bf16[2,512,256]{2,1,0:T(8,128)(2,1)S(1)}, bf16[2,512,256]{2,1,0:T(8,128)(2,1)S(1)}, u32[]{:S(2)}, u32[]{:S(2)}) collective-permute-start(bf16[2,512,256]{2,1,0:T(8,128)(2,1)S(1)} %get-tuple-element.288.refs_0_), channel_id=1, source_target_pairs={{0,4},{1,3},{4,8},{5,1},{8,12},{9,5},{12,14},{13,9},{14,10},{15,13... | collective-permute-start | bytes 1572872 | tf_op jit(solution)/shard_map/ppermute | solution.py:135
  96.3 8.9 %collective-permute-start.44 = (f32[64,128]{1,0:T(8,128)S(1)}, f32[64,128]{1,0:T(8,128)S(1)}, u32[]{:S(2)}, u32[]{:S(2)}) collective-permute-start(f32[64,128]{1,0:T(8,128)S(1)} %get-tuple-element.287.refs_0_), channel_id=1, source_target_pairs={{0,2},{1,3},{2,0},{3,1},{4,6},{5,7},{6,4},{7,5},{8,10},{9,11},{10,... | collective-permute-start | bytes 98312 | tf_op jit(solution)/shard_map/ppermute | solution.py:226
  (32 other events, 149.0 us)

commit v5 on v4

--- a/solution.py
+++ b/solution.py
@@ -225,7 +225,7 @@
     def pass_on(self, value, mask):
         return lax.ppermute(value, "row", partner_pairs(self.devices, mask))
 
-    def round(self, count=1):
+    def round(self, count=1, event=None):
         for _ in range(count):
             if not self.rounds:
                 return
@@ -245,7 +245,10 @@
             elif kind == "last":
                 self.mine = join_halves(line, core_bit, self.mine, self.pass_on(self.mine, 1))
             else:
-                self.mine = add_all(line, [self.mine, self.pass_on(self.mine, kind)])
+                got = self.pass_on(self.mine, kind)
+                if event is not None:
+                    (got,) = gate([got], [event])
+                self.mine = add_all(line, [self.mine, got])
 
     def held(self):
         return [self.mine] if self.theirs is None else [self.mine, self.theirs]
@@ -802,7 +805,7 @@
     applied, mine, theirs, first_gram = result
     total = Total(line, bits, mine, theirs, devices, False)
     total.rounds.pop()
-    total.round()
+    total.round(2)
     first = factor(line, first_gram)
     while snap_ring.done < steps - 1:
         (first,) = gate_all([total, snap_ring], [first])
@@ -812,18 +815,18 @@
 
     snap_ring.step()
     snap_ring.pass_on_full()
-    total.round()
     if end > 16:
         new_cov = fill(new_cov, range(10, end - 6))
     new_cov = fill(new_cov, [end - 6, end - 4])
+    blocks = [b for group in snap_ring.groups for b in group]
+    new_cov, copies = fill_own(new_cov, [blocks[end - 5], blocks[end - 3]], [end - 5, end - 3])
+    total.round(event=copies[0])
     (first, new_cov) = gate_all([total, snap_ring], [first, new_cov])
     snap_ring.pass_on()
-    total.round()
-    new_cov = fill(new_cov, [end - 5, end - 3])
-    (first, new_cov) = gate_all([total, snap_ring], [first, new_cov])
+    blocks = [b for group in snap_ring.groups for b in group]
+    new_cov, copies = fill_own(new_cov, blocks[end - 2 : end], [end - 2, end - 1])
     while total.rounds:
-        total.round()
-    new_cov = fill(new_cov, [end - 2, end - 1])
+        total.round(event=copies[0])
     (first, new_cov) = gate_all([total], [first, new_cov])
     theirs = lax.ppermute(total.mine, "row", swap)
     factors = both_factors(line, bits, total.mine, theirs, first)

time: 125 us -> 122 us (0.976)
  waiting for transfers between devices: 24.1 us -> 16.7 us
  starting transfers between devices: 32.1 us -> 35 us
  Pallas kernels: 58.5 us -> 60.4 us
    ppermute x4, waiting for transfers between devices: 7.8 us -> 0.87 us  [pass_on(): return lax.ppermute(value, 'row', partner_pairs(self.devices, mask))]
    ppermute x4, starting transfers between devices: 2.89 us -> 5.55 us  [pass_on(): return lax.ppermute(value, 'row', partner_pairs(self.devices, mask))]
    pallas_call x7, Pallas kernels: 20.3 us -> 22.2 us  [covariance_part(): pl.pallas_call(kernel, out_shape=(f32(*prior_cov.shape),) + tuple((jax.Sh...]
  transfers between devices with their start and end apart: 52 -> 52, of which waited for: 15 -> 12; matrix products, arithmetic and copies ran while one was open for 1% -> 1% of each run, Pallas kernels for 40% -> 43%
where the time goes in v5:
time: 122 us
  Pallas kernels  60.4 us (50%)
  starting transfers between devices  35 us (29%)
  waiting for transfers between devices  16.7 us (14%)
  local copies, waits for them, and re-layouts  8.57 us (7%)
    pallas_call x17, Pallas kernels, small_kernel(): pl.pallas_call(kernel, out_shape=out_shape, in_specs=[in_smem] + [in_vmem...  26.9 us
    ppermute x21, starting transfers between devices, step(): lax.ppermute(b, 'row', pairs)  23.8 us
    pallas_call x7, Pallas kernels, covariance_part(): pl.pallas_call(kernel, out_shape=(f32(*prior_cov.shape),) + tuple((jax.Sh...  22.2 us
    ppermute x21, waiting for transfers between devices, step(): lax.ppermute(b, 'row', pairs)  12.9 us
    unnamed x8, local copies, waits for them, and re-layouts  7.88 us
    ppermute x4, starting transfers between devices, pass_on(): return lax.ppermute(value, 'row', partner_pairs(self.devices, mask))  5.55 us
    pallas_call x1, Pallas kernels, both_factors(): pl.pallas_call(kernel, out_shape=f32(rank, rank), in_specs=[in_smem] + [i...  5.4 us
    ppermute x24, starting transfers between devices, pass_on(): group += [block, lax.ppermute(copy, 'row', self.swap)]  5.35 us
  transfers between devices with their start and end apart: 52, of which 12 were waited for; matrix products, arithmetic and copies ran while one was open for 1% of the time, Pallas kernels for 43%

profile of v5, /device:TPU:0, one launch (start us, length us, event | category | flops | bytes accessed | tf_op | source)
XLA Modules:
  0.0 121.9 jit_solution(8068787772039982406)
XLA Ops:
  0.6 3.0 %collective-permute-start.5 = (bf16[2,512,256]{2,1,0:T(8,128)(2,1)}, bf16[2,512,256]{2,1,0:T(8,128)(2,1)S(1)}, u32[]{:S(2)}, u32[]{:S(2)}) collective-permute-start(bf16[2,512,256]{2,1,0:T(8,128)(2,1)} %snap_ref.1), channel_id=1, source_target_pairs={{0,2},{1,5},{4,0},{5,9},{8,4},{9,13},{12,8},{13,15},{14,12},{15,11... | collective-permute-start | bytes 1572872 | tf_op jit(solution)/shard_map/ppermute | solution.py:135
  9.4 2.0 %collective-permute-start.2 = (bf16[656,128]{1,0:T(8,128)(2,1)S(1)}, bf16[656,128]{1,0:T(8,128)(2,1)S(1)}, u32[]{:S(2)}, u32[]{:S(2)}) collective-permute-start(bf16[656,128]{1,0:T(8,128)(2,1)S(1)} %pack.2.event_ref.refs_0_), channel_id=1, source_target_pairs={{0,2},{1,5},{4,0},{5,9},{8,4},{9,13},{12,8},{13,15},{14,12},{15,11... | collective-permute-start | bytes 503816 | tf_op jit(solution)/shard_map/ppermute | solution.py:135
  11.5 5.8 %copy-done = f32[512,8192]{1,0:T(8,128)S(1)} copy-done((f32[512,8192]{1,0:T(8,128)S(1)}, f32[512,8192]{1,0:T(8,128)}, u32[]{:S(2)}) %copy-start) | copy-done | bytes 16777240
  20.2 2.1 %collective-permute-start.6 = (bf16[656,128]{1,0:T(8,128)(2,1)S(1)}, bf16[656,128]{1,0:T(8,128)(2,1)S(1)}, u32[]{:S(2)}, u32[]{:S(2)}) collective-permute-start(bf16[656,128]{1,0:T(8,128)(2,1)S(1)} %get-tuple-element.162.refs_0_), channel_id=1, source_target_pairs={{0,4},{1,3},{4,8},{5,1},{8,12},{9,5},{12,14},{13,9},{14,10},{15,13... | collective-permute-start | bytes 503816 | tf_op jit(solution)/shard_map/ppermute | solution.py:135
  24.3 2.8 %collective-permute-done.6.refs_0_ = bf16[656,128]{1,0:T(8,128)(2,1)S(1)} collective-permute-done((bf16[656,128]{1,0:T(8,128)(2,1)S(1)}, bf16[656,128]{1,0:T(8,128)(2,1)S(1)}, u32[]{:S(2)}, u32[]{:S(2)}) %collective-permute-start.6) | collective-permute-done | bytes 167968 | tf_op jit(solution)/shard_map/ppermute | solution.py:135
  30.4 2.7 %covariance_part.7.refs_7_ = f32[512,8192]{1,0:T(8,128)} custom-call(s32[1,18]{1,0:T(1,128)S(1)} %constant_dynamic-slice_fusion.line_ref, f32[512,8192]{1,0:T(8,128)S(1)} %copy-done.1, bf16[2,512,256]{2,1,0:T(8,128)(2,1)S(1)} %get-tuple-element.155.snap_ref.refs_0_.refs_5_.refs_7_, ...), custom_call_target="tpu_custom_call" | custom-call | tf_op jit(solution)/shard_map/covariance_part/pallas_call | solution.py:664
  33.0 1.9 %product_part.9 = (f32[512,128]{1,0:T(8,128)S(1)}, f32[128,128]{1,0:T(8,128)S(1)}, f32[128,128]{1,0:T(8,128)S(1)}) custom-call(s32[1,18]{1,0:T(1,128)S(1)} %constant_dynamic-slice_fusion.line_ref, f32[512,8192]{1,0:T(8,128)S(1)} %copy-done.1, bf16[656,128]{1,0:T(8,128)(2,1)S(1)} %get-tuple-element.162.refs_0_, ...), custom_call_target="tpu_custom_call" | custom-call | tf_op jit(solution)/shard_map/product_part/pallas_call | solution.py:159
  39.2 2.8 %covariance_part.8 = (f32[512,8192]{1,0:T(8,128)}, bf16[2,512,256]{2,1,0:T(8,128)(2,1)S(1)}, bf16[2,512,256]{2,1,0:T(8,128)(2,1)S(1)}) custom-call(s32[1,18]{1,0:T(1,128)S(1)} %constant_dynamic-slice_fusion.line_ref, f32[512,8192]{1,0:T(8,128)S(1)} %copy-done.1, ...), custom_call_target="tpu_custom_call", output_to_operand_aliasing={{0}: (5, {})} | custom-call | tf_op jit(solution)/shard_map/covariance_part/pallas_call | solution.py:664
  42.0 1.9 %product_part.10 = (f32[512,128]{1,0:T(8,128)S(1)}, f32[128,128]{1,0:T(8,128)S(1)}, f32[128,128]{1,0:T(8,128)S(1)}) custom-call(s32[1,18]{1,0:T(1,128)S(1)} %constant_dynamic-slice_fusion.line_ref, f32[512,8192]{1,0:T(8,128)S(1)} %copy-done.1, bf16[656,128]{1,0:T(8,128)(2,1)S(1)} %get-tuple-element.171.refs_0_, ...), custom_call_target="tpu_custom_call" | custom-call | tf_op jit(solution)/shard_map/product_part/pallas_call | solution.py:159
  44.6 1.9 %product_part.11 = (f32[512,128]{1,0:T(8,128)S(1)}, f32[128,128]{1,0:T(8,128)S(1)}, f32[128,128]{1,0:T(8,128)S(1)}) custom-call(s32[1,18]{1,0:T(1,128)S(1)} %constant_dynamic-slice_fusion.line_ref, f32[512,8192]{1,0:T(8,128)S(1)} %copy-done.1, bf16[656,128]{1,0:T(8,128)(2,1)S(1)} %get-tuple-element.187.refs_0_, ...), custom_call_target="tpu_custom_call" | custom-call | tf_op jit(solution)/shard_map/product_part/pallas_call | solution.py:159
  49.8 1.9 %collective-permute-done.15.refs_0_ = bf16[2,512,256]{2,1,0:T(8,128)(2,1)S(1)} collective-permute-done((bf16[2,512,256]{2,1,0:T(8,128)(2,1)S(1)}, bf16[2,512,256]{2,1,0:T(8,128)(2,1)S(1)}, u32[]{:S(2)}, u32[]{:S(2)}) %collective-permute-start.15) | collective-permute-done | bytes 524320 | tf_op jit(solution)/shard_map/ppermute | solution.py:135
  55.1 4.2 %covariance_part.9.refs_5_ = f32[512,8192]{1,0:T(8,128)} custom-call(s32[1,18]{1,0:T(1,128)S(1)} %constant_dynamic-slice_fusion.line_ref, f32[512,8192]{1,0:T(8,128)S(1)} %copy-done.1, bf16[2,512,256]{2,1,0:T(8,128)(2,1)S(1)} %get-tuple-element.155.snap_ref.refs_0_.refs_5_.refs_7_, ...), custom_call_target="tpu_custom_call", output_to_operand_aliasing={{}: (7, {})} | custom-call | tf_op jit(solution)/shard_map/covariance_part/pallas_call | solution.py:664
  64.9 2.7 %covariance_part.10.refs_9_ = f32[512,8192]{1,0:T(8,128)} custom-call(s32[1,18]{1,0:T(1,128)S(1)} %constant_dynamic-slice_fusion.line_ref, f32[512,8192]{1,0:T(8,128)S(1)} %copy-done.1, bf16[2,512,256]{2,1,0:T(8,128)(2,1)S(1)} %get-tuple-element.155.snap_ref.refs_0_.refs_5_.refs_7_, ...), custom_call_target="tpu_custom_call", output_to_operand_aliasing={{}: (5, {})} | custom-call | tf_op jit(solution)/shard_map/covariance_part/pallas_call | solution.py:664
  70.9 2.5 %product_part.13 = (f32[512,128]{1,0:T(8,128)S(1)}, f32[256,128]{1,0:T(8,128)S(1)}, f32[256,128]{1,0:T(8,128)S(1)}, f32[128,128]{1,0:T(8,128)S(1)}, f32[1,128]{1,0:T(1,128)S(1)}) custom-call(s32[1,18]{1,0:T(1,128)S(1)} %constant_dynamic-slice_fusion.line_ref, f32[512,8192]{1,0:T(8,128)S(1)} %copy-done.1, bf16[784,128]{1,0:T(8,128)(2,1)S(1)} %get-tuple-element.223.refs_0_, ...), custom_call_target="tpu_custom_call" | custom-call | tf_op jit(solution)/shard_map/product_part/pallas_call | solution.py:159
  73.4 2.3 %collective-permute-done.33.refs_0_ = bf16[784,128]{1,0:T(8,128)(2,1)S(1)} collective-permute-done((bf16[784,128]{1,0:T(8,128)(2,1)S(1)}, bf16[784,128]{1,0:T(8,128)(2,1)S(1)}, u32[]{:S(2)}, u32[]{:S(2)}) %collective-permute-start.33) | collective-permute-done | bytes 200736 | tf_op jit(solution)/shard_map/ppermute | solution.py:135
  77.4 2.5 %product_part.14 = (f32[512,128]{1,0:T(8,128)S(1)}, f32[256,128]{1,0:T(8,128)S(1)}, f32[256,128]{1,0:T(8,128)S(1)}, f32[128,128]{1,0:T(8,128)S(1)}, f32[1,128]{1,0:T(1,128)S(1)}) custom-call(s32[1,18]{1,0:T(1,128)S(1)} %constant_dynamic-slice_fusion.line_ref, f32[512,8192]{1,0:T(8,128)S(1)} %copy-done.1, bf16[784,128]{1,0:T(8,128)(2,1)S(1)} %get-tuple-element.236.refs_0_, ...), custom_call_target="tpu_custom_call" | custom-call | tf_op jit(solution)/shard_map/product_part/pallas_call | solution.py:159
  83.5 2.5 %product_part.15 = (f32[512,128]{1,0:T(8,128)S(1)}, f32[256,128]{1,0:T(8,128)S(1)}, f32[256,128]{1,0:T(8,128)S(1)}, f32[128,128]{1,0:T(8,128)S(1)}, f32[1,128]{1,0:T(1,128)S(1)}) custom-call(s32[1,18]{1,0:T(1,128)S(1)} %constant_dynamic-slice_fusion.line_ref, f32[512,8192]{1,0:T(8,128)S(1)} %copy-done.1, bf16[784,128]{1,0:T(8,128)(2,1)S(1)} %get-tuple-element.252.refs_0_, ...), custom_call_target="tpu_custom_call" | custom-call | tf_op jit(solution)/shard_map/product_part/pallas_call | solution.py:159
  86.0 2.3 %product_end.3 = (f32[512,128]{1,0:T(8,128)S(1)}, f32[64,128]{1,0:T(8,128)S(1)}, f32[64,128]{1,0:T(8,128)S(1)}, f32[128,128]{1,0:T(8,128)S(1)}) custom-call(s32[1,18]{1,0:T(1,128)S(1)} %constant_dynamic-slice_fusion.line_ref, f32[512,8192]{1,0:T(8,128)S(1)} %copy-done.1, bf16[784,128]{1,0:T(8,128)(2,1)S(1)} %get-tuple-element.266.refs_0_, ...), custom_call_target="tpu_custom_call" | custom-call | tf_op jit(solution)/shard_map/product_end/pallas_call | solution.py:490
  91.3 4.9 %factor.1.refs_3_ = f32[128,128]{1,0:T(8,128)S(1)} custom-call(s32[1,18]{1,0:T(1,128)S(1)} %constant_dynamic-slice_fusion.line_ref, f32[128,128]{1,0:T(8,128)S(1)} %get-tuple-element.283.gram_ref), custom_call_target="tpu_custom_call" | custom-call | tf_op jit(solution)/shard_map/factor/pallas_call | solution.py:159
  100.3 2.7 %covariance_part.11.refs_2_ = f32[512,8192]{1,0:T(8,128)} custom-call(s32[1,18]{1,0:T(1,128)S(1)} %constant_dynamic-slice_fusion.line_ref, f32[512,8192]{1,0:T(8,128)S(1)} %copy-done.1, bf16[2,512,256]{2,1,0:T(8,128)(2,1)S(1)} %get-tuple-element.155.snap_ref.refs_0_.refs_5_.refs_7_, ...), custom_call_target="tpu_custom_call", output_to_operand_aliasing={{}: (5, {})} | custom-call | tf_op jit(solution)/shard_map/covariance_part/pallas_call | solution.py:664
  103.0 3.6 %covariance_part.12 = (f32[512,8192]{1,0:T(8,128)}, bf16[2,512,256]{2,1,0:T(8,128)(2,1)S(1)}, bf16[2,512,256]{2,1,0:T(8,128)(2,1)}) custom-call(s32[1,18]{1,0:T(1,128)S(1)} %constant_dynamic-slice_fusion.line_ref, f32[512,8192]{1,0:T(8,128)S(1)} %copy-done.1, ...), custom_call_target="tpu_custom_call", output_to_operand_aliasing={{0}: (5, {})} | custom-call | tf_op jit(solution)/shard_map/covariance_part/pallas_call | solution.py:664
  107.3 2.2 %collective-permute-start.49 = (f32[64,128]{1,0:T(8,128)S(1)}, f32[64,128]{1,0:T(8,128)S(1)}, u32[]{:S(2)}, u32[]{:S(2)}) collective-permute-start(f32[64,128]{1,0:T(8,128)S(1)} %get-tuple-element.292.refs_0_), channel_id=1, source_target_pairs={{0,8},{1,9},{2,10},{3,11},{4,12},{5,13},{6,14},{7,15},{8,0},{9,1},... | collective-permute-start | bytes 98312 | tf_op jit(solution)/shard_map/ppermute | solution.py:226
  109.5 3.6 %covariance_part.13 = (f32[512,8192]{1,0:T(8,128)}, bf16[2,512,256]{2,1,0:T(8,128)(2,1)S(1)}, bf16[2,512,256]{2,1,0:T(8,128)(2,1)}) custom-call(s32[1,18]{1,0:T(1,128)S(1)} %constant_dynamic-slice_fusion.line_ref, f32[512,8192]{1,0:T(8,128)S(1)} %copy-done.1, ...), custom_call_target="tpu_custom_call", output_to_operand_aliasing={{0}: (5, {})} | custom-call | tf_op jit(solution)/shard_map/covariance_part/pallas_call | solution.py:664
  114.9 5.4 %both_factors.1.factors_ref = f32[128,128]{1,0:T(8,128)S(1)} custom-call(s32[1,18]{1,0:T(1,128)S(1)} %constant_dynamic-slice_fusion.line_ref, f32[64,128]{1,0:T(8,128)S(1)} %get-tuple-element.299.gram_ref, f32[64,128]{1,0:T(8,128)S(1)} %collective-permute-done.51.theirs_ref, f32[128,128]{1,0:T(8,128)S(1)} %get-tuple-element.300.first_ref), custom_call_target="tpu_custom_call" | custom-call | tf_op jit(solution)/shard_map/both_factors/pallas_call | solution.py:616
  (142 shorter events, 50.7 us)
Async XLA Ops:
  0.6 19.1 %collective-permute-start.5 = (bf16[2,512,256]{2,1,0:T(8,128)(2,1)}, bf16[2,512,256]{2,1,0:T(8,128)(2,1)S(1)}, u32[]{:S(2)}, u32[]{:S(2)}) collective-permute-start(bf16[2,512,256]{2,1,0:T(8,128)(2,1)} %snap_ref.1), channel_id=1, source_target_pairs={{0,2},{1,5},{4,0},{5,9},{8,4},{9,13},{12,8},{13,15},{14,12},{15,11... | collective-permute-start | bytes 1572872 | tf_op jit(solution)/shard_map/ppermute | solution.py:135
  3.6 16.1 %collective-permute-start.4 = (bf16[2,512,256]{2,1,0:T(8,128)(2,1)}, bf16[2,512,256]{2,1,0:T(8,128)(2,1)S(1)}, u32[]{:S(2)}, u32[]{:S(2)}) collective-permute-start(bf16[2,512,256]{2,1,0:T(8,128)(2,1)} %snap_ref.1), channel_id=1, source_target_pairs={{0,4},{1,3},{4,8},{5,1},{8,12},{9,5},{12,14},{13,9},{14,10},{15,13... | collective-permute-start | bytes 1572872 | tf_op jit(solution)/shard_map/ppermute | solution.py:135
  9.4 10.4 %collective-permute-start.2 = (bf16[656,128]{1,0:T(8,128)(2,1)S(1)}, bf16[656,128]{1,0:T(8,128)(2,1)S(1)}, u32[]{:S(2)}, u32[]{:S(2)}) collective-permute-start(bf16[656,128]{1,0:T(8,128)(2,1)S(1)} %pack.2.event_ref.refs_0_), channel_id=1, source_target_pairs={{0,2},{1,5},{4,0},{5,9},{8,4},{9,13},{12,8},{13,15},{14,12},{15,11... | collective-permute-start | bytes 503816 | tf_op jit(solution)/shard_map/ppermute | solution.py:135
  11.3 8.4 %collective-permute-start.1 = (bf16[656,128]{1,0:T(8,128)(2,1)S(1)}, bf16[656,128]{1,0:T(8,128)(2,1)S(1)}, u32[]{:S(2)}, u32[]{:S(2)}) collective-permute-start(bf16[656,128]{1,0:T(8,128)(2,1)S(1)} %pack.2.event_ref.refs_0_), channel_id=1, source_target_pairs={{0,4},{1,3},{4,8},{5,1},{8,12},{9,5},{12,14},{13,9},{14,10},{15,13... | collective-permute-start | bytes 503816 | tf_op jit(solution)/shard_map/ppermute | solution.py:135
  11.4 8.3 %collective-permute-start.3 = (bf16[656,128]{1,0:T(8,128)(2,1)S(1)}, bf16[656,128]{1,0:T(8,128)(2,1)S(1)}, u32[]{:S(2)}, u32[]{:S(2)}) collective-permute-start(bf16[656,128]{1,0:T(8,128)(2,1)S(1)} %pack.2.event_ref.refs_0_), channel_id=1, source_target_pairs={{0,1},{1,0},{2,3},{3,2},{4,5},{5,4},{6,7},{7,6},{8,9},{9,8},{10,11... | collective-permute-start | bytes 503816 | tf_op jit(solution)/shard_map/ppermute | solution.py:119
  19.8 7.9 %collective-permute-start.10 = (bf16[2,512,256]{2,1,0:T(8,128)(2,1)S(1)}, bf16[2,512,256]{2,1,0:T(8,128)(2,1)S(1)}, u32[]{:S(2)}, u32[]{:S(2)}) collective-permute-start(bf16[2,512,256]{2,1,0:T(8,128)(2,1)S(1)} %get-tuple-element.168), channel_id=1, source_target_pairs={{0,1},{1,0},{2,3},{3,2},{4,5},{5,4},{6,7},{7,6},{8,9},{9,8},{10,11... | collective-permute-start | bytes 1572872 | tf_op jit(solution)/shard_map/ppermute | solution.py:119
  20.2 6.9 %collective-permute-start.6 = (bf16[656,128]{1,0:T(8,128)(2,1)S(1)}, bf16[656,128]{1,0:T(8,128)(2,1)S(1)}, u32[]{:S(2)}, u32[]{:S(2)}) collective-permute-start(bf16[656,128]{1,0:T(8,128)(2,1)S(1)} %get-tuple-element.162.refs_0_), channel_id=1, source_target_pairs={{0,4},{1,3},{4,8},{5,1},{8,12},{9,5},{12,14},{13,9},{14,10},{15,13... | collective-permute-start | bytes 503816 | tf_op jit(solution)/shard_map/ppermute | solution.py:135
  27.7 7.2 %collective-permute-start.11 = (bf16[656,128]{1,0:T(8,128)(2,1)S(1)}, bf16[656,128]{1,0:T(8,128)(2,1)S(1)}, u32[]{:S(2)}, u32[]{:S(2)}) collective-permute-start(bf16[656,128]{1,0:T(8,128)(2,1)S(1)} %get-tuple-element.171.refs_0_), channel_id=1, source_target_pairs={{0,4},{1,3},{4,8},{5,1},{8,12},{9,5},{12,14},{13,9},{14,10},{15,13... | collective-permute-start | bytes 503816 | tf_op jit(solution)/shard_map/ppermute | solution.py:135
  35.0 8.9 %collective-permute-start.17 = (bf16[656,128]{1,0:T(8,128)(2,1)S(1)}, bf16[656,128]{1,0:T(8,128)(2,1)S(1)}, u32[]{:S(2)}, u32[]{:S(2)}) collective-permute-start(bf16[656,128]{1,0:T(8,128)(2,1)S(1)} %get-tuple-element.187.refs_0_), channel_id=1, source_target_pairs={{0,4},{1,3},{4,8},{5,1},{8,12},{9,5},{12,14},{13,9},{14,10},{15,13... | collective-permute-start | bytes 503816 | tf_op jit(solution)/shard_map/ppermute | solution.py:135
  36.6 7.3 %collective-permute-start.19 = (bf16[656,128]{1,0:T(8,128)(2,1)S(1)}, bf16[656,128]{1,0:T(8,128)(2,1)S(1)}, u32[]{:S(2)}, u32[]{:S(2)}) collective-permute-start(bf16[656,128]{1,0:T(8,128)(2,1)S(1)} %get-tuple-element.193.refs_2_), channel_id=1, source_target_pairs={{0,1},{1,0},{2,3},{3,2},{4,5},{5,4},{6,7},{7,6},{8,9},{9,8},{10,11... | collective-permute-start | bytes 503816 | tf_op jit(solution)/shard_map/ppermute | solution.py:119
  36.6 7.3 %collective-permute-start.18 = (bf16[656,128]{1,0:T(8,128)(2,1)S(1)}, bf16[656,128]{1,0:T(8,128)(2,1)S(1)}, u32[]{:S(2)}, u32[]{:S(2)}) collective-permute-start(bf16[656,128]{1,0:T(8,128)(2,1)S(1)} %get-tuple-element.187.refs_0_), channel_id=1, source_target_pairs={{0,1},{1,0},{2,3},{3,2},{4,5},{5,4},{6,7},{7,6},{8,9},{9,8},{10,11... | collective-permute-start | bytes 503816 | tf_op jit(solution)/shard_map/ppermute | solution.py:119
  37.2 14.5 %collective-permute-start.15 = (bf16[2,512,256]{2,1,0:T(8,128)(2,1)S(1)}, bf16[2,512,256]{2,1,0:T(8,128)(2,1)S(1)}, u32[]{:S(2)}, u32[]{:S(2)}) collective-permute-start(bf16[2,512,256]{2,1,0:T(8,128)(2,1)S(1)} %get-tuple-element.185.refs_0_), channel_id=1, source_target_pairs={{0,4},{1,3},{4,8},{5,1},{8,12},{9,5},{12,14},{13,9},{14,10},{15,13... | collective-permute-start | bytes 1572872 | tf_op jit(solution)/shard_map/ppermute | solution.py:135
  38.8 12.9 %collective-permute-start.16 = (bf16[2,512,256]{2,1,0:T(8,128)(2,1)S(1)}, bf16[2,512,256]{2,1,0:T(8,128)(2,1)S(1)}, u32[]{:S(2)}, u32[]{:S(2)}) collective-permute-start(bf16[2,512,256]{2,1,0:T(8,128)(2,1)S(1)} %get-tuple-element.186.refs_1_), channel_id=1, source_target_pairs={{0,2},{1,5},{4,0},{5,9},{8,4},{9,13},{12,8},{13,15},{14,12},{15,11... | collective-permute-start | bytes 1572872 | tf_op jit(solution)/shard_map/ppermute | solution.py:135
  44.0 7.7 %collective-permute-start.20 = (bf16[2,512,256]{2,1,0:T(8,128)(2,1)S(1)}, bf16[2,512,256]{2,1,0:T(8,128)(2,1)S(1)}, u32[]{:S(2)}, u32[]{:S(2)}) collective-permute-start(bf16[2,512,256]{2,1,0:T(8,128)(2,1)S(1)} %get-tuple-element.200), channel_id=1, source_target_pairs={{0,1},{1,0},{2,3},{3,2},{4,5},{5,4},{6,7},{7,6},{8,9},{9,8},{10,11... | collective-permute-start | bytes 1572872 | tf_op jit(solution)/shard_map/ppermute | solution.py:119
  44.0 7.6 %collective-permute-start.21 = (bf16[2,512,256]{2,1,0:T(8,128)(2,1)S(1)}, bf16[2,512,256]{2,1,0:T(8,128)(2,1)S(1)}, u32[]{:S(2)}, u32[]{:S(2)}) collective-permute-start(bf16[2,512,256]{2,1,0:T(8,128)(2,1)S(1)} %get-tuple-element.201), channel_id=1, source_target_pairs={{0,1},{1,0},{2,3},{3,2},{4,5},{5,4},{6,7},{7,6},{8,9},{9,8},{10,11... | collective-permute-start | bytes 1572872 | tf_op jit(solution)/shard_map/ppermute | solution.py:119
  52.5 8.1 %collective-permute-start.27 = (bf16[2,512,256]{2,1,0:T(8,128)(2,1)S(1)}, bf16[2,512,256]{2,1,0:T(8,128)(2,1)S(1)}, u32[]{:S(2)}, u32[]{:S(2)}) collective-permute-start(bf16[2,512,256]{2,1,0:T(8,128)(2,1)S(1)} %get-tuple-element.218.refs_2_.refs_3_), channel_id=1, source_target_pairs={{0,1},{1,0},{2,3},{3,2},{4,5},{5,4},{6,7},{7,6},{8,9},{9,8},{10,11... | collective-permute-start | bytes 1572872 | tf_op jit(solution)/shard_map/ppermute | solution.py:119
  52.5 8.1 %collective-permute-start.28 = (bf16[2,512,256]{2,1,0:T(8,128)(2,1)S(1)}, bf16[2,512,256]{2,1,0:T(8,128)(2,1)S(1)}, u32[]{:S(2)}, u32[]{:S(2)}) collective-permute-start(bf16[2,512,256]{2,1,0:T(8,128)(2,1)S(1)} %get-tuple-element.219.refs_3_.refs_4_), channel_id=1, source_target_pairs={{0,1},{1,0},{2,3},{3,2},{4,5},{5,4},{6,7},{7,6},{8,9},{9,8},{10,11... | collective-permute-start | bytes 1572872 | tf_op jit(solution)/shard_map/ppermute | solution.py:119
  53.0 7.6 %collective-permute-start.25 = (bf16[784,128]{1,0:T(8,128)(2,1)S(1)}, bf16[784,128]{1,0:T(8,128)(2,1)S(1)}, u32[]{:S(2)}, u32[]{:S(2)}) collective-permute-start(bf16[784,128]{1,0:T(8,128)(2,1)S(1)} %pack.3.refs_2_.refs_0_), channel_id=1, source_target_pairs={{0,2},{1,5},{4,0},{5,9},{8,4},{9,13},{12,8},{13,15},{14,12},{15,11... | collective-permute-start | bytes 602120 | tf_op jit(solution)/shard_map/ppermute | solution.py:135
  60.6 7.6 %collective-permute-start.29 = (bf16[784,128]{1,0:T(8,128)(2,1)S(1)}, bf16[784,128]{1,0:T(8,128)(2,1)S(1)}, u32[]{:S(2)}, u32[]{:S(2)}) collective-permute-start(bf16[784,128]{1,0:T(8,128)(2,1)S(1)} %get-tuple-element.223.refs_0_), channel_id=1, source_target_pairs={{0,4},{1,3},{4,8},{5,1},{8,12},{9,5},{12,14},{13,9},{14,10},{15,13... | collective-permute-start | bytes 602120 | tf_op jit(solution)/shard_map/ppermute | solution.py:135
  68.3 7.3 %collective-permute-start.33 = (bf16[784,128]{1,0:T(8,128)(2,1)S(1)}, bf16[784,128]{1,0:T(8,128)(2,1)S(1)}, u32[]{:S(2)}, u32[]{:S(2)}) collective-permute-start(bf16[784,128]{1,0:T(8,128)(2,1)S(1)} %get-tuple-element.236.refs_0_), channel_id=1, source_target_pairs={{0,4},{1,3},{4,8},{5,1},{8,12},{9,5},{12,14},{13,9},{14,10},{15,13... | collective-permute-start | bytes 602120 | tf_op jit(solution)/shard_map/ppermute | solution.py:135
  81.4 15.4 %collective-permute-start.43 = (bf16[2,512,256]{2,1,0:T(8,128)(2,1)S(1)}, bf16[2,512,256]{2,1,0:T(8,128)(2,1)S(1)}, u32[]{:S(2)}, u32[]{:S(2)}) collective-permute-start(bf16[2,512,256]{2,1,0:T(8,128)(2,1)S(1)} %get-tuple-element.281), channel_id=1, source_target_pairs={{0,4},{1,3},{4,8},{5,1},{8,12},{9,5},{12,14},{13,9},{14,10},{15,13... | collective-permute-start | bytes 1572872 | tf_op jit(solution)/shard_map/ppermute | solution.py:135
  82.7 14.1 %collective-permute-start.44 = (bf16[2,512,256]{2,1,0:T(8,128)(2,1)S(1)}, bf16[2,512,256]{2,1,0:T(8,128)(2,1)S(1)}, u32[]{:S(2)}, u32[]{:S(2)}) collective-permute-start(bf16[2,512,256]{2,1,0:T(8,128)(2,1)S(1)} %get-tuple-element.282), channel_id=1, source_target_pairs={{0,2},{1,5},{4,0},{5,9},{8,4},{9,13},{12,8},{13,15},{14,12},{15,11... | collective-permute-start | bytes 1572872 | tf_op jit(solution)/shard_map/ppermute | solution.py:135
  97.4 9.7 %collective-permute-start.48 = (bf16[2,512,256]{2,1,0:T(8,128)(2,1)S(1)}, bf16[2,512,256]{2,1,0:T(8,128)(2,1)S(1)}, u32[]{:S(2)}, u32[]{:S(2)}) collective-permute-start(bf16[2,512,256]{2,1,0:T(8,128)(2,1)S(1)} %get-tuple-element.286.refs_0_), channel_id=1, source_target_pairs={{0,4},{1,3},{4,8},{5,1},{8,12},{9,5},{12,14},{13,9},{14,10},{15,13... | collective-permute-start | bytes 1572872 | tf_op jit(solution)/shard_map/ppermute | solution.py:135
  98.5 8.0 %collective-permute-start.45 = (f32[64,128]{1,0:T(8,128)S(1)}, f32[64,128]{1,0:T(8,128)S(1)}, u32[]{:S(2)}, u32[]{:S(2)}) collective-permute-start(f32[64,128]{1,0:T(8,128)S(1)} %get-tuple-element.285.refs_0_), channel_id=1, source_target_pairs={{0,4},{1,5},{2,6},{3,7},{4,0},{5,1},{6,2},{7,3},{8,12},{9,13},{10,... | collective-permute-start | bytes 98312 | tf_op jit(solution)/shard_map/ppermute | solution.py:226
  (32 other events, 143.2 us)
